TPU v7x, 32 devices: a whole 2x2x4 slice. The times are simulated.
32 devices in a mesh: section: 2 (over x), seq: 4 (over y, core), tp: 4 (over z).
Axes of the slice: x: 2, y: 2, z: 4, core: 2. Of those that a mesh axis runs over, the one named last changes fastest.
Arguments:
- inputs: bfloat16 [4, 1024, 2048], P(None, ('seq', 'tp')), may hold values from -6 to 6
- cotangent: bfloat16 [4, 1024, 2048], P(None, 'seq'), may hold values from -6 to 6
- doc_start: int32 [4, 1024], P(None, 'seq'), may hold values from 0 to 4095, as said below
- norm_in: float32 [2, 2048], P('section'), may hold values from 0.5 to 1.5
- query_weight: bfloat16 [2, 2048, 1024], P('section', None, 'tp'), may hold values from -0.125 to 0.125
- key_weight: bfloat16 [2, 2048, 1024], P('section', None, 'tp'), may hold values from -0.125 to 0.125
- value_weight: bfloat16 [2, 2048, 2048], P('section', None, 'tp'), may hold values from -0.125 to 0.125
- outgate_weight: bfloat16 [2, 2048, 2048], P('section', None, 'tp'), may hold values from -0.125 to 0.125
- decay_weight: bfloat16 [2, 2048, 8], P('section', None, 'tp'), may hold values from -0.125 to 0.125
- beta_weight: bfloat16 [2, 2048, 8], P('section', None, 'tp'), may hold values from -0.125 to 0.125
- conv_query: float32 [2, 4, 1024], P('section', None, 'tp'), may hold values from -0.6 to 0.6
- conv_key: float32 [2, 4, 1024], P('section', None, 'tp'), may hold values from -0.6 to 0.6
- conv_value: float32 [2, 4, 2048], P('section', None, 'tp'), may hold values from -0.6 to 0.6
- decay_log: float32 [2, 8], P('section', 'tp'), may hold values from -7 to -3
- decay_bias: float32 [2, 8], P('section', 'tp'), may hold values from -2 to 1
- head_norm: float32 [2, 256], P('section'), may hold values from 0.5 to 1.5
- out_weight: bfloat16 [2, 2048, 2048], P('section', 'tp'), may hold values from -0.125 to 0.125
- norm_feed: float32 [2, 2048], P('section'), may hold values from 0.5 to 1.5
- gate_weight: bfloat16 [2, 2048, 5632], P('section', None, 'tp'), may hold values from -0.125 to 0.125
- up_weight: bfloat16 [2, 2048, 5632], P('section', None, 'tp'), may hold values from -0.125 to 0.125
- down_weight: bfloat16 [2, 5632, 2048], P('section', 'tp'), may hold values from -0.078125 to 0.078125
Outputs:
- section_out: float32 [2, 4, 1024, 2048], P('section', None, ('seq', 'tp'))
- section_in_grad: float32 [2, 4, 1024, 2048], P('section', None, ('seq', 'tp'))
- grad_norm_in: float32 [2, 2048], P('section')
- grad_query: float32 [2, 2048, 1024], P('section', 'seq', 'tp')
- grad_key: float32 [2, 2048, 1024], P('section', 'seq', 'tp')
- grad_value: float32 [2, 2048, 2048], P('section', 'seq', 'tp')
- grad_outgate: float32 [2, 2048, 2048], P('section', 'seq', 'tp')
- grad_decay: float32 [2, 2048, 8], P('section', 'seq', 'tp')
- grad_beta: float32 [2, 2048, 8], P('section', 'seq', 'tp')
- grad_conv_query: float32 [2, 4, 1024], P('section', None, 'tp')
- grad_conv_key: float32 [2, 4, 1024], P('section', None, 'tp')
- grad_conv_value: float32 [2, 4, 2048], P('section', None, 'tp')
- grad_decay_log: float32 [2, 8], P('section', 'tp')
- grad_decay_bias: float32 [2, 8], P('section', 'tp')
- grad_head_norm: float32 [2, 256], P('section')
- grad_out: float32 [2, 2048, 2048], P('section', 'tp', 'seq')
- grad_norm_feed: float32 [2, 2048], P('section')
- grad_gate: float32 [2, 2048, 5632], P('section', 'seq', 'tp')
- grad_up: float32 [2, 2048, 5632], P('section', 'seq', 'tp')
- grad_down: float32 [2, 5632, 2048], P('section', 'tp', 'seq')
Inputs may be any that keep to these rules, and one draw needn't show every extreme that they name: `doc_start`: each entry is the position where its token's document starts: entries never fall along the positions, none exceeds its own position, an entry equals its own position wherever it differs from the entry before it; position 0 and the last position each start a document.
All inputs are finite; a program needn't handle non-finite values.
Results may differ from a plain program's by a relative error of at most 0.039.
Values sent between devices are 32-bit elements; how exact they have to be, the bound alone decides.
No kernel may reach another device: no remote copies, remote signals or barrier semaphores. Data moves between devices by JAX's collectives and lax.ppermute only.
A program may use at most 384 MiB of HBM per device.

v0:
```python
from functools import partial

import jax
import jax.numpy as jnp
from jax import lax
from jax.sharding import PartitionSpec as P

BLOCK = 64


EPSILON = 1e-06
TOP_PRECISION = lax.Precision.HIGHEST


def shifted(value, axis, steps):
    count = lax.axis_size(axis)
    pairs = [(source, (source + steps) % count) for source in range(count)]
    return lax.ppermute(value, axis, pairs)


def carried_in(x, axis, combine, identity, reverse):
    size, mine = (lax.axis_size(axis), lax.axis_index(axis))
    everything = jax.tree.map(lambda part: lax.all_gather(part, axis), x)
    start = jax.tree.map(
        lambda part, zero: jnp.broadcast_to(jnp.asarray(zero, part.dtype), part.shape), x, identity
    )

    def turn(k, before):
        at = size - 1 - k if reverse else k
        reached = at > mine if reverse else at < mine
        new = combine(before, jax.tree.map(lambda part: part[at], everything))
        return jax.tree.map(lambda a, b: jnp.where(reached, a, b), new, before)

    return lax.fori_loop(0, size, turn, start)


def from_behind(value, axis, steps):
    count = lax.axis_size(axis)
    initial, last = (max(0, -steps), min(count, count - steps))
    return lax.ppermute(value, axis, [(source, source + steps) for source in range(initial, last)])


def row_norm(values, gain_vector):
    return values * lax.rsqrt(jnp.mean(values * values, -1, keepdims=True) + EPSILON) * gain_vector


def matmul_high(first_matrix, second_matrix):
    return jnp.matmul(first_matrix, second_matrix, precision=TOP_PRECISION)


def flip_last(values):
    return jnp.swapaxes(values, -1, -2)


def compose(earlier, later):
    return (matmul_high(later[0], earlier[0]), matmul_high(later[0], earlier[1]) + later[1])


def inner_left(first_matrix, second_matrix):
    return lax.dot_general(
        first_matrix, second_matrix, (((0,), (0,)), ((), ())), preferred_element_type=jnp.float32
    )


def inner_right(first_matrix, second_matrix):
    return lax.dot_general(
        first_matrix, second_matrix, (((1,), (1,)), ((), ())), preferred_element_type=jnp.float32
    )


def gather_rows(rows_part):
    return lax.all_gather(rows_part, "tp", axis=0, tiled=True)


def causal_conv(values, border, taps):
    padded = jnp.concatenate([border, values], 0)
    summed = jnp.zeros_like(values)
    for offset in range(taps.shape[0]):
        summed = summed + taps[offset] * padded[offset : offset + values.shape[0]]
    return summed


def unit_heads(values, head_size):
    shaped = values.reshape(values.shape[0], -1, head_size)
    return shaped * lax.rsqrt(jnp.sum(shaped * shaped, -1, keepdims=True) + EPSILON)


def gated_unit(gate_act, up_act):
    return jax.nn.silu(gate_act) * up_act


def block_step(state_now, block_items):
    query_rows, key_rows, value_rows, log_decay, beta_gate, resets = block_items
    span = resets.shape[0]
    cumulative = jnp.cumsum(log_decay, -1)
    counts = jnp.cumsum(resets)
    lower_mask = jnp.tril(jnp.ones((span, span), bool))
    strict = jnp.tril(jnp.ones((span, span), bool), -1)
    linked = (counts[:, None] == counts[None, :]) & lower_mask
    spread = cumulative[:, :, None] - cumulative[:, None, :]
    decays = jnp.where(linked, jnp.exp(jnp.where(linked, spread, 0.0)), 0.0)
    head_decay = jnp.exp(cumulative) * (counts == 0.0)
    tail_decay = jnp.exp(cumulative[:, -1:] - cumulative) * (counts == counts[-1])
    key_gram = matmul_high(key_rows, flip_last(key_rows))
    mixing = jnp.eye(span, dtype=jnp.float32) + beta_gate[:, :, None] * jnp.where(
        strict, decays * key_gram, 0.0
    )
    extended = jnp.concatenate([jnp.zeros(key_rows.shape, jnp.float32), value_rows], -1)
    target = beta_gate[:, :, None] * (
        extended - head_decay[:, :, None] * matmul_high(key_rows, state_now)
    )
    update = lax.linalg.triangular_solve(
        mixing, target, left_side=True, lower=True, unit_diagonal=True
    )
    scores = matmul_high(query_rows, flip_last(key_rows)) * decays
    output_rows = head_decay[:, :, None] * matmul_high(query_rows, state_now) + matmul_high(
        scores, update
    )
    state_now = head_decay[:, -1:, None] * state_now + matmul_high(
        flip_last(key_rows * tail_decay[:, :, None]), update
    )
    return (state_now, output_rows)


def mixer_local(
    proj_query,
    proj_key,
    proj_value,
    proj_decay,
    proj_beta,
    border_query,
    border_key,
    border_value,
    conv_query,
    conv_key,
    conv_value,
    decay_log,
    decay_bias,
    resets,
):
    row_count = proj_query.shape[0]
    head_count = decay_log.shape[0]
    key_size = proj_query.shape[1] // head_count
    value_size = proj_value.shape[1] // head_count
    query_rows = unit_heads(
        jax.nn.silu(causal_conv(proj_query, border_query, conv_query)), key_size
    ) * key_size ** (-0.5)
    key_rows = unit_heads(jax.nn.silu(causal_conv(proj_key, border_key, conv_key)), key_size)
    value_rows = jax.nn.silu(causal_conv(proj_value, border_value, conv_value)).reshape(
        row_count, head_count, value_size
    )
    log_decay = -jnp.exp(decay_log) * jax.nn.softplus(proj_decay + decay_bias)
    beta_gate = jax.nn.sigmoid(proj_beta)
    blocks = row_count // BLOCK

    def heads_first(tensor_in):
        shaped = tensor_in.reshape((blocks, BLOCK) + tensor_in.shape[1:])
        if tensor_in.ndim > 1:
            return jnp.moveaxis(shaped, 2, 1)
        return shaped

    initial = jnp.concatenate(
        [
            jnp.broadcast_to(
                jnp.eye(key_size, dtype=jnp.float32), (head_count, key_size, key_size)
            ),
            jnp.zeros((head_count, key_size, value_size), jnp.float32),
        ],
        -1,
    )
    final_state, output_rows = lax.scan(
        block_step,
        initial,
        (
            heads_first(query_rows),
            heads_first(key_rows),
            heads_first(value_rows),
            heads_first(log_decay),
            heads_first(beta_gate),
            heads_first(resets),
        ),
    )
    output_rows = jnp.moveaxis(output_rows, 1, 2).reshape(
        row_count, head_count, key_size + value_size
    )
    return (
        output_rows[:, :, :key_size],
        output_rows[:, :, key_size:],
        final_state[:, :, :key_size],
        final_state[:, :, key_size:],
    )


def mixer_output(carried_query, local_output, initial_state_value, proj_outgate, head_norm):
    row_count, head_count, value_size = local_output.shape
    output_rows = local_output + jnp.einsum(
        "sqi,qif->sqf", carried_query, initial_state_value, precision=TOP_PRECISION
    )
    normed = (
        output_rows
        * lax.rsqrt(jnp.mean(output_rows * output_rows, -1, keepdims=True) + EPSILON)
        * head_norm
    )
    return (normed * jax.nn.silu(proj_outgate.reshape(row_count, head_count, value_size))).reshape(
        row_count, head_count * value_size
    )


def fetch(buffer, slot_index):
    return lax.dynamic_index_in_dim(buffer, slot_index, 0, keepdims=False)


def store(buffer, value, slot_index, is_valid):
    previous = fetch(buffer, slot_index)
    return lax.dynamic_update_index_in_dim(
        buffer, jnp.where(is_valid, value, previous), slot_index, 0
    )


def add_tail(gradient, tail_grad):
    border_rows = tail_grad.shape[0]
    return jnp.concatenate([gradient[:-border_rows], gradient[-border_rows:] + tail_grad], 0)


def local(
    inputs,
    cotangent,
    doc_start,
    norm_in,
    query_weight,
    key_weight,
    value_weight,
    outgate_weight,
    decay_weight,
    beta_weight,
    conv_query,
    conv_key,
    conv_value,
    decay_log,
    decay_bias,
    head_norm,
    out_weight,
    norm_feed,
    gate_weight,
    up_weight,
    down_weight,
):
    layer_items = [
        member[0]
        for member in (
            norm_in,
            query_weight,
            key_weight,
            value_weight,
            outgate_weight,
            decay_weight,
            beta_weight,
            conv_query,
            conv_key,
            conv_value,
            decay_log,
            decay_bias,
            head_norm,
            out_weight,
            norm_feed,
            gate_weight,
            up_weight,
            down_weight,
        )
    ]
    (
        norm_in,
        query_weight,
        key_weight,
        value_weight,
        outgate_weight,
        decay_weight,
        beta_weight,
        conv_query,
        conv_key,
        conv_value,
        decay_log,
        decay_bias,
        head_norm,
        out_weight,
        norm_feed,
        gate_weight,
        up_weight,
        down_weight,
    ) = layer_items
    micro_count, row_count, width = inputs.shape
    block_rows = cotangent.shape[1]
    seq_size = lax.axis_size("seq")
    seq_index = lax.axis_index("seq")
    tp_index = lax.axis_index("tp")
    section_index = lax.axis_index("section")
    first_device = seq_index == 0
    final_device = seq_index == seq_size - 1
    head_count = decay_log.shape[0]
    key_size = query_weight.shape[1] // head_count
    value_size = value_weight.shape[1] // head_count
    border_rows = conv_query.shape[0] - 1
    in_weights = (query_weight, key_weight, value_weight, outgate_weight, decay_weight, beta_weight)
    identity = (
        jnp.broadcast_to(jnp.eye(key_size, dtype=jnp.float32), (head_count, key_size, key_size)),
        jnp.zeros((head_count, key_size, value_size), jnp.float32),
    )
    offsets = jnp.arange(block_rows, dtype=jnp.int32)

    def reset_flags(slot_index):
        places = slot_index * (block_rows * seq_size) + seq_index * block_rows + offsets
        return (fetch(doc_start, slot_index) == places).astype(jnp.float32)

    def project(hidden):
        return tuple(
            (jnp.dot(hidden, weight, preferred_element_type=jnp.float32) for weight in in_weights)
        )

    zero_border = tuple(
        (
            jnp.zeros((border_rows, weight.shape[1]), jnp.float32)
            for weight in (query_weight, key_weight, value_weight)
        )
    )
    border_carry = zero_border
    state_send = jnp.zeros((head_count, key_size, value_size), jnp.float32)
    received_rows = jnp.zeros((row_count, width), jnp.float32)
    kept_input = jnp.zeros((micro_count, block_rows, width), jnp.float32)
    kept_mixed = jnp.zeros((micro_count, block_rows, width), jnp.float32)
    kept_state = jnp.zeros((micro_count, head_count, key_size, value_size), jnp.float32)
    kept_border = tuple(
        (jnp.zeros((micro_count,) + member.shape, jnp.float32) for member in zero_border)
    )
    section_out = jnp.zeros((micro_count, row_count, width), jnp.float32)
    for step_index in range(micro_count + 1):
        micro_index = step_index - section_index
        is_valid = (micro_index >= 0) & (micro_index < micro_count)
        slot_index = jnp.clip(micro_index, 0, micro_count - 1)
        in_rows = jnp.where(
            section_index == 0, fetch(inputs, slot_index).astype(jnp.float32), received_rows
        )
        residual = gather_rows(in_rows)
        resets = reset_flags(slot_index)
        projected_rows = project(row_norm(residual, norm_in).astype(jnp.bfloat16))
        moved = shifted(
            (
                projected_rows[0][block_rows - border_rows :],
                projected_rows[1][block_rows - border_rows :],
                projected_rows[2][block_rows - border_rows :],
                state_send,
            ),
            "seq",
            1,
        )
        borders = tuple(
            (jnp.where(first_device, border_carry[member], moved[member]) for member in range(3))
        )
        border_carry = tuple(
            (jnp.where(is_valid, moved[member], border_carry[member]) for member in range(3))
        )
        carried_state = jnp.where(first_device, moved[3], 0.0)
        carried_query, local_output, trans_map, trans_shift = mixer_local(
            projected_rows[0],
            projected_rows[1],
            projected_rows[2],
            projected_rows[4],
            projected_rows[5],
            borders[0],
            borders[1],
            borders[2],
            conv_query,
            conv_key,
            conv_value,
            decay_log,
            decay_bias,
            resets,
        )
        entry_shift = trans_shift + matmul_high(trans_map, carried_state)
        prefix = carried_in((trans_map, entry_shift), "seq", compose, identity, False)
        initial_state_value = jnp.where(first_device, carried_state, prefix[1])
        end_state = matmul_high(trans_map, initial_state_value) + trans_shift
        state_send = jnp.where(is_valid & final_device, end_state, state_send)
        gated = mixer_output(
            carried_query, local_output, initial_state_value, projected_rows[3], head_norm
        ).astype(jnp.bfloat16)
        mixed = residual + lax.psum(
            jnp.dot(gated, out_weight, preferred_element_type=jnp.float32), "tp"
        )
        hidden_feed = row_norm(mixed, norm_feed).astype(jnp.bfloat16)
        inner_act = gated_unit(
            jnp.dot(hidden_feed, gate_weight, preferred_element_type=jnp.float32),
            jnp.dot(hidden_feed, up_weight, preferred_element_type=jnp.float32),
        ).astype(jnp.bfloat16)
        out_rows = lax.dynamic_slice_in_dim(
            mixed, tp_index * row_count, row_count, 0
        ) + lax.psum_scatter(
            jnp.dot(inner_act, down_weight, preferred_element_type=jnp.float32),
            "tp",
            scatter_dimension=0,
            tiled=True,
        )
        section_out = store(section_out, out_rows, slot_index, is_valid)
        kept_input = store(kept_input, residual, slot_index, is_valid)
        kept_mixed = store(kept_mixed, mixed, slot_index, is_valid)
        kept_state = store(kept_state, initial_state_value, slot_index, is_valid)
        kept_border = tuple(
            (
                store(kept_border[member], borders[member], slot_index, is_valid)
                for member in range(3)
            )
        )
        if step_index < micro_count:
            received_rows = from_behind(out_rows, "section", 1)
    weight_list = (
        query_weight,
        key_weight,
        value_weight,
        outgate_weight,
        decay_weight,
        beta_weight,
        gate_weight,
        up_weight,
        out_weight,
        down_weight,
    )
    totals = [jnp.zeros(weight.shape, jnp.float32) for weight in weight_list]
    small_grads = [
        jnp.zeros(member.shape, jnp.float32)
        for member in (
            norm_in,
            norm_feed,
            head_norm,
            decay_log,
            decay_bias,
            conv_query,
            conv_key,
            conv_value,
        )
    ]
    received_grad = jnp.zeros((row_count, width), jnp.float32)
    tail_carry = zero_border
    state_grad_carry = jnp.zeros((head_count, key_size, value_size), jnp.float32)
    section_in_grad = jnp.zeros((micro_count, row_count, width), jnp.float32)
    for step_index in range(micro_count + 1):
        micro_index = micro_count - step_index - section_index
        is_valid = (micro_index >= 0) & (micro_index < micro_count)
        slot_index = jnp.clip(micro_index, 0, micro_count - 1)
        handed_grad = gather_rows(received_grad)
        top_grad = jnp.where(
            section_index == 1, fetch(cotangent, slot_index).astype(jnp.float32), handed_grad
        )
        residual = fetch(kept_input, slot_index)
        mixed = fetch(kept_mixed, slot_index)
        initial_state_value = fetch(kept_state, slot_index)
        borders = tuple((fetch(kept_border[member], slot_index) for member in range(3)))
        resets = reset_flags(slot_index)
        hidden_feed = row_norm(mixed, norm_feed).astype(jnp.bfloat16)
        activation, act_back = jax.vjp(
            gated_unit,
            jnp.dot(hidden_feed, gate_weight, preferred_element_type=jnp.float32),
            jnp.dot(hidden_feed, up_weight, preferred_element_type=jnp.float32),
        )
        inner_act = activation.astype(jnp.bfloat16)
        top_low = top_grad.astype(jnp.bfloat16)
        gate_grad, up_grad = act_back(inner_right(top_low, down_weight))
        gate_low = gate_grad.astype(jnp.bfloat16)
        up_low = up_grad.astype(jnp.bfloat16)
        feed_part = inner_right(gate_low, gate_weight) + inner_right(up_low, up_weight)
        hidden_feed_grad = lax.psum(feed_part, "tp")
        _, feed_norm_back = jax.vjp(row_norm, mixed, norm_feed)
        mixed_back, feed_gain_grad = feed_norm_back(hidden_feed_grad)
        mixed_grad = top_grad + mixed_back
        hidden = row_norm(residual, norm_in).astype(jnp.bfloat16)
        projected_rows = project(hidden)
        local_values, local_back = jax.vjp(
            partial(mixer_local, resets=resets),
            projected_rows[0],
            projected_rows[1],
            projected_rows[2],
            projected_rows[4],
            projected_rows[5],
            borders[0],
            borders[1],
            borders[2],
            conv_query,
            conv_key,
            conv_value,
            decay_log,
            decay_bias,
        )
        carried_query, local_output, trans_map, trans_shift = local_values
        gated_value, output_back = jax.vjp(
            mixer_output,
            carried_query,
            local_output,
            initial_state_value,
            projected_rows[3],
            head_norm,
        )
        gated = gated_value.astype(jnp.bfloat16)
        mixer_low = mixed_grad.astype(jnp.bfloat16)
        carry_grad, local_grad, state_local, outgate_grad, head_gain_grad = output_back(
            inner_right(mixer_low, out_weight)
        )
        map_back = flip_last(trans_map)
        entry_grad = state_local + jnp.where(
            final_device, matmul_high(map_back, state_grad_carry), 0.0
        )
        suffix = carried_in((map_back, entry_grad), "seq", compose, identity, True)
        end_grad = jnp.where(final_device, state_grad_carry, suffix[1])
        start_grad = state_local + matmul_high(map_back, end_grad)
        local_grads = local_back(
            (
                carry_grad,
                local_grad,
                matmul_high(end_grad, flip_last(initial_state_value)),
                end_grad,
            )
        )
        moved = shifted((local_grads[5], local_grads[6], local_grads[7], start_grad), "seq", -1)
        tail_grads = tuple(
            (jnp.where(final_device, tail_carry[member], moved[member]) for member in range(3))
        )
        tail_carry = tuple(
            (jnp.where(is_valid, moved[member], tail_carry[member]) for member in range(3))
        )
        state_grad_carry = jnp.where(is_valid, moved[3], state_grad_carry)
        proj_low = [
            add_tail(local_grads[0], tail_grads[0]).astype(jnp.bfloat16),
            add_tail(local_grads[1], tail_grads[1]).astype(jnp.bfloat16),
            add_tail(local_grads[2], tail_grads[2]).astype(jnp.bfloat16),
            outgate_grad.astype(jnp.bfloat16),
            local_grads[3].astype(jnp.bfloat16),
            local_grads[4].astype(jnp.bfloat16),
        ]
        mixer_part = inner_right(proj_low[0], in_weights[0])
        for member in range(1, 6):
            mixer_part = mixer_part + inner_right(proj_low[member], in_weights[member])
        hidden_grad, head_gain_total = lax.psum((mixer_part, head_gain_grad), "tp")
        _, in_norm_back = jax.vjp(row_norm, residual, norm_in)
        residual_back, in_gain_grad = in_norm_back(hidden_grad)
        residual_grad = mixed_grad + residual_back
        own_grad = lax.dynamic_slice_in_dim(residual_grad, tp_index * row_count, row_count, 0)
        section_in_grad = store(section_in_grad, own_grad, slot_index, is_valid)
        step_grads = [inner_left(hidden, proj_low[member]) for member in range(6)]
        step_grads = step_grads + [
            inner_left(hidden_feed, gate_low),
            inner_left(hidden_feed, up_low),
            inner_left(gated, mixer_low),
            inner_left(inner_act, top_low),
        ]
        step_grads = [jnp.where(is_valid, member, 0.0) for member in step_grads]
        totals = [summed + part for summed, part in zip(totals, step_grads)]
        small_step = [
            in_gain_grad,
            feed_gain_grad,
            head_gain_total,
            local_grads[11],
            local_grads[12],
            local_grads[8],
            local_grads[9],
            local_grads[10],
        ]
        small_grads = [
            summed + jnp.where(is_valid, part, 0.0) for summed, part in zip(small_grads, small_step)
        ]
        if step_index < micro_count:
            received_grad = from_behind(own_grad, "section", -1)
    totals = (
        lax.psum_scatter(totals[0], "seq", scatter_dimension=0, tiled=True),
        lax.psum_scatter(totals[1], "seq", scatter_dimension=0, tiled=True),
        lax.psum_scatter(totals[2], "seq", scatter_dimension=0, tiled=True),
        lax.psum_scatter(totals[3], "seq", scatter_dimension=0, tiled=True),
        lax.psum_scatter(totals[4], "seq", scatter_dimension=0, tiled=True),
        lax.psum_scatter(totals[5], "seq", scatter_dimension=0, tiled=True),
        lax.psum_scatter(totals[6], "seq", scatter_dimension=0, tiled=True),
        lax.psum_scatter(totals[7], "seq", scatter_dimension=0, tiled=True),
        lax.psum_scatter(totals[8], "seq", scatter_dimension=1, tiled=True),
        lax.psum_scatter(totals[9], "seq", scatter_dimension=1, tiled=True),
    )
    small_grads = lax.psum(
        (
            small_grads[0],
            small_grads[1],
            small_grads[2],
            small_grads[3],
            small_grads[4],
            small_grads[5],
            small_grads[6],
            small_grads[7],
        ),
        "seq",
    )
    return (
        section_out[None],
        section_in_grad[None],
        small_grads[0][None],
        totals[0][None],
        totals[1][None],
        totals[2][None],
        totals[3][None],
        totals[4][None],
        totals[5][None],
        small_grads[5][None],
        small_grads[6][None],
        small_grads[7][None],
        small_grads[3][None],
        small_grads[4][None],
        small_grads[2][None],
        totals[8][None],
        small_grads[1][None],
        totals[6][None],
        totals[7][None],
        totals[9][None],
    )


def solution(mesh):
    placed = (
        P(None, ("seq", "tp"), None),
        P(None, "seq", None),
        P(None, "seq"),
        P("section", None),
        P("section", None, "tp"),
        P("section", None, "tp"),
        P("section", None, "tp"),
        P("section", None, "tp"),
        P("section", None, "tp"),
        P("section", None, "tp"),
        P("section", None, "tp"),
        P("section", None, "tp"),
        P("section", None, "tp"),
        P("section", "tp"),
        P("section", "tp"),
        P("section", None),
        P("section", "tp", None),
        P("section", None),
        P("section", None, "tp"),
        P("section", None, "tp"),
        P("section", "tp", None),
    )
    return jax.shard_map(
        local,
        mesh=mesh,
        in_specs=placed,
        out_specs=(
            P("section", None, ("seq", "tp"), None),
            P("section", None, ("seq", "tp"), None),
            P("section", None),
            P("section", "seq", "tp"),
            P("section", "seq", "tp"),
            P("section", "seq", "tp"),
            P("section", "seq", "tp"),
            P("section", "seq", "tp"),
            P("section", "seq", "tp"),
            P("section", None, "tp"),
            P("section", None, "tp"),
            P("section", None, "tp"),
            P("section", "tp"),
            P("section", "tp"),
            P("section", None),
            P("section", "tp", "seq"),
            P("section", None),
            P("section", "seq", "tp"),
            P("section", "seq", "tp"),
            P("section", "tp", "seq"),
        ),
        check_vma=False,
    )
```

profile of v0, /device:TPU:0, one launch (start us, length us, event | category | flops | bytes accessed | tf_op | source)
XLA Modules:
  0.0 5979.5 jit_solution(7081598432755951207)
XLA Ops:
  13.9 45.0 all-gather.57.cloned.1.call-done
  100.4 138.9 %while.685 = (s32[]{:T(128)}, f32[2,128,384]{2,1,0:T(8,128)}, f32[4,2,64,384]{3,2,1,0:T(8,128)}, f32[4,2,64]{2,1,0:T(2,128)}, f32[4,64]{1,0:T(4,128)}, /*index=5...) while((s32[]{:T(128)}, f32[2,128,384]{2,1,0:T(8,128)}, ...), condition=%wide.region_6.8_spmd, body=%wide.region_3.7_spmd.sunk | while | flops 327766528 | bytes 4965717 | solution.py:171
  277.7 86.6 %all-reduce.179.cloned.1.call-done = f32[256,2048]{1,0:T(8,128)} async-done(((f32[256,2048]{1,0:T(8,128)}), f32[256,2048]{1,0:T(8,128)}) %all-reduce.179.cloned.1.call-update) | async-done | bytes 2097168 | tf_op jit(solution)/shard_map/psum | solution.py:386
  386.0 42.9 reduce-scatter.20.cloned.1.call-done
  453.1 42.3 all-gather.41.cloned.1.call-done
  539.4 160.3 %while.686 = (s32[]{:T(128)}, f32[2,128,384]{2,1,0:T(8,128)}, f32[4,2,64,384]{3,2,1,0:T(8,128)}, f32[4,2,64]{2,1,0:T(2,128)}, f32[4,64]{1,0:T(4,128)}, /*index=5...) while((s32[]{:T(128)}, f32[2,128,384]{2,1,0:T(8,128)}, ...), condition=%wide.region_19.21_spmd, body=%wide.region_16.20_spmd.sunk | while | flops 327766528 | bytes 4995413 | solution.py:171
  747.0 74.7 %all-reduce.181.cloned.1.call-done = f32[256,2048]{1,0:T(8,128)} async-done(((f32[256,2048]{1,0:T(8,128)}), f32[256,2048]{1,0:T(8,128)}) %all-reduce.181.cloned.1.call-update) | async-done | bytes 2097168 | tf_op jit(solution)/shard_map/psum | solution.py:386
  997.7 160.3 %while.687 = (s32[]{:T(128)}, f32[2,128,384]{2,1,0:T(8,128)}, f32[4,2,64,384]{3,2,1,0:T(8,128)}, f32[4,2,64]{2,1,0:T(2,128)}, f32[4,64]{1,0:T(4,128)}, /*index=5...) while((s32[]{:T(128)}, f32[2,128,384]{2,1,0:T(8,128)}, ...), condition=%wide.region_32.34_spmd, body=%wide.region_29.33_spmd.sunk | while | flops 327766528 | bytes 4995413 | solution.py:171
  1202.1 78.0 %all-reduce.183.cloned.1.call-done = f32[256,2048]{1,0:T(8,128)} async-done(((f32[256,2048]{1,0:T(8,128)}), f32[256,2048]{1,0:T(8,128)}) %all-reduce.183.cloned.1.call-update) | async-done | bytes 2097168 | tf_op jit(solution)/shard_map/psum | solution.py:386
  1456.1 160.7 %while.688 = (s32[]{:T(128)}, f32[2,128,384]{2,1,0:T(8,128)}, f32[4,2,64,384]{3,2,1,0:T(8,128)}, f32[4,2,64]{2,1,0:T(2,128)}, f32[4,64]{1,0:T(4,128)}, /*index=5...) while((s32[]{:T(128)}, f32[2,128,384]{2,1,0:T(8,128)}, ...), condition=%wide.region_45.47_spmd, body=%wide.region_42.46_spmd.sunk | while | flops 327766528 | bytes 4995413 | solution.py:171
  1660.6 78.1 %all-reduce.185.cloned.1.call-done = f32[256,2048]{1,0:T(8,128)} async-done(((f32[256,2048]{1,0:T(8,128)}), f32[256,2048]{1,0:T(8,128)}) %all-reduce.185.cloned.1.call-update) | async-done | bytes 2097168 | tf_op jit(solution)/shard_map/psum | solution.py:386
  1914.3 138.7 %while.689 = (s32[]{:T(128)}, f32[2,128,384]{2,1,0:T(8,128)}, f32[4,2,64,384]{3,2,1,0:T(8,128)}, f32[4,2,64]{2,1,0:T(2,128)}, f32[4,64]{1,0:T(4,128)}, /*index=5...) while((s32[]{:T(128)}, f32[2,128,384]{2,1,0:T(8,128)}, ...), condition=%wide.region_58.60_spmd, body=%wide.region_55.59_spmd.sunk | while | flops 327766528 | bytes 4965717 | solution.py:171
  2105.8 68.2 %all-reduce.187.cloned.1.call-done = f32[256,2048]{1,0:T(8,128)} async-done(((f32[256,2048]{1,0:T(8,128)}), f32[256,2048]{1,0:T(8,128)}) %all-reduce.187.cloned.1.call-update) | async-done | bytes 2097168 | tf_op jit(solution)/shard_map/psum | solution.py:386
  2263.9 158.6 %while.690 = (s32[]{:T(128)}, f32[2,128,384]{2,1,0:T(8,128)}, f32[4,2,64,384]{3,2,1,0:T(8,128)}, pred[4,2,64,64]{3,2,1,0:T(32,128)(4,1)}, f32[4,2,64,64]{3,2,1,0...) while((s32[]{:T(128)}, f32[2,128,384]{2,1,0:T(8,128)}, ...), condition=%wide.region_74.77_spmd.clone, body=%wide.region_71.76_spmd.clone.sunk | while | flops 327972096 | bytes 9603193 | solution.py:171
  2485.7 196.9 %while.695 = (s32[]{:T(128)}, f32[2,128,384]{2,1,0:T(8,128)}, f32[4,2,64,128]{3,2,1,0:T(8,128)}, f32[4,2,64,128]{3,2,1,0:T(8,128)}, f32[4,2,64,256]{3,2,1,0:T(8,...) while((s32[]{:T(128)}, f32[2,128,384]{2,1,0:T(8,128)}, ...), condition=%wide.region_90.95_spmd.clone.clone, body=%wide.region_79.94_spmd.clone.clone.sunk | while | flops 662180928 | bytes 26401804 | solution.py:171
  2728.6 85.3 %all-reduce.191.cloned.1.call-done = f32[256,2048]{1,0:T(8,128)} async-done(((f32[256,2048]{1,0:T(8,128)}), f32[256,2048]{1,0:T(8,128)}) %all-reduce.191.cloned.1.call-update) | async-done | bytes 2097168 | tf_op jit(solution)/shard_map/psum | solution.py:539
  2919.8 158.7 %while.691 = (s32[]{:T(128)}, f32[2,128,384]{2,1,0:T(8,128)}, f32[4,2,64,384]{3,2,1,0:T(8,128)}, pred[4,2,64,64]{3,2,1,0:T(32,128)(4,1)}, f32[4,2,64,64]{3,2,1,0...) while((s32[]{:T(128)}, f32[2,128,384]{2,1,0:T(8,128)}, ...), condition=%wide.region_104.109_spmd.clone, body=%wide.region_101.108_spmd.clone.sunk | while | flops 327972096 | bytes 9603193 | solution.py:171
  3135.6 196.8 %while.696 = (s32[]{:T(128)}, f32[2,128,384]{2,1,0:T(8,128)}, f32[4,2,64,128]{3,2,1,0:T(8,128)}, f32[4,2,64,128]{3,2,1,0:T(8,128)}, f32[4,2,64,256]{3,2,1,0:T(8,...) while((s32[]{:T(128)}, f32[2,128,384]{2,1,0:T(8,128)}, ...), condition=%wide.region_120.125_spmd.clone.clone, body=%wide.region_109.124_spmd.clone.clone.sunk | while | flops 662180928 | bytes 26401804 | solution.py:171
  3379.9 82.1 %all-reduce.195.cloned.1.call-done = f32[256,2048]{1,0:T(8,128)} async-done(((f32[256,2048]{1,0:T(8,128)}), f32[256,2048]{1,0:T(8,128)}) %all-reduce.195.cloned.1.call-update) | async-done | bytes 2097168 | tf_op jit(solution)/shard_map/psum | solution.py:539
  3566.3 157.7 %while.692 = (s32[]{:T(128)}, f32[2,128,384]{2,1,0:T(8,128)}, f32[4,2,64,384]{3,2,1,0:T(8,128)}, pred[4,2,64,64]{3,2,1,0:T(32,128)(4,1)}, f32[4,2,64,64]{3,2,1,0...) while((s32[]{:T(128)}, f32[2,128,384]{2,1,0:T(8,128)}, ...), condition=%wide.region_134.139_spmd.clone, body=%wide.region_131.138_spmd.clone.sunk | while | flops 327972096 | bytes 9603193 | solution.py:171
  3773.5 197.0 %while.697 = (s32[]{:T(128)}, f32[2,128,384]{2,1,0:T(8,128)}, f32[4,2,64,128]{3,2,1,0:T(8,128)}, f32[4,2,64,128]{3,2,1,0:T(8,128)}, f32[4,2,64,256]{3,2,1,0:T(8,...) while((s32[]{:T(128)}, f32[2,128,384]{2,1,0:T(8,128)}, ...), condition=%wide.region_150.155_spmd.clone.clone, body=%wide.region_139.154_spmd.clone.clone.sunk | while | flops 662180928 | bytes 26401804 | solution.py:171
  4017.4 82.9 %all-reduce.199.cloned.1.call-done = f32[256,2048]{1,0:T(8,128)} async-done(((f32[256,2048]{1,0:T(8,128)}), f32[256,2048]{1,0:T(8,128)}) %all-reduce.199.cloned.1.call-update) | async-done | bytes 2097168 | tf_op jit(solution)/shard_map/psum | solution.py:539
  4204.9 158.0 %while.693 = (s32[]{:T(128)}, f32[2,128,384]{2,1,0:T(8,128)}, f32[4,2,64,384]{3,2,1,0:T(8,128)}, pred[4,2,64,64]{3,2,1,0:T(32,128)(4,1)}, f32[4,2,64,64]{3,2,1,0...) while((s32[]{:T(128)}, f32[2,128,384]{2,1,0:T(8,128)}, ...), condition=%wide.region_164.169_spmd.clone, body=%wide.region_161.168_spmd.clone.sunk | while | flops 327972096 | bytes 9603193 | solution.py:171
  4412.7 196.6 %while.698 = (s32[]{:T(128)}, f32[2,128,384]{2,1,0:T(8,128)}, f32[4,2,64,128]{3,2,1,0:T(8,128)}, f32[4,2,64,128]{3,2,1,0:T(8,128)}, f32[4,2,64,256]{3,2,1,0:T(8,...) while((s32[]{:T(128)}, f32[2,128,384]{2,1,0:T(8,128)}, ...), condition=%wide.region_180.185_spmd.clone.clone, body=%wide.region_169.184_spmd.clone.clone.sunk | while | flops 662180928 | bytes 26401804 | solution.py:171
  4654.1 82.9 %all-reduce.203.cloned.1.call-done = f32[256,2048]{1,0:T(8,128)} async-done(((f32[256,2048]{1,0:T(8,128)}), f32[256,2048]{1,0:T(8,128)}) %all-reduce.203.cloned.1.call-update) | async-done | bytes 2097168 | tf_op jit(solution)/shard_map/psum | solution.py:539
  4841.6 158.2 %while.694 = (s32[]{:T(128)}, f32[2,128,384]{2,1,0:T(8,128)}, f32[4,2,64,384]{3,2,1,0:T(8,128)}, pred[4,2,64,64]{3,2,1,0:T(32,128)(4,1)}, f32[4,2,64,64]{3,2,1,0...) while((s32[]{:T(128)}, f32[2,128,384]{2,1,0:T(8,128)}, ...), condition=%wide.region_194.199_spmd.clone, body=%wide.region_191.198_spmd.clone.sunk | while | flops 327972096 | bytes 9603193 | solution.py:171
  5050.2 196.4 %while.699 = (s32[]{:T(128)}, f32[2,128,384]{2,1,0:T(8,128)}, f32[4,2,64,128]{3,2,1,0:T(8,128)}, f32[4,2,64,128]{3,2,1,0:T(8,128)}, f32[4,2,64,256]{3,2,1,0:T(8,...) while((s32[]{:T(128)}, f32[2,128,384]{2,1,0:T(8,128)}, ...), condition=%wide.region_210.215_spmd.clone.clone, body=%wide.region_199.214_spmd.clone.clone.sunk | while | flops 662180928 | bytes 26401804 | solution.py:171
  5317.8 56.6 all-reduce.207.cloned.1.call-done
  5639.8 46.5 reduce-scatter.34.cloned.1.call-done
  5686.3 95.4 %reduce-scatter.40.cloned.1.call-done = f32[512,1408]{1,0:T(8,128)} async-done(((f32[2048,1408]{1,0:T(8,128)}), f32[512,1408]{1,0:T(8,128)}) %reduce-scatter.40.cloned.1.call-update) | async-done | bytes 2883600 | tf_op jit(solution)/shard_map/reduce_scatter | solution.py:576
  5781.7 95.4 %reduce-scatter.42.cloned.1.call-done = f32[512,1408]{1,0:T(8,128)} async-done(((f32[2048,1408]{1,0:T(8,128)}), f32[512,1408]{1,0:T(8,128)}) %reduce-scatter.42.cloned.1.call-update) | async-done | bytes 2883600 | tf_op jit(solution)/shard_map/reduce_scatter | solution.py:577
  5877.1 95.4 %reduce-scatter.44.cloned.1.call-done = f32[1408,512]{1,0:T(8,128)} async-done(((f32[1408,2048]{1,0:T(8,128)}), f32[1408,512]{1,0:T(8,128)}) %reduce-scatter.44.cloned.1.call-update) | async-done | bytes 2883600 | tf_op jit(solution)/shard_map/reduce_scatter | solution.py:579
  (6431 shorter events, 4764.7 us)
Async XLA Ops:
  9.3 252.2 %all-gather.59.cloned.1.call-start = ((), (), s32[]{:S(2)}) async-start(), calls=%async_computation.52 | async-start | bytes 1310720 | tf_op jit(solution)/shard_map/all_gather | solution.py:23
  10.0 229.2 %collective-permute-start.3 = (f32[2,128,256]{2,1,0:T(8,128)}, f32[2,128,256]{2,1,0:T(8,128)}, u32[]{:S(2)}, u32[]{:S(2)}) collective-permute-start(f32[2,128,256]{2,1,0:T(8,128)} %broadcast.3249), channel_id=1, source_target_pairs={{0,4},{4,8},{8,12},{12,0},{1,5},{5,9},{9,13},{13,1},{2,6},{6,10},{... | collective-permute-start | bytes 786440 | tf_op jit(solution)/shard_map/ppermute | solution.py:18
  448.7 271.7 %all-gather.61.cloned.1.call-start = ((), (), s32[]{:S(2)}) async-start(), calls=%async_computation.53 | async-start | bytes 1310720 | tf_op jit(solution)/shard_map/all_gather | solution.py:23
  453.1 246.6 %collective-permute-start.8 = (f32[2,128,256]{2,1,0:T(8,128)}, f32[2,128,256]{2,1,0:T(8,128)}, u32[]{:S(2)}, u32[]{:S(2)}) collective-permute-start(f32[2,128,256]{2,1,0:T(8,128)} %fusion.1252), channel_id=1, source_target_pairs={{0,4},{4,8},{8,12},{12,0},{1,5},{5,9},{9,13},{13,1},{2,6},{6,10},{... | collective-permute-start | bytes 786440 | tf_op jit(solution)/shard_map/ppermute | solution.py:18
  907.2 271.4 %all-gather.63.cloned.1.call-start = ((), (), s32[]{:S(2)}) async-start(), calls=%async_computation.54 | async-start | bytes 1310720 | tf_op jit(solution)/shard_map/all_gather | solution.py:23
  911.6 246.4 %collective-permute-start.13 = (f32[2,128,256]{2,1,0:T(8,128)}, f32[2,128,256]{2,1,0:T(8,128)}, u32[]{:S(2)}, u32[]{:S(2)}) collective-permute-start(f32[2,128,256]{2,1,0:T(8,128)} %fusion.1251), channel_id=1, source_target_pairs={{0,4},{4,8},{8,12},{12,0},{1,5},{5,9},{9,13},{13,1},{2,6},{6,10},{... | collective-permute-start | bytes 786440 | tf_op jit(solution)/shard_map/ppermute | solution.py:18
  1365.6 271.8 %all-gather.65.cloned.1.call-start = ((), (), s32[]{:S(2)}) async-start(), calls=%async_computation.55 | async-start | bytes 1310720 | tf_op jit(solution)/shard_map/all_gather | solution.py:23
  1370.1 246.7 %collective-permute-start.18 = (f32[2,128,256]{2,1,0:T(8,128)}, f32[2,128,256]{2,1,0:T(8,128)}, u32[]{:S(2)}, u32[]{:S(2)}) collective-permute-start(f32[2,128,256]{2,1,0:T(8,128)} %fusion.1250), channel_id=1, source_target_pairs={{0,4},{4,8},{8,12},{12,0},{1,5},{5,9},{9,13},{13,1},{2,6},{6,10},{... | collective-permute-start | bytes 786440 | tf_op jit(solution)/shard_map/ppermute | solution.py:18
  1824.2 247.9 %all-gather.67.cloned.1.call-start = ((), (), s32[]{:S(2)}) async-start(), calls=%async_computation.56 | async-start | bytes 1310720 | tf_op jit(solution)/shard_map/all_gather | solution.py:23
  1828.7 224.4 %collective-permute-start.23 = (f32[2,128,256]{2,1,0:T(8,128)}, f32[2,128,256]{2,1,0:T(8,128)}, u32[]{:S(2)}, u32[]{:S(2)}) collective-permute-start(f32[2,128,256]{2,1,0:T(8,128)} %fusion.1249), channel_id=1, source_target_pairs={{0,4},{4,8},{8,12},{12,0},{1,5},{5,9},{9,13},{13,1},{2,6},{6,10},{... | collective-permute-start | bytes 786440 | tf_op jit(solution)/shard_map/ppermute | solution.py:18
  2088.3 353.0 %all-reduce.189.cloned.1.call-start = ((), (), s32[]{:S(2)}) async-start(), calls=%async_computation.29 | async-start | bytes 4194304 | tf_op jit(solution)/shard_map/psum | solution.py:469
  2244.1 229.8 %all-gather.69.cloned.1.call-start = ((), (), s32[]{:S(2)}) async-start(), calls=%async_computation.57 | async-start | bytes 1310720 | tf_op jit(solution)/shard_map/all_gather | solution.py:23
  2458.1 355.8 %all-reduce.191.cloned.1.call-start = ((), (), s32[]{:S(2)}) async-start(), calls=%async_computation.30 | async-start | bytes 4194304 | tf_op jit(solution)/shard_map/psum | solution.py:539
  2838.3 249.1 %all-reduce.193.cloned.1.call-start = ((), (), s32[]{:S(2)}) async-start(), calls=%async_computation.32 | async-start | bytes 4194304 | tf_op jit(solution)/shard_map/psum | solution.py:469
  3102.4 359.7 %all-reduce.195.cloned.1.call-start = ((), (), s32[]{:S(2)}) async-start(), calls=%async_computation.33 | async-start | bytes 4194304 | tf_op jit(solution)/shard_map/psum | solution.py:539
  3485.0 246.6 %all-reduce.197.cloned.1.call-start = ((), (), s32[]{:S(2)}) async-start(), calls=%async_computation.35 | async-start | bytes 4194304 | tf_op jit(solution)/shard_map/psum | solution.py:469
  3746.4 354.0 %all-reduce.199.cloned.1.call-start = ((), (), s32[]{:S(2)}) async-start(), calls=%async_computation.36 | async-start | bytes 4194304 | tf_op jit(solution)/shard_map/psum | solution.py:539
  4123.3 247.2 %all-reduce.201.cloned.1.call-start = ((), (), s32[]{:S(2)}) async-start(), calls=%async_computation.38 | async-start | bytes 4194304 | tf_op jit(solution)/shard_map/psum | solution.py:469
  4385.5 351.5 %all-reduce.203.cloned.1.call-start = ((), (), s32[]{:S(2)}) async-start(), calls=%async_computation.39 | async-start | bytes 4194304 | tf_op jit(solution)/shard_map/psum | solution.py:539
  4759.9 248.8 %all-reduce.205.cloned.1.call-start = ((), (), s32[]{:S(2)}) async-start(), calls=%async_computation.41 | async-start | bytes 4194304 | tf_op jit(solution)/shard_map/psum | solution.py:469
  5022.9 351.5 %all-reduce.207.cloned.1.call-start = ((), (), s32[]{:S(2)}) async-start(), calls=%async_computation.42 | async-start | bytes 4194304 | tf_op jit(solution)/shard_map/psum | solution.py:539
  5288.9 311.5 %reduce-scatter.28.cloned.1.call-start = ((), (), s32[]{:S(2)}) async-start(), calls=%async_computation.28 | async-start | bytes 2621440 | tf_op jit(solution)/shard_map/reduce_scatter | solution.py:396
  5307.4 329.0 %reduce-scatter.46.cloned.1.call-start = ((), (), s32[]{:S(2)}) async-start(), calls=%async_computation.62 | async-start | bytes 1310720
  5381.6 256.4 %reduce-scatter.48.cloned.1.call-start = ((), (), s32[]{:S(2)}) async-start(), calls=%async_computation.63 | async-start | bytes 1310720
  5385.9 253.8 %reduce-scatter.30.cloned.1.call-start = ((), (), s32[]{:S(2)}) async-start(), calls=%async_computation.43 | async-start | bytes 2621440 | tf_op jit(solution)/shard_map/reduce_scatter | solution.py:570
  5389.7 250.0 %reduce-scatter.32.cloned.1.call-start = ((), (), s32[]{:S(2)}) async-start(), calls=%async_computation.44 | async-start | bytes 2621440 | tf_op jit(solution)/shard_map/reduce_scatter | solution.py:571
  5397.4 242.3 %reduce-scatter.36.cloned.1.call-start = ((), (), s32[]{:S(2)}) async-start(), calls=%async_computation.46 | async-start | bytes 5242880 | tf_op jit(solution)/shard_map/reduce_scatter | solution.py:573
  5407.3 232.4 %reduce-scatter.38.cloned.1.call-start = ((), (), s32[]{:S(2)}) async-start(), calls=%async_computation.47 | async-start | bytes 5242880 | tf_op jit(solution)/shard_map/reduce_scatter | solution.py:578
  5439.3 247.0 %reduce-scatter.34.cloned.1.call-start = ((), (), s32[]{:S(2)}) async-start(), calls=%async_computation.45 | async-start | bytes 5242880 | tf_op jit(solution)/shard_map/reduce_scatter | solution.py:572
  5448.8 332.9 %reduce-scatter.40.cloned.1.call-start = ((), (), s32[]{:S(2)}) async-start(), calls=%async_computation.48 | async-start | bytes 14417920 | tf_op jit(solution)/shard_map/reduce_scatter | solution.py:576
  5500.8 376.3 %reduce-scatter.42.cloned.1.call-start = ((), (), s32[]{:S(2)}) async-start(), calls=%async_computation.49 | async-start | bytes 14417920 | tf_op jit(solution)/shard_map/reduce_scatter | solution.py:577
  5551.4 421.1 %reduce-scatter.44.cloned.1.call-start = ((), (), s32[]{:S(2)}) async-start(), calls=%async_computation.50 | async-start | bytes 14417920 | tf_op jit(solution)/shard_map/reduce_scatter | solution.py:579
  (1623 other events, 15062.9 us)
Sparse Core Ops, SparseCore 0:
  10.2 48.6 all-gather.56
  277.8 86.5 all-reduce.178
  448.8 46.4 all-gather.40
  737.1 84.5 all-reduce.180
  907.4 46.4 all-gather.42
  1195.4 84.6 all-reduce.182
  1304.2 42.9 reduce-scatter.23
  1365.7 46.4 all-gather.44
  1654.1 84.5 all-reduce.184
  1762.8 42.8 reduce-scatter.25
  1824.3 46.4 all-gather.46
  2088.4 85.5 all-reduce.186
  2244.2 85.4 all-reduce.188
  2727.4 86.4 all-reduce.190
  2838.4 44.1 all-gather.48
  2901.6 84.5 all-reduce.192
  3377.0 85.0 all-reduce.194
  3485.1 44.1 all-gather.50
  3548.3 84.6 all-reduce.196
  4014.4 85.8 all-reduce.198
  4123.5 44.1 all-gather.52
  4186.6 84.5 all-reduce.200
  4651.7 85.2 all-reduce.202
  4760.0 44.1 all-gather.54
  4823.2 84.5 all-reduce.204
  5289.0 85.3 all-reduce.206
  5546.1 44.5 reduce-scatter.35
  5593.8 45.2 reduce-scatter.37
  5642.1 44.1 reduce-scatter.33
  5689.5 92.1 reduce-scatter.39
  5784.9 92.1 reduce-scatter.41
  5880.3 92.1 reduce-scatter.43
  (17 shorter events, 408.5 us)
where the time goes:
time: 6040 us; the launch traced here: 5980 us
  waiting for transfers between devices  1640 us (27%)
  matrix products  1620 us (27%)
  other arithmetic  1490 us (25%)
  local copies, waits for them, and re-layouts  1030 us (17%)
  blocking collectives  122 us (2%)
    dot_general x543, matrix products, matmul_high(): return jnp.matmul(first_matrix, second_matrix, precision=TOP_PRECISION)  862 us
    another operation x260, other arithmetic, block_step(): lax.linalg.triangular_solve(mixing, target, left_side=True, lower=True, u...  721 us
    psum x5, waiting for transfers between devices, local(): hidden_grad, head_gain_total = lax.psum((mixer_part, head_gain_grad), 'tp')  390 us
    psum x5, waiting for transfers between devices, local(): lax.psum(jnp.dot(gated, out_weight, preferred_element_type=jnp.float32),...  386 us
    all_gather x9, waiting for transfers between devices, gather_rows(): return lax.all_gather(rows_part, 'tp', axis=0, tiled=True)  247 us
    dot_general x50, matrix products, inner_left(): lax.dot_general(first_matrix, second_matrix, (((0,), (0,)), ((), ())), pr...  204 us
    another operation x257, local copies, waits for them, and re-layouts  200 us
    reduce_scatter x5, waiting for transfers between devices, local(): lax.psum_scatter(jnp.dot(inner_act, down_weight, preferred_element_type=j...  166 us

commit v1 on v0

v1 whole, which is shorter than its diff:
```python
from functools import partial

import jax
import jax.numpy as jnp
from jax import lax
from jax.experimental import pallas as pl
from jax.experimental.pallas import tpu as pltpu
from jax.sharding import PartitionSpec as P

EPSILON = 1e-06
F32 = jnp.float32
LOW = jnp.bfloat16
VMEM_BYTES = 48 * 1024 * 1024


def full_dot(a, b, contract=((1,), (0,))):
    return lax.dot_general(
        a, b, (contract, ((), ())), precision=lax.Precision.HIGHEST, preferred_element_type=F32
    )


def low_dot(a, b, contract=((1,), (0,))):
    return lax.dot_general(a, b, (contract, ((), ())), preferred_element_type=F32)


NN = ((1,), (0,))
NT = ((1,), (1,))
TN = ((0,), (0,))


def sigmoid(x):
    return 1.0 / (1.0 + jnp.exp(-x))


def places(size):
    return (
        lax.broadcasted_iota(jnp.int32, (size, size), 0),
        lax.broadcasted_iota(jnp.int32, (size, size), 1),
    )


def unit_lower_inverse(strict_part, rows, cols):
    size = strict_part.shape[0]
    inner = jnp.where((rows >> 3) == (cols >> 3), strict_part, 0.0)
    second = full_dot(inner, inner)
    fourth = full_dot(second, second)
    inverse = jnp.where(rows == cols, 1.0, 0.0) - inner
    inverse = inverse + full_dot(inverse, second)
    inverse = inverse + full_dot(inverse, fourth)
    level = 3
    while (1 << level) < size:
        joined = ((rows >> (level + 1)) == (cols >> (level + 1))) & ((rows >> level) != (cols >> level))
        inverse = inverse - full_dot(inverse, full_dot(jnp.where(joined, strict_part, 0.0), inverse))
        level += 1
    return inverse


def with_border(border, values):
    return jnp.concatenate([border, values], 0)


def taps_back(padded, steps):
    rolled = padded if steps == 0 else pltpu.roll(padded, steps, 0)
    return rolled[8:]


def conv_sum(padded, taps):
    count = taps.shape[0]
    total = taps[0:1] * taps_back(padded, count - 1)
    for member in range(1, count):
        total = total + taps[member : member + 1] * taps_back(padded, count - 1 - member)
    return total


def conv_transposed(grad, taps):
    count = taps.shape[0]
    padded = jnp.concatenate([jnp.zeros((8, grad.shape[1]), F32), grad], 0)
    size = padded.shape[0]
    total = taps[count - 1 : count] * padded
    for member in range(count - 1):
        total = total + taps[member : member + 1] * pltpu.roll(padded, size - (count - 1 - member), 0)
    return total


def conv_taps_grad(padded, grad, count):
    return jnp.concatenate(
        [
            jnp.sum(grad * taps_back(padded, count - 1 - member), 0, keepdims=True)
            for member in range(count)
        ],
        0,
    )


def pick_lane(values, lane):
    lanes = lax.broadcasted_iota(jnp.int32, values.shape, 1)
    return jnp.sum(jnp.where(lanes == lane, values, 0.0), 1, keepdims=True)


def softplus(x):
    return jnp.maximum(x, 0.0) + jnp.log(1.0 + jnp.exp(-jnp.abs(x)))


def token_gates(side, resets, head, heads, rate, bias):
    size = side.shape[0]
    rows, cols = places(size)
    shifted = pick_lane(side, head) + bias
    log_decay = -rate * softplus(shifted)
    beta = sigmoid(pick_lane(side, heads + head))
    lanes = lax.broadcasted_iota(jnp.int32, (size, 128), 1)
    pair = jnp.where(lanes == 0, log_decay, jnp.where(lanes == 1, resets, 0.0))
    lower = jnp.where(rows >= cols, 1.0, 0.0)
    as_columns = full_dot(lower, pair)
    as_rows = full_dot(pair, lower, ((0,), (1,)))
    total, count = as_columns[:, 0:1], as_columns[:, 1:2]
    linked = (jnp.abs(count - as_rows[1:2, :]) < 0.5) & (rows >= cols)
    decays = jnp.where(linked, jnp.exp(jnp.minimum(total - as_rows[0:1, :], 0.0)), 0.0)
    last_total, last_count = total[size - 1 : size], count[size - 1 : size]
    head_decay = jnp.where(count < 0.5, jnp.exp(total), 0.0)
    tail_decay = jnp.where(
        jnp.abs(count - last_count) < 0.5, jnp.exp(jnp.minimum(last_total - total, 0.0)), 0.0
    )
    return shifted, log_decay, beta, decays, head_decay, tail_decay, rows, cols, lower


def silu_unit(summed, scale):
    gate = sigmoid(summed)
    act = summed * gate
    inverse = lax.rsqrt(jnp.sum(act * act, 1, keepdims=True) + EPSILON)
    return act, gate, inverse, act * (inverse * scale)


def silu_unit_back(grad, summed, gate, act, inverse, scale):
    unit = act * inverse
    grad = grad * scale
    act_grad = inverse * (grad - unit * jnp.sum(grad * unit, 1, keepdims=True))
    return act_grad * gate * (1.0 + summed * (1.0 - gate))


def local_kernel(
    heads, query_ref, key_ref, value_ref, side_ref, resets_ref, border_q, border_k, border_v,
    taps_q, taps_k, taps_v, rate_ref, bias_ref, carried_ref, local_ref, map_ref, inverse_ref,
):
    head = pl.program_id(0)
    key_size = query_ref.shape[1]
    _, _, beta, decays, head_decay, tail_decay, rows, cols, _ = token_gates(
        side_ref[...], resets_ref[:, 0:1], head, heads, rate_ref[head], bias_ref[head]
    )
    query = silu_unit(conv_sum(with_border(border_q[...], query_ref[...]), taps_q[...]), key_size**-0.5)[3]
    key = silu_unit(conv_sum(with_border(border_k[...], key_ref[...]), taps_k[...]), 1.0)[3]
    summed = conv_sum(with_border(border_v[...], value_ref[...]), taps_v[...])
    value = summed * sigmoid(summed)
    gram = full_dot(key, key, NT)
    mixing = beta * jnp.where(rows > cols, decays * gram, 0.0)
    inverse = unit_lower_inverse(mixing, rows, cols)
    inverse_ref[0] = inverse
    both = full_dot(inverse, jnp.concatenate([(beta * head_decay) * key, beta * value], 1))
    scores = full_dot(query, key, NT) * decays
    read = full_dot(scores, both)
    carried_ref[...] = head_decay * query - read[:, :key_size]
    local_ref[...] = read[:, key_size:]
    written = full_dot(key * tail_decay, both, TN)
    size = key.shape[0]
    krows, kcols = places(key_size)
    kept = jnp.where(krows == kcols, head_decay[size - 1 : size], 0.0)
    map_ref[0] = jnp.concatenate([kept - written[:, :key_size], written[:, key_size:]], 1)


def gate_kernel(
    me_ref, maps_ref, state_ref, carried_ref, local_ref, outgate_ref, gain_ref,
    gated_ref, output_ref, entry_ref, end_ref,
):
    key_size = state_ref.shape[1]
    me = me_ref[0]
    state = state_ref[0]
    entry = state
    for at in range(maps_ref.shape[0]):
        if at:
            entry = jnp.where(me == at, state, entry)
        step = maps_ref[at, 0]
        state = full_dot(step[:, :key_size], state) + step[:, key_size:]
    entry_ref[0] = entry
    end_ref[0] = state
    output = local_ref[...] + full_dot(carried_ref[...], entry)
    output_ref[...] = output
    normed = output * lax.rsqrt(jnp.mean(output * output, 1, keepdims=True) + EPSILON) * gain_ref[...]
    gate = outgate_ref[...]
    gated_ref[...] = (normed * (gate * sigmoid(gate))).astype(LOW).astype(F32)


def gate_back_kernel(
    top_ref, weight_ref, output_ref, outgate_ref, gain_ref, carried_ref,
    top_low_ref, output_grad_ref, outgate_grad_ref, gain_grad_ref, entry_ref,
):
    top_low = top_ref[...].astype(LOW)
    top_low_ref[...] = top_low
    grad = low_dot(top_low, weight_ref[...], NT)
    output, gate, gain = output_ref[...], outgate_ref[...], gain_ref[...]
    inverse = lax.rsqrt(jnp.mean(output * output, 1, keepdims=True) + EPSILON)
    unit = output * inverse
    opened = sigmoid(gate)
    swished = gate * opened
    outgate_grad_ref[...] = (grad * unit * gain * (opened * (1.0 + gate * (1.0 - opened)))).astype(LOW)
    gain_grad_ref[0] = jnp.sum(grad * unit * swished, 0, keepdims=True)
    unit_grad = grad * gain * swished
    output_grad = inverse * (unit_grad - unit * jnp.mean(unit_grad * unit, 1, keepdims=True))
    output_grad_ref[...] = output_grad
    entry_ref[0] = full_dot(carried_ref[...], output_grad, TN)


def local_back_kernel(
    heads, me_ref, maps_ref, entries_ref, state_grad_ref, query_ref, key_ref, value_ref, side_ref,
    resets_ref, border_q, border_k, border_v, taps_q, taps_k, taps_v, rate_ref, bias_ref,
    inverse_ref, entry_state_ref, output_grad_ref,
    dquery_ref, dkey_ref, dvalue_ref, dborder_q, dborder_k, dborder_v, dtaps_q, dtaps_k, dtaps_v,
    dside_ref, start_grad_ref,
):
    head = pl.program_id(0)
    key_size = query_ref.shape[1]
    size = query_ref.shape[0]
    scale = key_size**-0.5
    me = me_ref[0]
    state_grad = state_grad_ref[0]
    end_grad = state_grad
    count = maps_ref.shape[0]
    for at in reversed(range(count)):
        if at < count - 1:
            end_grad = jnp.where(me == at, state_grad, end_grad)
        state_grad = full_dot(maps_ref[at, 0], state_grad, TN) + entries_ref[at, 0]
    start_grad_ref[0] = state_grad

    shifted, log_decay, beta, decays, head_decay, tail_decay, rows, cols, lower = token_gates(
        side_ref[...], resets_ref[:, 0:1], head, heads, rate_ref[head], bias_ref[head]
    )
    padded_q = with_border(border_q[...], query_ref[...])
    padded_k = with_border(border_k[...], key_ref[...])
    padded_v = with_border(border_v[...], value_ref[...])
    summed_q = conv_sum(padded_q, taps_q[...])
    summed_k = conv_sum(padded_k, taps_k[...])
    summed_v = conv_sum(padded_v, taps_v[...])
    act_q, gate_q, inverse_q, query = silu_unit(summed_q, scale)
    act_k, gate_k, inverse_k, key = silu_unit(summed_k, 1.0)
    gate_v = sigmoid(summed_v)
    value = summed_v * gate_v
    state = entry_state_ref[0]
    inverse = inverse_ref[0]
    output_grad = output_grad_ref[...]

    gram = full_dot(key, key, NT)
    pure = full_dot(query, key, NT)
    scores = pure * decays
    tail_key = key * tail_decay
    residue = value - head_decay * full_dot(key, state)
    update = full_dot(inverse, beta * residue)
    update_grad = full_dot(scores, output_grad, TN) + full_dot(tail_key, end_grad)
    target_grad = full_dot(inverse, update_grad, TN)
    strict = rows > cols
    mixing_grad = jnp.where(strict, -full_dot(target_grad, update, NT), 0.0)
    scores_grad = full_dot(output_grad, update, NT)
    pure_grad = scores_grad * decays
    reached = full_dot(output_grad, state, NT)
    erased = full_dot(target_grad, state, NT)
    kept = full_dot(update, end_grad, NT)
    weighted = mixing_grad * decays
    gram_grad = weighted * beta
    query_grad = head_decay * reached + full_dot(pure_grad, key)
    key_grad = (
        full_dot(pure_grad, query, TN)
        + tail_decay * kept
        - (beta * head_decay) * erased
        + full_dot(gram_grad, key)
        + full_dot(gram_grad, key, TN)
    )
    value_grad = beta * target_grad
    beta_grad = jnp.sum(target_grad * residue, 1, keepdims=True) + jnp.sum(
        weighted * gram, 1, keepdims=True
    )
    spread = pure_grad * pure + gram_grad * gram
    head_decay_grad = jnp.sum(query * reached, 1, keepdims=True) - beta * jnp.sum(
        key * erased, 1, keepdims=True
    )
    tail_part = tail_decay * jnp.sum(key * kept, 1, keepdims=True)
    ones = jnp.ones((size, 128), F32)
    column_sums = full_dot(spread, ones, TN)[:, 0:1]
    total_grad = (
        head_decay * head_decay_grad - tail_part + jnp.sum(spread, 1, keepdims=True) - column_sums
    )
    last_grad = jnp.sum(tail_part, 0, keepdims=True) + head_decay[size - 1 : size] * jnp.sum(
        jnp.sum(end_grad * state, 1, keepdims=True), 0, keepdims=True
    )
    places_col = lax.broadcasted_iota(jnp.int32, (size, 1), 0)
    total_grad = total_grad + jnp.where(places_col == size - 1, last_grad, 0.0)
    lanes = lax.broadcasted_iota(jnp.int32, (size, 128), 1)
    log_grad = full_dot(lower, jnp.where(lanes == 0, total_grad, 0.0), TN)[:, 0:1]
    decay_grad = log_grad * (-rate_ref[head]) * sigmoid(shifted)
    beta_in_grad = beta_grad * beta * (1.0 - beta)
    dside_ref[0] = jnp.where(
        lanes == 0,
        decay_grad,
        jnp.where(lanes == 1, beta_in_grad, jnp.where(lanes == 2, log_grad * log_decay, 0.0)),
    )

    summed_q_grad = silu_unit_back(query_grad, summed_q, gate_q, act_q, inverse_q, scale)
    summed_k_grad = silu_unit_back(key_grad, summed_k, gate_k, act_k, inverse_k, 1.0)
    summed_v_grad = value_grad * gate_v * (1.0 + summed_v * (1.0 - gate_v))
    for grad, padded, taps, out, border_out, taps_out in (
        (summed_q_grad, padded_q, taps_q, dquery_ref, dborder_q, dtaps_q),
        (summed_k_grad, padded_k, taps_k, dkey_ref, dborder_k, dtaps_k),
        (summed_v_grad, padded_v, taps_v, dvalue_ref, dborder_v, dtaps_v),
    ):
        spread_out = conv_transposed(grad, taps[...])
        border_out[...] = spread_out[:8]
        out[...] = spread_out[8:]
        taps_out[...] = conv_taps_grad(padded, grad, taps.shape[0])


def block(shape, place):
    return pl.BlockSpec(shape, place)


def smem():
    return pl.BlockSpec(memory_space=pltpu.SMEM)


def params():
    return pltpu.CompilerParams(vmem_limit_bytes=VMEM_BYTES)


def projection_specs(rows, heads, key_size, value_size, count):
    ratio = value_size // key_size
    return [
        block((rows, key_size), lambda h: (0, h)),
        block((rows, key_size), lambda h: (0, heads + h)),
        block((rows, value_size), lambda h: (0, 2 * heads // ratio + h)),
        block((rows, 128), lambda h: (0, (2 + 2 * ratio) * heads * key_size // 128)),
        block((rows, 128), lambda h: (0, 0)),
        block((8, key_size), lambda h: (0, h)),
        block((8, key_size), lambda h: (0, heads + h)),
        block((8, value_size), lambda h: (0, 2 * heads // ratio + h)),
        block((count, key_size), lambda h: (0, h)),
        block((count, key_size), lambda h: (0, h)),
        block((count, value_size), lambda h: (0, h)),
        smem(),
        smem(),
    ]


def mixer_local(sizes, projected, resets, border, taps, rate, bias):
    heads, key_size, value_size = sizes
    rows = projected.shape[0]
    return pl.pallas_call(
        partial(local_kernel, heads),
        grid=(heads,),
        in_specs=projection_specs(rows, heads, key_size, value_size, taps[0].shape[0]),
        out_specs=[
            block((rows, key_size), lambda h: (0, h)),
            block((rows, value_size), lambda h: (0, h)),
            block((1, key_size, key_size + value_size), lambda h: (h, 0, 0)),
            block((1, rows, rows), lambda h: (h, 0, 0)),
        ],
        out_shape=[
            jax.ShapeDtypeStruct((rows, heads * key_size), F32),
            jax.ShapeDtypeStruct((rows, heads * value_size), F32),
            jax.ShapeDtypeStruct((heads, key_size, key_size + value_size), F32),
            jax.ShapeDtypeStruct((heads, rows, rows), F32),
        ],
        compiler_params=params(),
        name="mixer_local",
    )(projected, projected, projected, projected, resets, border, border, border, *taps, rate, bias)


def mixer_gate(sizes, me, maps, state, carried, local, projected, gain):
    heads, key_size, value_size = sizes
    rows = projected.shape[0]
    ratio = value_size // key_size
    seq = maps.shape[0]
    return pl.pallas_call(
        gate_kernel,
        grid=(heads,),
        in_specs=[
            smem(),
            block((seq, 1, key_size, key_size + value_size), lambda h: (0, h, 0, 0)),
            block((1, key_size, value_size), lambda h: (h, 0, 0)),
            block((rows, key_size), lambda h: (0, h)),
            block((rows, value_size), lambda h: (0, h)),
            block((rows, value_size), lambda h: (0, 2 * heads // ratio + heads + h)),
            block((1, value_size), lambda h: (0, 0)),
        ],
        out_specs=[
            block((rows, value_size), lambda h: (0, h)),
            block((rows, value_size), lambda h: (0, h)),
            block((1, key_size, value_size), lambda h: (h, 0, 0)),
            block((1, key_size, value_size), lambda h: (h, 0, 0)),
        ],
        out_shape=[
            jax.ShapeDtypeStruct((rows, heads * value_size), F32),
            jax.ShapeDtypeStruct((rows, heads * value_size), F32),
            jax.ShapeDtypeStruct((heads, key_size, value_size), F32),
            jax.ShapeDtypeStruct((heads, key_size, value_size), F32),
        ],
        compiler_params=params(),
        name="mixer_gate",
    )(me, maps, state, carried, local, projected, gain)


def mixer_gate_back(sizes, top, weight, output, projected, gain, carried):
    heads, key_size, value_size = sizes
    rows, width = top.shape
    ratio = value_size // key_size
    return pl.pallas_call(
        gate_back_kernel,
        grid=(heads,),
        in_specs=[
            block((rows, width), lambda h: (0, 0)),
            block((value_size, width), lambda h: (h, 0)),
            block((rows, value_size), lambda h: (0, h)),
            block((rows, value_size), lambda h: (0, 2 * heads // ratio + heads + h)),
            block((1, value_size), lambda h: (0, 0)),
            block((rows, key_size), lambda h: (0, h)),
        ],
        out_specs=[
            block((rows, width), lambda h: (0, 0)),
            block((rows, value_size), lambda h: (0, h)),
            block((rows, value_size), lambda h: (0, h)),
            block((1, 1, value_size), lambda h: (h, 0, 0)),
            block((1, key_size, value_size), lambda h: (h, 0, 0)),
        ],
        out_shape=[
            jax.ShapeDtypeStruct((rows, width), LOW),
            jax.ShapeDtypeStruct((rows, heads * value_size), F32),
            jax.ShapeDtypeStruct((rows, heads * value_size), LOW),
            jax.ShapeDtypeStruct((heads, 1, value_size), F32),
            jax.ShapeDtypeStruct((heads, key_size, value_size), F32),
        ],
        compiler_params=params(),
        name="mixer_gate_back",
    )(top, weight, output, projected, gain, carried)


def mixer_local_back(
    sizes, me, maps, entries, state_grad, projected, resets, border, taps, rate, bias, inverse,
    entry_state, output_grad,
):
    heads, key_size, value_size = sizes
    rows = projected.shape[0]
    seq = maps.shape[0]
    count = taps[0].shape[0]
    q_block = block((rows, key_size), lambda h: (0, h))
    v_block = block((rows, value_size), lambda h: (0, h))
    s_block = block((1, key_size, value_size), lambda h: (h, 0, 0))
    return pl.pallas_call(
        partial(local_back_kernel, heads),
        grid=(heads,),
        in_specs=[
            smem(),
            block((seq, 1, key_size, key_size), lambda h: (0, h, 0, 0)),
            block((seq, 1, key_size, value_size), lambda h: (0, h, 0, 0)),
            s_block,
        ]
        + projection_specs(rows, heads, key_size, value_size, count)
        + [block((1, rows, rows), lambda h: (h, 0, 0)), s_block, v_block],
        out_specs=[
            q_block,
            q_block,
            v_block,
            block((8, key_size), lambda h: (0, h)),
            block((8, key_size), lambda h: (0, h)),
            block((8, value_size), lambda h: (0, h)),
            block((count, key_size), lambda h: (0, h)),
            block((count, key_size), lambda h: (0, h)),
            block((count, value_size), lambda h: (0, h)),
            block((1, rows, 128), lambda h: (h, 0, 0)),
            s_block,
        ],
        out_shape=[
            jax.ShapeDtypeStruct((rows, heads * key_size), F32),
            jax.ShapeDtypeStruct((rows, heads * key_size), F32),
            jax.ShapeDtypeStruct((rows, heads * value_size), F32),
            jax.ShapeDtypeStruct((8, heads * key_size), F32),
            jax.ShapeDtypeStruct((8, heads * key_size), F32),
            jax.ShapeDtypeStruct((8, heads * value_size), F32),
            jax.ShapeDtypeStruct((count, heads * key_size), F32),
            jax.ShapeDtypeStruct((count, heads * key_size), F32),
            jax.ShapeDtypeStruct((count, heads * value_size), F32),
            jax.ShapeDtypeStruct((heads, rows, 128), F32),
            jax.ShapeDtypeStruct((heads, key_size, value_size), F32),
        ],
        compiler_params=params(),
        name="mixer_local_back",
    )(
        me, maps, entries, state_grad, projected, projected, projected, projected, resets,
        border, border, border, *taps, rate, bias, inverse, entry_state, output_grad,
    )


def narrow_kernel(wide_ref, low_ref):
    low_ref[...] = wide_ref[...].astype(LOW)


def widen_kernel(low_ref, wide_ref):
    wide_ref[...] = low_ref[...].astype(F32)


def recast(kernel, values, dtype):
    rows, cols = values.shape
    tile = min(rows, 256)
    return pl.pallas_call(
        kernel,
        grid=(rows // tile,),
        in_specs=[block((tile, cols), lambda i: (i, 0))],
        out_specs=block((tile, cols), lambda i: (i, 0)),
        out_shape=jax.ShapeDtypeStruct((rows, cols), dtype),
        compiler_params=params(),
    )(values)


def join_kernel(rows_ref, gated_ref, weight_ref, gain_ref, mixed_ref, hidden_ref, total):
    step = pl.program_id(0)

    @pl.when(step == 0)
    def _():
        total[...] = rows_ref[...]

    total[...] += low_dot(gated_ref[0].astype(LOW), weight_ref[...])

    @pl.when(step == pl.num_programs(0) - 1)
    def _():
        mixed = total[...]
        mixed_ref[...] = mixed
        inverse = lax.rsqrt(jnp.mean(mixed * mixed, 1, keepdims=True) + EPSILON)
        hidden_ref[...] = (mixed * inverse * gain_ref[...]).astype(LOW)


def join_heads(rows, gated, weight, gain):
    parts, count, depth = gated.shape
    width = weight.shape[1]
    whole = block((count, width), lambda i: (0, 0))
    return pl.pallas_call(
        join_kernel,
        grid=(parts,),
        in_specs=[
            whole,
            block((1, count, depth), lambda i: (i, 0, 0)),
            block((depth, width), lambda i: (i, 0)),
            block((1, width), lambda i: (0, 0)),
        ],
        out_specs=[whole, whole],
        out_shape=[
            jax.ShapeDtypeStruct((count, width), F32),
            jax.ShapeDtypeStruct((count, width), LOW),
        ],
        scratch_shapes=[pltpu.VMEM((count, width), F32)],
        compiler_params=params(),
        name="join_heads",
    )(rows, gated, weight, gain)


def top_kernel(last_ref, given_ref, handed_ref, low_ref):
    given = given_ref[...].astype(F32)
    low_ref[...] = jnp.where(last_ref[0] == 1, given, handed_ref[...]).astype(LOW)


def pick_top(last, given, handed):
    rows, cols = given.shape
    tile = rows // 4
    spec = block((tile, cols), lambda i: (i, 0))
    return pl.pallas_call(
        top_kernel,
        grid=(4,),
        in_specs=[smem(), spec, spec],
        out_specs=spec,
        out_shape=jax.ShapeDtypeStruct((rows, cols), LOW),
        compiler_params=params(),
        name="pick_top",
    )(last, given, handed)


def row_norm(values, gain):
    return values * lax.rsqrt(jnp.mean(values * values, -1, keepdims=True) + EPSILON) * gain


def row_norm_back(values, gain, grad):
    inverse = lax.rsqrt(jnp.mean(values * values, -1, keepdims=True) + EPSILON)
    unit = values * inverse
    scaled = grad * gain
    back = inverse * (scaled - unit * jnp.mean(unit * scaled, -1, keepdims=True))
    return back, jnp.sum(unit * grad, 0)


def ring(value, axis, steps):
    count = lax.axis_size(axis)
    return lax.ppermute(value, axis, [(at, (at + steps) % count) for at in range(count)])


def handed_on(value, axis, steps):
    count = lax.axis_size(axis)
    first, last = max(0, -steps), min(count, count - steps)
    return lax.ppermute(value, axis, [(at, at + steps) for at in range(first, last)])


def scatter_sum(values, axis):
    count = lax.axis_size("seq")
    if count % 2:
        return lax.psum_scatter(values, "seq", scatter_dimension=axis, tiled=True)
    index = lax.axis_index("seq")
    core, chip = index % 2, index // 2
    chips = count // 2
    shape = values.shape
    chunk = shape[axis] // count
    split = values.reshape(shape[:axis] + (chips, 2, chunk) + shape[axis + 1 :])
    pick = lambda array, at, dim: lax.dynamic_index_in_dim(array, at, dim, keepdims=False)
    other = lax.ppermute(
        pick(split, 1 - core, axis + 1), "seq", [(at, at ^ 1) for at in range(count)]
    )
    summed = pick(split, core, axis + 1) + other
    if chips == 2:
        other = lax.ppermute(pick(summed, 1 - chip, axis), "seq", [(at, at ^ 2) for at in range(4)])
        return pick(summed, chip, axis) + other
    summed = summed.reshape(shape[:axis] + (chips * chunk,) + shape[axis + 1 :])
    groups = [[2 * at + half for at in range(chips)] for half in range(2)]
    return lax.psum_scatter(
        summed, "seq", scatter_dimension=axis, axis_index_groups=groups, tiled=True
    )


def local(
    inputs, cotangent, doc_start, norm_in, query_weight, key_weight, value_weight, outgate_weight,
    decay_weight, beta_weight, conv_query, conv_key, conv_value, decay_log, decay_bias, head_norm,
    out_weight, norm_feed, gate_weight, up_weight, down_weight,
):
    query_weight, key_weight, value_weight = query_weight[0], key_weight[0], value_weight[0]
    outgate_weight, decay_weight, beta_weight = outgate_weight[0], decay_weight[0], beta_weight[0]
    gate_weight, up_weight, down_weight, out_weight = (
        gate_weight[0], up_weight[0], down_weight[0], out_weight[0],
    )
    taps = (conv_query[0], conv_key[0], conv_value[0])
    rate, bias = jnp.exp(decay_log[0]), decay_bias[0]
    heads = bias.shape[0]
    key_size = query_weight.shape[1] // heads
    value_size = value_weight.shape[1] // heads
    sizes = (heads, key_size, value_size)
    key_cols, value_cols = heads * key_size, heads * value_size
    micros, own_rows, width = inputs.shape
    rows = cotangent.shape[1]
    seq_size, seq_index = lax.axis_size("seq"), lax.axis_index("seq")
    tp_index = lax.axis_index("tp")
    section = lax.axis_index("section")
    at_start, at_end = seq_index == 0, seq_index == seq_size - 1
    me = seq_index.astype(jnp.int32).reshape(1)
    last_section = section.astype(jnp.int32).reshape(1)
    group = 2 if micros % 2 == 0 else 1
    groups = micros // group

    def own(values):
        return lax.dynamic_slice_in_dim(values, tp_index * own_rows, own_rows, 0)

    part = width // seq_size
    piece = lax.dynamic_slice_in_dim(out_weight, seq_index * part, part, 1)
    piece = lax.all_gather(recast(widen_kernel, piece, F32), "tp", axis=0, tiled=True)
    pieces = lax.all_gather(piece, "seq", axis=0)
    low_pieces = recast(narrow_kernel, pieces.reshape(-1, part), LOW).reshape(pieces.shape)
    out_full = jnp.moveaxis(low_pieces, 0, 1).reshape(-1, width)

    spare = jnp.zeros((width, 128 - 2 * heads), LOW)
    in_weight = jnp.concatenate(
        [query_weight, key_weight, value_weight, outgate_weight, decay_weight, beta_weight, spare], 1
    )
    conv_cols = 2 * key_cols + value_cols
    offsets = jnp.arange(rows, dtype=jnp.int32)

    def micro_of(step, member):
        return jnp.clip(step - section, 0, groups - 1) * group + member

    def reset_flags(micro):
        starts = micro * (rows * seq_size) + seq_index * rows + offsets
        flags = lax.dynamic_index_in_dim(doc_start, micro, 0, keepdims=False) == starts
        return jnp.broadcast_to(flags.astype(F32)[:, None], (rows, 128))

    saved = {}
    section_rows = {}
    received = [jnp.zeros((own_rows, width), F32)] * group
    border_carry = jnp.zeros((8, conv_cols), F32)
    state = jnp.zeros((heads, key_size, value_size), F32)
    for step in range(groups + 1):
        sent = []
        for member in range(group):
            micro = micro_of(step, member)
            given = lax.dynamic_index_in_dim(inputs, micro, 0, keepdims=False).astype(F32)
            entering = jnp.where(section == 0, given, received[member])
            residual = lax.all_gather(entering, "tp", axis=0, tiled=True)
            hidden = row_norm(residual, norm_in).astype(LOW)
            tail = low_dot(hidden[rows - 8 :], in_weight[:, :conv_cols])
            moved = ring(tail, "seq", 1)
            border = jnp.where(at_start, border_carry, moved)
            border_carry = moved
            projected = low_dot(hidden, in_weight)
            resets = reset_flags(micro)
            carried, local_out, maps, inverse = mixer_local(
                sizes, projected, resets, border, taps, rate, bias
            )
            all_maps = lax.all_gather(maps, "seq", axis=0)
            gated, output, entry_state, state = mixer_gate(
                sizes, me, all_maps, state, carried, local_out, projected, head_norm
            )
            mixed, hidden_feed = join_heads(
                residual, lax.all_gather(gated, "tp", axis=0), out_full, norm_feed
            )
            gate_act = low_dot(hidden_feed, gate_weight)
            up_act = low_dot(hidden_feed, up_weight)
            inner = (gate_act * sigmoid(gate_act) * up_act).astype(LOW)
            out_rows = own(mixed) + lax.psum_scatter(
                low_dot(inner, down_weight), "tp", scatter_dimension=0, tiled=True
            )
            section_rows[step, member] = out_rows
            if step < groups:
                sent.append(handed_on(out_rows, "section", 1))
            saved[step, member] = dict(
                entering=entering, hidden=hidden, border=border, projected=projected, resets=resets,
                carried=carried, maps=all_maps[..., :key_size], inverse=inverse, gated=gated,
                output=output, entry_state=entry_state, mixed=own(mixed), hidden_feed=hidden_feed,
                gate_act=gate_act, up_act=up_act, inner=inner,
            )
        received = sent

    received = [jnp.zeros((own_rows, width), F32)] * group
    tail_carry = jnp.zeros((8, conv_cols), F32)
    state_grad = jnp.zeros((heads, key_size, value_size), F32)
    in_grads = {}
    norm_in_grad = jnp.zeros((width,), F32)
    norm_feed_grad = jnp.zeros((width,), F32)
    gain_grad = jnp.zeros((value_size,), F32)
    taps_grads = [jnp.zeros(member.shape, F32) for member in taps]
    side_grad = jnp.zeros((heads, 128), F32)
    for back_step in range(groups + 1):
        step = groups - back_step
        sent = [None] * group
        for member in reversed(range(group)):
            kept = saved[step, member]
            micro = micro_of(step, member)
            given = lax.dynamic_index_in_dim(cotangent, micro, 0, keepdims=False)
            if step == 0:
                given = jnp.where(section == 0, given, jnp.zeros_like(given))
            if back_step:
                handed = lax.all_gather(received[member], "tp", axis=0, tiled=True)
                top_low = pick_top(last_section, given, handed)
            else:
                top_low = jnp.where(section == 0, jnp.zeros_like(given), given)
            top_own = jnp.where(section == 0, received[member], own(given).astype(F32))
            kept["top_low"] = top_low
            inner_grad = low_dot(top_low, down_weight, NT)
            gate_act, up_act = kept["gate_act"], kept["up_act"]
            opened = sigmoid(gate_act)
            gate_low = (inner_grad * up_act * (opened * (1.0 + gate_act * (1.0 - opened)))).astype(LOW)
            up_low = (inner_grad * gate_act * opened).astype(LOW)
            kept["gate_low"], kept["up_low"] = gate_low, up_low
            feed_grad = lax.psum_scatter(
                low_dot(gate_low, gate_weight, NT) + low_dot(up_low, up_weight, NT),
                "tp",
                scatter_dimension=0,
                tiled=True,
            )
            mixed_back, feed_part = row_norm_back(kept["mixed"], norm_feed[0], feed_grad)
            norm_feed_grad = norm_feed_grad + feed_part
            mixed_grad = top_own + mixed_back
            mixed_full = lax.all_gather(mixed_grad, "tp", axis=0, tiled=True)
            mixed_low, output_grad, outgate_low, gain_part, entry_grad = mixer_gate_back(
                sizes, mixed_full, out_weight, kept["output"], kept["projected"], head_norm,
                kept["carried"],
            )
            kept["mixed_low"] = mixed_low
            gain_grad = gain_grad + jnp.sum(gain_part, (0, 1))
            all_entries = lax.all_gather(entry_grad, "seq", axis=0)
            (
                query_grad, key_grad, value_grad, border_q, border_k, border_v, taps_q, taps_k,
                taps_v, side, state_grad,
            ) = mixer_local_back(
                sizes, me, kept["maps"], all_entries, state_grad, kept["projected"],
                kept["resets"], kept["border"], taps, rate, bias, kept["inverse"],
                kept["entry_state"], output_grad,
            )
            moved = ring(jnp.concatenate([border_q, border_k, border_v], 1), "seq", -1)
            tail = jnp.where(at_end, tail_carry, moved)
            tail_carry = moved
            conv_grad = jnp.concatenate([query_grad, key_grad, value_grad], 1)
            conv_grad = jnp.concatenate([conv_grad[: rows - 8], conv_grad[rows - 8 :] + tail], 0)
            projected_low = jnp.concatenate(
                [
                    conv_grad.astype(LOW),
                    outgate_low,
                    side[:, :, 0].T.astype(LOW),
                    side[:, :, 1].T.astype(LOW),
                    jnp.zeros((rows, 128 - 2 * heads), LOW),
                ],
                1,
            )
            kept["projected_low"] = projected_low
            taps_grads = [
                total + part for total, part in zip(taps_grads, (taps_q, taps_k, taps_v))
            ]
            side_grad = side_grad + jnp.sum(side, 1)
            hidden_grad = lax.psum_scatter(
                low_dot(projected_low, in_weight, NT), "tp", scatter_dimension=0, tiled=True
            )
            entering_back, in_part = row_norm_back(kept["entering"], norm_in[0], hidden_grad)
            norm_in_grad = norm_in_grad + in_part
            own_grad = mixed_grad + entering_back
            in_grads[step, member] = own_grad
            if back_step < groups:
                sent[member] = handed_on(own_grad, "section", -1)
        received = sent

    def of_section(values):
        return [
            jnp.where(section == 0, values[at, member], values[at + 1, member])
            for at in range(groups)
            for member in range(group)
        ]

    def all_rows(name):
        outer = [
            jnp.where(section == 0, saved[0, member][name], saved[groups, member][name])
            for member in range(group)
        ]
        inner = [saved[at, member][name] for at in range(1, groups) for member in range(group)]
        return jnp.concatenate(outer + inner, 0)

    hidden_all, hidden_feed_all = all_rows("hidden"), all_rows("hidden_feed")
    top_all = all_rows("top_low")
    grad_gate = scatter_sum(low_dot(hidden_feed_all, all_rows("gate_low"), TN), 0)
    grad_up = scatter_sum(low_dot(hidden_feed_all, all_rows("up_low"), TN), 0)
    grad_down = scatter_sum(low_dot(all_rows("inner"), top_all, TN), 1)
    grad_out = scatter_sum(low_dot(all_rows("gated").astype(LOW), all_rows("mixed_low"), TN), 1)
    grad_in = scatter_sum(low_dot(hidden_all, all_rows("projected_low"), TN), 0)

    own_tp = jnp.arange(lax.axis_size("tp")) == tp_index
    per_tp = jnp.concatenate(
        [member.reshape(-1) for member in taps_grads] + [side_grad[:, 2], side_grad[:, 0]]
    )
    small = lax.psum(
        jnp.concatenate(
            [
                norm_in_grad,
                norm_feed_grad,
                gain_grad,
                jnp.where(own_tp[:, None], per_tp[None], 0.0).reshape(-1),
            ]
        ),
        ("seq", "tp"),
    )
    norm_in_grad, norm_feed_grad = small[:width], small[width : 2 * width]
    gain_grad = small[2 * width : 2 * width + value_size]
    per_tp = lax.dynamic_slice_in_dim(
        small, 2 * width + value_size + tp_index * per_tp.shape[0], per_tp.shape[0], 0
    )
    pieces, at = [], 0
    for member in taps:
        pieces.append(per_tp[at : at + member.size].reshape(member.shape))
        at += member.size
    log_grad, bias_grad = per_tp[at : at + heads], per_tp[at + heads : at + 2 * heads]
    bounds = [
        0, key_cols, 2 * key_cols, conv_cols, conv_cols + value_cols, conv_cols + value_cols + heads,
        conv_cols + value_cols + 2 * heads,
    ]
    in_parts = [grad_in[:, low:high] for low, high in zip(bounds[:-1], bounds[1:])]
    return (
        jnp.stack(of_section(section_rows))[None],
        jnp.stack(of_section(in_grads))[None],
        norm_in_grad[None],
        *[member[None] for member in in_parts],
        *[member[None] for member in pieces],
        log_grad[None],
        bias_grad[None],
        gain_grad[None],
        grad_out[None],
        norm_feed_grad[None],
        grad_gate[None],
        grad_up[None],
        grad_down[None],
    )


def solution(mesh):
    by_column, by_row = P("section", None, "tp"), P("section", "tp", None)
    placed = (
        P(None, ("seq", "tp"), None),
        P(None, "seq", None),
        P(None, "seq"),
        P("section", None),
        *[by_column] * 9,
        P("section", "tp"),
        P("section", "tp"),
        P("section", None),
        by_row,
        P("section", None),
        by_column,
        by_column,
        by_row,
    )
    rows_out = P("section", None, ("seq", "tp"), None)
    both = P("section", "seq", "tp")
    return jax.shard_map(
        local,
        mesh=mesh,
        in_specs=placed,
        out_specs=(
            rows_out,
            rows_out,
            P("section", None),
            *[both] * 6,
            *[by_column] * 3,
            P("section", "tp"),
            P("section", "tp"),
            P("section", None),
            P("section", "tp", "seq"),
            P("section", None),
            both,
            both,
            P("section", "tp", "seq"),
        ),
        check_vma=False,
    )
```

time: 6040 us -> 2900 us (0.48)
  matrix products: 1620 us -> 290 us
  other arithmetic: 1490 us -> 173 us
  local copies, waits for them, and re-layouts: 1030 us -> 449 us
  Pallas kernels: 0 us -> 319 us
  blocking collectives: 122 us -> 0 us
    dot_general x768 -> x59, matrix products: 1470 us -> 290 us  [low_dot(): lax.dot_general(a, b, (contract, ((), ())), preferred_element_type=F32)]
    another operation x355 -> x12, other arithmetic: 784 us -> 21.4 us  [the longest x3 7.68 us: local(): jnp.stack(of_section(in_grads))[None]]
    psum x15 -> x1, waiting for transfers between devices: 776 us -> 83.2 us  [local(): lax.psum(jnp.concatenate([norm_in_grad, norm_feed_grad, gain_grad, jnp.wh...]
    all_gather x19 -> x36, waiting for transfers between devices: 266 us -> 840 us  [the longest x6 261 us: local(): residual = lax.all_gather(entering, 'tp', axis=0, tiled=True)]
    pallas_call x0 -> x36, Pallas kernels: none -> 319 us  [the longest x6 123 us: mixer_local(): pl.pallas_call(partial(local_kernel, heads), grid=(heads,), in_specs=proj...]
    another operation x267 -> x5, local copies, waits for them, and re-layouts: 220 us -> 1.84 us  [the longest x3 1.81 us: local(): member[None]]
    unnamed x1703 -> x940, local copies, waits for them, and re-layouts: 88.4 us -> 248 us
    mul x155 -> x0, local copies, waits for them, and re-layouts: 157 us -> none  [the longest x20 24.9 us: block_step(): head_decay[:, :, None] * matmul_high(query_rows, state_now)]
where the time goes in v1:
time: 2900 us; the launch traced here: 2880 us
  waiting for transfers between devices  1590 us (55%)
  local copies, waits for them, and re-layouts  449 us (15%)
  Pallas kernels  319 us (11%)
  matrix products  290 us (10%)
  other arithmetic  173 us (6%)
  starting transfers between devices  41 us (1%)
    dot_general x59, matrix products, low_dot(): lax.dot_general(a, b, (contract, ((), ())), preferred_element_type=F32)  290 us
    all_gather x6, waiting for transfers between devices, local(): residual = lax.all_gather(entering, 'tp', axis=0, tiled=True)  261 us
    unnamed x940, local copies, waits for them, and re-layouts  248 us
    reduce_scatter x6, waiting for transfers between devices, local(): lax.psum_scatter(low_dot(inner, down_weight), 'tp', scatter_dimension=0,...  209 us
    all_gather x6, waiting for transfers between devices, local(): mixed_full = lax.all_gather(mixed_grad, 'tp', axis=0, tiled=True)  170 us
    all_gather x6, waiting for transfers between devices, local(): lax.all_gather(gated, 'tp', axis=0)  148 us
    reduce_scatter x6, waiting for transfers between devices, local(): lax.psum_scatter(low_dot(projected_low, in_weight, NT), 'tp', scatter_dim...  147 us
    reduce_scatter x6, waiting for transfers between devices, local(): lax.psum_scatter(low_dot(gate_low, gate_weight, NT) + low_dot(up_low, up_...  130 us
  transfers between devices with their start and end apart: 85, of which 56 were waited for; matrix products, arithmetic and copies ran while one was open for 22% of the time, Pallas kernels for 9%

profile of v1, /device:TPU:0, one launch (start us, length us, event | category | flops | bytes accessed | tf_op | source)
XLA Modules:
  0.0 2885.0 jit_solution(7266342208531259977)
XLA Ops:
  24.9 33.9 %all-gather.96.cloned.1.call-done = f32[1,256,2048]{2,1,0:T(8,128)} async-done(((f32[1,64,2048]{2,1,0:T(8,128)}), f32[1,256,2048]{2,1,0:T(8,128)}) %all-gather.96.cloned.1.call-update) | async-done | bytes 2097168 | tf_op jit(solution)/shard_map/all_gather | solution.py:690
  60.6 45.0 %all-gather.88.cloned.1.call-done = f32[1,256,2048]{2,1,0:T(8,128)} async-done(((f32[1,64,2048]{2,1,0:T(8,128)}), f32[1,256,2048]{2,1,0:T(8,128)}) %all-gather.88.cloned.1.call-update) | async-done | bytes 2097168 | tf_op jit(solution)/shard_map/all_gather | solution.py:690
  241.3 95.3 %all-gather.94.cloned.1.call-done.wide_ref = f32[8192,512]{1,0:T(8,128)} async-done(((f32[2048,512]{1,0:T(8,128)}), f32[8192,512]{1,0:T(8,128)}) %all-gather.94.cloned.1.call-update) | async-done | bytes 16777232 | tf_op jit(solution)/shard_map/all_gather | solution.py:660
  409.0 22.0 all-gather.92.cloned.1.call-done
  483.4 39.1 %reduce-scatter.19.cloned.1.call-done = f32[64,2048]{1,0:T(8,128)} async-done(((f32[256,2048]{1,0:T(8,128)}), f32[64,2048]{1,0:T(8,128)}) %reduce-scatter.19.cloned.1.call-update) | async-done | bytes 524304 | tf_op jit(solution)/shard_map/reduce_scatter | solution.py:711
  543.1 46.2 %all-gather.62.cloned.1.call-done.rows_ref = f32[256,2048]{1,0:T(8,128)} async-done(((f32[64,2048]{1,0:T(8,128)}), f32[256,2048]{1,0:T(8,128)}) %all-gather.62.cloned.1.call-update) | async-done | bytes 2097168 | tf_op jit(solution)/shard_map/all_gather | solution.py:690
  591.1 44.3 %all-gather.60.cloned.1.call-done.rows_ref = f32[256,2048]{1,0:T(8,128)} async-done(((f32[64,2048]{1,0:T(8,128)}), f32[256,2048]{1,0:T(8,128)}) %all-gather.60.cloned.1.call-update) | async-done | bytes 2097168 | tf_op jit(solution)/shard_map/all_gather | solution.py:690
  730.3 45.5 %all-gather.108.cloned.1.call-done = f32[1024,512]{1,0:T(8,128)} async-done(((f32[256,512]{1,0:T(8,128)}), f32[1024,512]{1,0:T(8,128)}) %all-gather.108.cloned.1.call-update) | async-done | bytes 2097168 | tf_op jit(solution)/shard_map/all_gather | solution.py:706
  800.2 21.6 all-gather.102.cloned.1.call-done
  874.2 39.0 %reduce-scatter.21.cloned.1.call-done = f32[64,2048]{1,0:T(8,128)} async-done(((f32[256,2048]{1,0:T(8,128)}), f32[64,2048]{1,0:T(8,128)}) %reduce-scatter.21.cloned.1.call-update) | async-done | bytes 524304 | tf_op jit(solution)/shard_map/reduce_scatter | solution.py:711
  933.9 47.0 %all-gather.64.cloned.1.call-done.rows_ref = f32[256,2048]{1,0:T(8,128)} async-done(((f32[64,2048]{1,0:T(8,128)}), f32[256,2048]{1,0:T(8,128)}) %all-gather.64.cloned.1.call-update) | async-done | bytes 2097168 | tf_op jit(solution)/shard_map/all_gather | solution.py:690
  982.7 44.3 %all-gather.66.cloned.1.call-done.rows_ref = f32[256,2048]{1,0:T(8,128)} async-done(((f32[64,2048]{1,0:T(8,128)}), f32[256,2048]{1,0:T(8,128)}) %all-gather.66.cloned.1.call-update) | async-done | bytes 2097168 | tf_op jit(solution)/shard_map/all_gather | solution.py:690
  1129.3 39.6 %all-gather.116.cloned.1.call-done = f32[1024,512]{1,0:T(8,128)} async-done(((f32[256,512]{1,0:T(8,128)}), f32[1024,512]{1,0:T(8,128)}) %all-gather.116.cloned.1.call-update) | async-done | bytes 2097168 | tf_op jit(solution)/shard_map/all_gather | solution.py:706
  1262.0 43.9 %reduce-scatter.31.cloned.1.call-done = f32[64,2048]{1,0:T(8,128)} async-done(((f32[256,2048]{1,0:T(8,128)}), f32[64,2048]{1,0:T(8,128)}) %reduce-scatter.31.cloned.1.call-update) | async-done | bytes 524304 | tf_op jit(solution)/shard_map/reduce_scatter | solution.py:756
  1308.4 42.9 %reduce-scatter.29.cloned.1.call-done = f32[64,2048]{1,0:T(8,128)} async-done(((f32[256,2048]{1,0:T(8,128)}), f32[64,2048]{1,0:T(8,128)}) %reduce-scatter.29.cloned.1.call-update) | async-done | bytes 524304 | tf_op jit(solution)/shard_map/reduce_scatter | solution.py:711
  1351.3 45.6 %reduce-scatter.27.cloned.1.call-done = f32[64,2048]{1,0:T(8,128)} async-done(((f32[256,2048]{1,0:T(8,128)}), f32[64,2048]{1,0:T(8,128)}) %reduce-scatter.27.cloned.1.call-update) | async-done | bytes 524304 | tf_op jit(solution)/shard_map/reduce_scatter | solution.py:711
  1401.7 44.5 %all-gather.70.cloned.1.call-done.top_ref = f32[256,2048]{1,0:T(8,128)} async-done(((f32[64,2048]{1,0:T(8,128)}), f32[256,2048]{1,0:T(8,128)}) %all-gather.70.cloned.1.call-update) | async-done | bytes 2097168 | tf_op jit(solution)/shard_map/all_gather | solution.py:765
  1457.6 34.7 %all-gather.68.cloned.1.call-done.top_ref = f32[256,2048]{1,0:T(8,128)} async-done(((f32[64,2048]{1,0:T(8,128)}), f32[256,2048]{1,0:T(8,128)}) %all-gather.68.cloned.1.call-update) | async-done | bytes 2097168 | tf_op jit(solution)/shard_map/all_gather | solution.py:765
  1614.4 22.1 reduce-scatter.35.cloned.1.call-done
  1638.5 44.2 %reduce-scatter.39.cloned.1.call-done = f32[64,2048]{1,0:T(8,128)} async-done(((f32[256,2048]{1,0:T(8,128)}), f32[64,2048]{1,0:T(8,128)}) %reduce-scatter.39.cloned.1.call-update) | async-done | bytes 524304 | tf_op jit(solution)/shard_map/reduce_scatter | solution.py:801
  1723.0 23.3 all-gather.72.cloned.1.call-done.handed_ref
  1767.3 25.1 all-gather.76.cloned.1.call-done.handed_ref
  1813.4 24.4 reduce-scatter.37.cloned.1.call-done
  1837.8 46.2 %reduce-scatter.41.cloned.1.call-done = f32[64,2048]{1,0:T(8,128)} async-done(((f32[256,2048]{1,0:T(8,128)}), f32[64,2048]{1,0:T(8,128)}) %reduce-scatter.41.cloned.1.call-update) | async-done | bytes 524304 | tf_op jit(solution)/shard_map/reduce_scatter | solution.py:756
  1890.8 44.1 %all-gather.78.cloned.1.call-done.top_ref = f32[256,2048]{1,0:T(8,128)} async-done(((f32[64,2048]{1,0:T(8,128)}), f32[256,2048]{1,0:T(8,128)}) %all-gather.78.cloned.1.call-update) | async-done | bytes 2097168 | tf_op jit(solution)/shard_map/all_gather | solution.py:765
  1945.8 35.4 %all-gather.74.cloned.1.call-done.top_ref = f32[256,2048]{1,0:T(8,128)} async-done(((f32[64,2048]{1,0:T(8,128)}), f32[256,2048]{1,0:T(8,128)}) %all-gather.74.cloned.1.call-update) | async-done | bytes 2097168 | tf_op jit(solution)/shard_map/all_gather | solution.py:765
  2103.1 22.2 reduce-scatter.43.cloned.1.call-done
  2127.2 44.2 %reduce-scatter.47.cloned.1.call-done = f32[64,2048]{1,0:T(8,128)} async-done(((f32[256,2048]{1,0:T(8,128)}), f32[64,2048]{1,0:T(8,128)}) %reduce-scatter.47.cloned.1.call-update) | async-done | bytes 524304 | tf_op jit(solution)/shard_map/reduce_scatter | solution.py:801
  2209.0 26.8 all-gather.80.cloned.1.call-done.handed_ref
  2258.3 23.7 all-gather.84.cloned.1.call-done.handed_ref
  2563.0 86.9 %collective-permute-done.18 = f32[8,1024]{1,0:T(8,128)} collective-permute-done((f32[8,1024]{1,0:T(8,128)}, f32[8,1024]{1,0:T(8,128)}, u32[]{:S(2)}, u32[]{:S(2)}) %collective-permute-start.18) | collective-permute-done | bytes 32800 | tf_op jit(solution)/shard_map/ppermute | solution.py:592
  2777.9 83.2 %all-reduce.2.cloned.1.call-done = f32[20752]{0:T(1024)} async-done(((f32[20752]{0:T(1024)}), f32[20752]{0:T(1024)}) %all-reduce.2.cloned.1.call-update) | async-done | bytes 83024 | tf_op jit(solution)/shard_map/psum | solution.py:839
  (1450 shorter events, 1539.4 us)
Async XLA Ops:
  10.2 177.2 %all-gather.58.cloned.1.call-start = ((), (), s32[]{:S(2)}) async-start(), calls=%async_computation.18 | async-start | bytes 5242880 | tf_op jit(solution)/shard_map/all_gather | solution.py:659
  12.3 195.2 %all-gather.90.cloned.1.call-start = ((), (), s32[]{:S(2)}) async-start(), calls=%async_computation.53 | async-start | bytes 1966080 | tf_op jit(solution)/shard_map/all_gather | solution.py:701
  169.2 167.4 %all-gather.94.cloned.1.call-start = ((), (), s32[]{:S(2)}) async-start(), calls=%async_computation.55 | async-start | bytes 20971520 | tf_op jit(solution)/shard_map/all_gather | solution.py:660
  187.4 197.4 %all-gather.104.cloned.1.call-start = ((), (), s32[]{:S(2)}) async-start(), calls=%async_computation.60 | async-start | bytes 2621440 | tf_op jit(solution)/shard_map/all_gather | solution.py:706
  240.3 190.7 %all-gather.92.cloned.1.call-start = ((), (), s32[]{:S(2)}) async-start(), calls=%async_computation.54 | async-start | bytes 2621440 | tf_op jit(solution)/shard_map/all_gather | solution.py:706
  241.1 235.5 %reduce-scatter.23.cloned.1.call-start = ((), (), s32[]{:S(2)}) async-start(), calls=%async_computation.22 | async-start | bytes 2621440 | tf_op jit(solution)/shard_map/reduce_scatter | solution.py:711
  408.7 113.8 %reduce-scatter.19.cloned.1.call-start = ((), (), s32[]{:S(2)}) async-start(), calls=%async_computation.19 | async-start | bytes 2621440 | tf_op jit(solution)/shard_map/reduce_scatter | solution.py:711
  455.0 134.3 %all-gather.62.cloned.1.call-start = ((), (), s32[]{:S(2)}) async-start(), calls=%async_computation.23 | async-start | bytes 2621440 | tf_op jit(solution)/shard_map/all_gather | solution.py:690
  543.1 155.9 %all-gather.98.cloned.1.call-start = ((), (), s32[]{:S(2)}) async-start(), calls=%async_computation.57 | async-start | bytes 1966080 | tf_op jit(solution)/shard_map/all_gather | solution.py:701
  730.2 137.0 %reduce-scatter.25.cloned.1.call-start = ((), (), s32[]{:S(2)}) async-start(), calls=%async_computation.24 | async-start | bytes 2621440 | tf_op jit(solution)/shard_map/reduce_scatter | solution.py:711
  845.8 135.1 %all-gather.64.cloned.1.call-start = ((), (), s32[]{:S(2)}) async-start(), calls=%async_computation.25 | async-start | bytes 2621440 | tf_op jit(solution)/shard_map/all_gather | solution.py:690
  933.8 159.1 %all-gather.110.cloned.1.call-start = ((), (), s32[]{:S(2)}) async-start(), calls=%async_computation.63 | async-start | bytes 1966080 | tf_op jit(solution)/shard_map/all_gather | solution.py:701
  1123.4 138.7 %reduce-scatter.33.cloned.1.call-start = ((), (), s32[]{:S(2)}) async-start(), calls=%async_computation.31 | async-start | bytes 2621440 | tf_op jit(solution)/shard_map/reduce_scatter | solution.py:756
  1249.9 147.0 %reduce-scatter.27.cloned.1.call-start = ((), (), s32[]{:S(2)}) async-start(), calls=%async_computation.26 | async-start | bytes 2621440 | tf_op jit(solution)/shard_map/reduce_scatter | solution.py:711
  1259.5 186.7 %all-gather.70.cloned.1.call-start = ((), (), s32[]{:S(2)}) async-start(), calls=%async_computation.32 | async-start | bytes 2621440 | tf_op jit(solution)/shard_map/all_gather | solution.py:765
  1503.7 132.8 %reduce-scatter.35.cloned.1.call-start = ((), (), s32[]{:S(2)}) async-start(), calls=%async_computation.33 | async-start | bytes 2621440 | tf_op jit(solution)/shard_map/reduce_scatter | solution.py:801
  1614.1 132.2 %all-gather.72.cloned.1.call-start = ((), (), s32[]{:S(2)}) async-start(), calls=%async_computation.34 | async-start | bytes 2621440 | tf_op jit(solution)/shard_map/all_gather | solution.py:744
  1718.6 119.2 %reduce-scatter.37.cloned.1.call-start = ((), (), s32[]{:S(2)}) async-start(), calls=%async_computation.35 | async-start | bytes 2621440 | tf_op jit(solution)/shard_map/reduce_scatter | solution.py:756
  1767.2 116.7 %reduce-scatter.41.cloned.1.call-start = ((), (), s32[]{:S(2)}) async-start(), calls=%async_computation.39 | async-start | bytes 2621440 | tf_op jit(solution)/shard_map/reduce_scatter | solution.py:756
  1813.3 121.7 %all-gather.78.cloned.1.call-start = ((), (), s32[]{:S(2)}) async-start(), calls=%async_computation.40 | async-start | bytes 2621440 | tf_op jit(solution)/shard_map/all_gather | solution.py:765
  1992.1 133.2 %reduce-scatter.43.cloned.1.call-start = ((), (), s32[]{:S(2)}) async-start(), calls=%async_computation.41 | async-start | bytes 2621440 | tf_op jit(solution)/shard_map/reduce_scatter | solution.py:801
  2102.8 133.0 %all-gather.80.cloned.1.call-start = ((), (), s32[]{:S(2)}) async-start(), calls=%async_computation.42 | async-start | bytes 2621440 | tf_op jit(solution)/shard_map/all_gather | solution.py:744
  2209.0 147.5 %reduce-scatter.45.cloned.1.call-start = ((), (), s32[]{:S(2)}) async-start(), calls=%async_computation.43 | async-start | bytes 2621440 | tf_op jit(solution)/shard_map/reduce_scatter | solution.py:756
  2258.2 115.1 %reduce-scatter.49.cloned.1.call-start = ((), (), s32[]{:S(2)}) async-start(), calls=%async_computation.47 | async-start | bytes 2621440 | tf_op jit(solution)/shard_map/reduce_scatter | solution.py:756
  2304.5 126.8 %all-gather.86.cloned.1.call-start = ((), (), s32[]{:S(2)}) async-start(), calls=%async_computation.48 | async-start | bytes 2621440 | tf_op jit(solution)/shard_map/all_gather | solution.py:765
  2451.0 256.2 %collective-permute-start.29 = (f32[1408,512]{1,0:T(8,128)}, f32[1408,512]{1,0:T(8,128)}, u32[]{:S(2)}, u32[]{:S(2)}) collective-permute-start(f32[1408,512]{1,0:T(8,128)} %dynamic-slice_bitcast_fusion.4), channel_id=1, source_target_pairs={{0,8},{4,12},{8,0},{12,4},{1,9},{5,13},{9,1},{13,5},{2,10},{6,14},... | collective-permute-start | bytes 8650760 | tf_op jit(solution)/shard_map/ppermute | solution.py:617
  2477.4 280.0 %reduce-scatter.53.cloned.1.call-start = ((), (), s32[]{:S(2)}) async-start(), calls=%async_computation.50 | async-start | bytes 2621440 | tf_op jit(solution)/shard_map/reduce_scatter | solution.py:801
  2481.3 231.1 %collective-permute-start.25 = (f32[512,1408]{1,0:T(8,128)}, f32[512,1408]{1,0:T(8,128)}, u32[]{:S(2)}, u32[]{:S(2)}) collective-permute-start(f32[512,1408]{1,0:T(8,128)} %dynamic-slice_bitcast_fusion.6), channel_id=1, source_target_pairs={{0,8},{4,12},{8,0},{12,4},{1,9},{5,13},{9,1},{13,5},{2,10},{6,14},... | collective-permute-start | bytes 8650760 | tf_op jit(solution)/shard_map/ppermute | solution.py:617
  2491.3 228.8 %collective-permute-start.27 = (f32[512,1408]{1,0:T(8,128)}, f32[512,1408]{1,0:T(8,128)}, u32[]{:S(2)}, u32[]{:S(2)}) collective-permute-start(f32[512,1408]{1,0:T(8,128)} %dynamic-slice_bitcast_fusion.5), channel_id=1, source_target_pairs={{0,8},{4,12},{8,0},{12,4},{1,9},{5,13},{9,1},{13,5},{2,10},{6,14},... | collective-permute-start | bytes 8650760 | tf_op jit(solution)/shard_map/ppermute | solution.py:617
  2514.4 135.6 %collective-permute-start.18 = (f32[8,1024]{1,0:T(8,128)}, f32[8,1024]{1,0:T(8,128)}, u32[]{:S(2)}, u32[]{:S(2)}) collective-permute-start(f32[8,1024]{1,0:T(8,128)} %pad_maximum_fusion.15), channel_id=1, source_target_pairs={{0,12},{4,0},{8,4},{12,8},{1,13},{5,1},{9,5},{13,9},{2,14},{6,2},{... | collective-permute-start | bytes 98312 | tf_op jit(solution)/shard_map/ppermute | solution.py:592
  2719.9 141.2 %all-reduce.2.cloned.1.call-start = ((), (), s32[]{:S(2)}) async-start(), calls=%async_computation.51 | async-start | bytes 172032 | tf_op jit(solution)/shard_map/psum | solution.py:839
  2740.2 127.5 %collective-permute-start.21 = (f32[512,1664]{1,0:T(8,128)}, f32[512,1664]{1,0:T(8,128)}, u32[]{:S(2)}, u32[]{:S(2)}) collective-permute-start(f32[512,1664]{1,0:T(8,128)} %dynamic-slice_bitcast_fusion.3), channel_id=1, source_target_pairs={{0,8},{4,12},{8,0},{12,4},{1,9},{5,13},{9,1},{13,5},{2,10},{6,14},... | collective-permute-start | bytes 10223624 | tf_op jit(solution)/shard_map/ppermute | solution.py:617
  (513 other events, 10824.0 us)
Sparse Core Ops, SparseCore 0:
  10.2 48.6 all-gather.95
  61.0 44.6 all-gather.87
  107.8 79.4 all-gather.57
  230.6 105.8 all-gather.93
  338.7 45.9 all-gather.103
  386.3 44.6 all-gather.91
  542.6 46.6 all-gather.61
  590.7 44.6 all-gather.59
  729.8 45.9 all-gather.107
  777.2 44.6 all-gather.101
  933.3 47.5 all-gather.63
  982.3 44.6 all-gather.65
  1122.9 45.9 all-gather.115
  1170.3 44.6 all-gather.111
  1262.7 43.1 reduce-scatter.30
  1353.7 43.1 reduce-scatter.26
  1401.2 44.9 all-gather.69
  1447.6 44.6 all-gather.67
  1591.4 45.0 reduce-scatter.34
  1639.5 43.1 reduce-scatter.38
  1701.7 44.5 all-gather.71
  1747.7 44.6 all-gather.75
  1890.0 44.9 all-gather.77
  1936.5 44.6 all-gather.73
  2080.2 45.0 reduce-scatter.42
  2191.2 44.5 all-gather.79
  2237.3 44.6 all-gather.83
  2330.1 43.1 reduce-scatter.48
  2378.8 44.9 all-gather.85
  2425.4 44.6 all-gather.81
  2728.7 43.1 reduce-scatter.50
  2776.0 85.0 all-reduce.1
  (23 shorter events, 687.8 us)

commit v2 on v1

v2 whole, which is shorter than its diff:
```python
from functools import partial

import jax
import jax.numpy as jnp
from jax import lax
from jax.experimental import pallas as pl
from jax.experimental.pallas import tpu as pltpu
from jax.sharding import PartitionSpec as P

EPSILON = 1e-06
F32 = jnp.float32
LOW = jnp.bfloat16
VMEM_BYTES = 48 * 1024 * 1024
GROUP = 2
NN = ((1,), (0,))
NT = ((1,), (1,))
TN = ((0,), (0,))


def low_dot(a, b, contract=NN):
    return lax.dot_general(a, b, (contract, ((), ())), preferred_element_type=F32)


def halves(x):
    high = x.astype(LOW)
    return high, (x - high.astype(F32)).astype(LOW)


def thirds(x):
    high = x.astype(LOW)
    rest = x - high.astype(F32)
    middle = rest.astype(LOW)
    return high, middle, (rest - middle.astype(F32)).astype(LOW)


def pair_dot(a, b, contract=NN):
    left, right = contract[0][0], contract[1][0]
    return low_dot(
        jnp.concatenate([a[0], a[0], a[1]], left),
        jnp.concatenate([b[0], b[1], b[0]], right),
        contract,
    )


def fine_dot(a, b, contract=NN):
    return pair_dot(halves(a), halves(b), contract)


def sigmoid(x):
    return 1.0 / (1.0 + jnp.exp(-x))


def places(size):
    return (
        lax.broadcasted_iota(jnp.int32, (size, size), 0),
        lax.broadcasted_iota(jnp.int32, (size, size), 1),
    )


def unit_lower_inverses(strict_parts, rows, cols):
    size = strict_parts[0].shape[0]
    near = (rows >> 3) == (cols >> 3)
    eye = jnp.where(rows == cols, 1.0, 0.0)
    inner = [jnp.where(near, part, 0.0) for part in strict_parts]
    split = [halves(part) for part in inner]
    second = [halves(pair_dot(part, part)) for part in split]
    fourth = [halves(pair_dot(part, part)) for part in second]
    inverse = [eye - part for part in inner]
    inverse = [part + pair_dot(halves(part), power) for part, power in zip(inverse, second)]
    inverse = [part + pair_dot(halves(part), power) for part, power in zip(inverse, fourth)]
    level = 3
    while (1 << level) < size:
        joined = ((rows >> (level + 1)) == (cols >> (level + 1))) & ((rows >> level) != (cols >> level))
        split = [halves(part) for part in inverse]
        middle = [
            halves(pair_dot(halves(jnp.where(joined, strict, 0.0)), part))
            for strict, part in zip(strict_parts, split)
        ]
        inverse = [
            part - pair_dot(pair, between) for part, pair, between in zip(inverse, split, middle)
        ]
        level += 1
    return inverse


def taps_back(padded, steps):
    rolled = padded if steps == 0 else pltpu.roll(padded, steps, 0)
    return rolled[8:]


def conv_sum(padded, taps):
    count = taps.shape[0]
    total = taps[0:1] * taps_back(padded, count - 1)
    for member in range(1, count):
        total = total + taps[member : member + 1] * taps_back(padded, count - 1 - member)
    return total


def conv_transposed(grad, taps):
    count = taps.shape[0]
    padded = jnp.concatenate([jnp.zeros((8, grad.shape[1]), F32), grad], 0)
    size = padded.shape[0]
    total = taps[count - 1 : count] * padded
    for member in range(count - 1):
        total = total + taps[member : member + 1] * pltpu.roll(padded, size - (count - 1 - member), 0)
    return total


def conv_taps_grad(padded, grad, count):
    return jnp.concatenate(
        [
            jnp.sum(grad * taps_back(padded, count - 1 - member), 0, keepdims=True)
            for member in range(count)
        ],
        0,
    )


def softplus(x):
    return jnp.maximum(x, 0.0) + jnp.log(1.0 + jnp.exp(-jnp.abs(x)))


class Gates:
    def __init__(self, side, resets, head, heads, rate, bias, rows, cols):
        size = side.shape[0]
        self.rate = rate
        self.shifted = side[:, head : head + 1] + bias
        self.log_decay = -rate * softplus(self.shifted)
        self.beta = sigmoid(side[:, heads + head : heads + head + 1])
        lanes = lax.broadcasted_iota(jnp.int32, (size, 128), 1)
        pair = jnp.where(lanes == 0, self.log_decay, jnp.where(lanes == 1, resets, 0.0))
        lower = jnp.where(rows >= cols, 1.0, 0.0).astype(LOW)
        split = thirds(pair)
        as_columns = low_dot(
            jnp.concatenate([lower] * 3, 1), jnp.concatenate(split, 0)
        )
        as_rows = low_dot(
            jnp.concatenate(split, 0), jnp.concatenate([lower] * 3, 1), ((0,), (1,))
        )
        total, count = as_columns[:, 0:1], as_columns[:, 1:2]
        linked = (jnp.abs(count - as_rows[1:2, :]) < 0.5) & (rows >= cols)
        self.decays = jnp.where(linked, jnp.exp(jnp.minimum(total - as_rows[0:1, :], 0.0)), 0.0)
        last_total, last_count = total[size - 1 : size], count[size - 1 : size]
        self.head_decay = jnp.where(count < 0.5, jnp.exp(total), 0.0)
        self.tail_decay = jnp.where(
            jnp.abs(count - last_count) < 0.5, jnp.exp(jnp.minimum(last_total - total, 0.0)), 0.0
        )


def silu_unit(summed, scale):
    gate = sigmoid(summed)
    act = summed * gate
    inverse = lax.rsqrt(jnp.sum(act * act, 1, keepdims=True) + EPSILON)
    return act, gate, inverse, act * (inverse * scale)


def silu_unit_back(grad, summed, gate, act, inverse, scale):
    unit = act * inverse
    grad = grad * scale
    act_grad = inverse * (grad - unit * jnp.sum(grad * unit, 1, keepdims=True))
    return act_grad * gate * (1.0 + summed * (1.0 - gate))


def head_columns(sizes, head):
    heads, key_size, value_size = sizes
    base = 2 * heads * key_size
    return (
        slice(head * key_size, (head + 1) * key_size),
        slice((heads + head) * key_size, (heads + head + 1) * key_size),
        slice(base + head * value_size, base + (head + 1) * value_size),
    )


def side_columns(sizes):
    heads, key_size, value_size = sizes
    start = 2 * heads * (key_size + value_size)
    return slice(start, start + 128)


def local_kernel(
    sizes, projected_ref, resets_ref, border_ref, taps_ref, rate_ref, bias_ref,
    carried_ref, local_ref, map_ref, inverse_ref,
):
    heads, key_size, value_size = sizes
    size = projected_ref.shape[0]
    rows, cols = places(size)
    side, resets = projected_ref[:, side_columns(sizes)], resets_ref[:, 0:1]
    gates, queries, keys, values, mixing = [], [], [], [], []
    for head in range(heads):
        gate = Gates(side, resets, head, heads, rate_ref[head], bias_ref[head], rows, cols)
        summed = [
            conv_sum(jnp.concatenate([border_ref[:, at], projected_ref[:, at]], 0), taps_ref[:, at])
            for at in head_columns(sizes, head)
        ]
        gates.append(gate)
        queries.append(silu_unit(summed[0], key_size**-0.5)[3])
        keys.append(silu_unit(summed[1], 1.0)[3])
        values.append(summed[2] * sigmoid(summed[2]))
        split = halves(keys[head])
        gram = pair_dot(split, split, NT)
        mixing.append(gate.beta * jnp.where(rows > cols, gate.decays * gram, 0.0))
    inverses = [halves(part) for part in unit_lower_inverses(mixing, rows, cols)]
    krows, kcols = places(key_size)
    for head in range(heads):
        gate, query, key, value, inverse = (
            gates[head], queries[head], keys[head], values[head], inverses[head],
        )
        inverse_ref[head, 0] = inverse[0]
        inverse_ref[head, 1] = inverse[1]
        both = halves(
            pair_dot(
                inverse,
                halves(jnp.concatenate([(gate.beta * gate.head_decay) * key, gate.beta * value], 1)),
            )
        )
        scores = fine_dot(query, key, NT) * gate.decays
        read = pair_dot(halves(scores), both)
        carried_ref[:, head * key_size : (head + 1) * key_size] = (
            gate.head_decay * query - read[:, :key_size]
        )
        local_ref[:, head * value_size : (head + 1) * value_size] = read[:, key_size:]
        written = pair_dot(halves(key * gate.tail_decay), both, TN)
        kept = jnp.where(krows == kcols, gate.head_decay[size - 1 : size], 0.0)
        map_ref[head, :, :key_size] = kept - written[:, :key_size]
        map_ref[head, :, key_size:] = written[:, key_size:]


def pick(refs, index, head):
    value = refs[0][head]
    for at in range(1, len(refs)):
        value = jnp.where(index == at, refs[at][head], value)
    return value


def gate_kernel(sizes, count, order_ref, *refs):
    heads, key_size, value_size = sizes
    maps = refs[:count]
    (
        state_ref, carried_ref, local_ref, outgate_ref, gain_ref, gated_ref, output_ref, entry_ref, end_ref,
    ) = refs[count:]
    states = [state_ref[head] for head in range(heads)]
    entries = list(states)
    for at in range(count):
        index = order_ref[at]
        for head in range(heads):
            if at:
                entries[head] = jnp.where(index == 0, states[head], entries[head])
            step = pick(maps, index, head)
            states[head] = fine_dot(step[:, :key_size], states[head]) + step[:, key_size:]
    for head in range(heads):
        at = slice(head * value_size, (head + 1) * value_size)
        entry_ref[head] = entries[head]
        end_ref[head] = states[head]
        output = local_ref[:, at] + fine_dot(
            carried_ref[:, head * key_size : (head + 1) * key_size], entries[head]
        )
        output_ref[:, at] = output
        normed = output * lax.rsqrt(jnp.mean(output * output, 1, keepdims=True) + EPSILON)
        gate = outgate_ref[:, at]
        gated_ref[:, at] = (normed * gain_ref[...] * (gate * sigmoid(gate))).astype(LOW).astype(F32)


def gate_back_kernel(sizes, count, order_ref, *refs):
    heads, key_size, value_size = sizes
    pieces = refs[:count]
    (
        output_ref, outgate_ref, gain_ref, carried_ref,
        output_grad_ref, outgate_grad_ref, gain_grad_ref, entry_ref, grads,
    ) = refs[count:]
    part = pieces[0].shape[0]
    for at, piece in enumerate(pieces):
        grads[pl.ds(pl.multiple_of(order_ref[at] * part, part), part), :] = piece[...]
    gain = gain_ref[...]
    total = jnp.zeros_like(gain)
    for head in range(heads):
        at = slice(head * value_size, (head + 1) * value_size)
        grad, output, gate = grads[:, at], output_ref[:, at], outgate_ref[:, at]
        inverse = lax.rsqrt(jnp.mean(output * output, 1, keepdims=True) + EPSILON)
        unit = output * inverse
        opened = sigmoid(gate)
        swished = gate * opened
        outgate_grad_ref[:, at] = (
            grad * unit * gain * (opened * (1.0 + gate * (1.0 - opened)))
        ).astype(LOW)
        total = total + jnp.sum(grad * unit * swished, 0, keepdims=True)
        unit_grad = grad * gain * swished
        output_grad = inverse * (unit_grad - unit * jnp.mean(unit_grad * unit, 1, keepdims=True))
        output_grad_ref[:, at] = output_grad
        entry_ref[head] = fine_dot(
            carried_ref[:, head * key_size : (head + 1) * key_size], output_grad, TN
        )
    gain_grad_ref[...] = total


def mix_back_kernel(count, target_ref, grad_ref, mixed_ref, top_ref, gain_ref, weight_ref, sum_ref, *refs):
    values, grad = mixed_ref[...], grad_ref[...]
    inverse = lax.rsqrt(jnp.mean(values * values, 1, keepdims=True) + EPSILON)
    unit = values * inverse
    scaled = grad * gain_ref[...]
    mixed_grad = top_ref[...] + inverse * (scaled - unit * jnp.mean(unit * scaled, 1, keepdims=True))
    refs[0][...] = mixed_grad
    sum_ref[...] = jnp.sum(unit * grad, 0, keepdims=True)
    low = mixed_grad.astype(LOW)
    part = weight_ref.shape[0] // count
    for at in range(count):
        place = pl.multiple_of(target_ref[at] * part, part)
        refs[1 + at][...] = low_dot(low, weight_ref[pl.ds(place, part), :], NT)


def local_back_kernel(sizes, count, order_ref, *refs):
    heads, key_size, value_size = sizes
    maps, entries = refs[:count], refs[count : 2 * count]
    (
        state_grad_ref, projected_ref, resets_ref, border_ref, taps_ref, rate_ref, bias_ref,
        inverse_ref, entry_state_ref, output_grad_ref,
        conv_grad_ref, border_grad_ref, taps_grad_ref, side_grad_ref, sums_ref, start_grad_ref,
    ) = refs[2 * count :]
    size = projected_ref.shape[0]
    scale = key_size**-0.5
    state_grads = [state_grad_ref[head] for head in range(heads)]
    end_grads = list(state_grads)
    for at in reversed(range(count)):
        index = order_ref[at]
        for head in range(heads):
            if at < count - 1:
                end_grads[head] = jnp.where(index == 0, state_grads[head], end_grads[head])
            step = pick(maps, index, head)[:, :key_size]
            state_grads[head] = fine_dot(step, state_grads[head], TN) + pick(entries, index, head)
    rows, cols = places(size)
    strict = rows > cols
    lower = jnp.where(rows >= cols, 1.0, 0.0).astype(LOW)
    lanes = lax.broadcasted_iota(jnp.int32, (size, 128), 1)
    at_row = lax.broadcasted_iota(jnp.int32, (size, 1), 0)
    sum_lanes = lax.broadcasted_iota(jnp.int32, (8, 128), 1)
    sum_rows = lax.broadcasted_iota(jnp.int32, (8, 128), 0)
    side, resets = projected_ref[:, side_columns(sizes)], resets_ref[:, 0:1]
    side_grad = jnp.zeros((size, 128), F32)
    sums = jnp.zeros((8, 128), F32)
    for head in range(heads):
        start_grad_ref[head] = state_grads[head]
        gate = Gates(side, resets, head, heads, rate_ref[head], bias_ref[head], rows, cols)
        columns = head_columns(sizes, head)
        padded = [jnp.concatenate([border_ref[:, at], projected_ref[:, at]], 0) for at in columns]
        summed = [conv_sum(part, taps_ref[:, at]) for part, at in zip(padded, columns)]
        act_q, gate_q, inverse_q, query = silu_unit(summed[0], scale)
        act_k, gate_k, inverse_k, key = silu_unit(summed[1], 1.0)
        gate_v = sigmoid(summed[2])
        value = summed[2] * gate_v
        beta, decays, head_decay, tail_decay = gate.beta, gate.decays, gate.head_decay, gate.tail_decay
        end_grad, state = end_grads[head], entry_state_ref[head]
        inverse = (inverse_ref[head, 0], inverse_ref[head, 1])
        output_grad = halves(output_grad_ref[:, head * value_size : (head + 1) * value_size])
        query_s, key_s, state_s, end_s = halves(query), halves(key), halves(state), halves(end_grad)

        gram = pair_dot(key_s, key_s, NT)
        pure = pair_dot(query_s, key_s, NT)
        residue = value - head_decay * pair_dot(key_s, state_s)
        update = halves(pair_dot(inverse, halves(beta * residue)))
        update_grad = pair_dot(halves(pure * decays), output_grad, TN) + pair_dot(
            halves(key * tail_decay), end_s
        )
        target_grad = pair_dot(inverse, halves(update_grad), TN)
        target_s = halves(target_grad)
        weighted = jnp.where(strict, -pair_dot(target_s, update, NT), 0.0) * decays
        pure_grad = pair_dot(output_grad, update, NT) * decays
        reached = pair_dot(output_grad, state_s, NT)
        erased = pair_dot(target_s, state_s, NT)
        kept = pair_dot(update, end_s, NT)
        gram_grad = weighted * beta
        pure_s, gram_s = halves(pure_grad), halves(gram_grad)
        query_grad = head_decay * reached + pair_dot(pure_s, key_s)
        key_grad = (
            pair_dot(pure_s, query_s, TN)
            + tail_decay * kept
            - (beta * head_decay) * erased
            + pair_dot(gram_s, key_s)
            + pair_dot(gram_s, key_s, TN)
        )
        value_grad = beta * target_grad
        beta_grad = jnp.sum(target_grad * residue, 1, keepdims=True) + jnp.sum(
            weighted * gram, 1, keepdims=True
        )
        spread = pure_grad * pure + gram_grad * gram
        head_decay_grad = jnp.sum(query * reached, 1, keepdims=True) - beta * jnp.sum(
            key * erased, 1, keepdims=True
        )
        tail_part = tail_decay * jnp.sum(key * kept, 1, keepdims=True)
        spread_s = jnp.concatenate(thirds(spread), 0)
        column_sums = low_dot(spread_s, jnp.ones((3 * size, 128), LOW), TN)[:, 0:1]
        total_grad = (
            head_decay * head_decay_grad - tail_part + jnp.sum(spread, 1, keepdims=True) - column_sums
        )
        last_grad = jnp.sum(tail_part, 0, keepdims=True) + head_decay[size - 1 : size] * jnp.sum(
            jnp.sum(end_grad * state, 1, keepdims=True), 0, keepdims=True
        )
        total_grad = total_grad + jnp.where(at_row == size - 1, last_grad, 0.0)
        total_s = jnp.concatenate(thirds(jnp.where(lanes == 0, total_grad, 0.0)), 0)
        log_grad = low_dot(jnp.concatenate([lower] * 3, 0), total_s, TN)[:, 0:1]
        decay_grad = log_grad * (-gate.rate) * sigmoid(gate.shifted)
        beta_in_grad = beta_grad * beta * (1.0 - beta)
        side_grad = jnp.where(
            lanes == head, decay_grad, jnp.where(lanes == heads + head, beta_in_grad, side_grad)
        )
        log_sum = jnp.sum(log_grad * gate.log_decay, 0, keepdims=True)
        bias_sum = jnp.sum(decay_grad, 0, keepdims=True)
        sums = jnp.where(
            (sum_lanes == head) & (sum_rows == 0),
            log_sum,
            jnp.where((sum_lanes == head) & (sum_rows == 1), bias_sum, sums),
        )
        grads = (
            silu_unit_back(query_grad, summed[0], gate_q, act_q, inverse_q, scale),
            silu_unit_back(key_grad, summed[1], gate_k, act_k, inverse_k, 1.0),
            value_grad * gate_v * (1.0 + summed[2] * (1.0 - gate_v)),
        )
        for grad, part, at in zip(grads, padded, columns):
            spread_out = conv_transposed(grad, taps_ref[:, at])
            border_grad_ref[:, at] = spread_out[:8]
            conv_grad_ref[:, at] = spread_out[8:]
            taps_grad_ref[:, at] = conv_taps_grad(part, grad, taps_ref.shape[0])
    side_grad_ref[...] = side_grad.astype(LOW)
    sums_ref[...] = sums


def smem():
    return pl.BlockSpec(memory_space=pltpu.SMEM)


def anywhere():
    return pl.BlockSpec(memory_space=pl.ANY)


def call(kernel, out_shape, operands, name, micros, in_specs=None, scratch=(), vmem=VMEM_BYTES):
    whole = lambda array: pl.BlockSpec(array.shape, lambda i: (0,) * len(array.shape))
    specs = [whole(array) for array in operands] if in_specs is None else in_specs
    specs = [whole(array) if spec is None else spec for spec, array in zip(specs, operands)]
    return pl.pallas_call(
        kernel,
        grid=(1,),
        in_specs=specs,
        out_specs=[whole(array) for array in out_shape],
        out_shape=out_shape,
        scratch_shapes=list(scratch),
        compiler_params=pltpu.CompilerParams(vmem_limit_bytes=vmem),
        cost_estimate=pl.CostEstimate(
            flops=int(micros * 3e+08), bytes_accessed=int(micros * 900000), transcendentals=0
        ),
        name=name,
    )(*operands)


def shape(dims, dtype=F32):
    return jax.ShapeDtypeStruct(tuple(dims), dtype)


def columns_spec(rows, width, at):
    return pl.BlockSpec((rows, width), lambda i: (0, at))


def mixer_local(sizes, projected, resets, border, taps, rate, bias):
    heads, key_size, value_size = sizes
    rows = projected.shape[0]
    return call(
        partial(local_kernel, sizes),
        [
            shape((rows, heads * key_size)),
            shape((rows, heads * value_size)),
            shape((heads, key_size, key_size + value_size)),
            shape((heads, 2, rows, rows), LOW),
        ],
        [projected, resets, border, taps, rate, bias],
        "mixer_local",
        12,
        [None, None, None, None, smem(), smem()],
    )


def mixer_gate(sizes, order, maps, state, carried, local, projected, gain):
    heads, key_size, value_size = sizes
    rows = projected.shape[0]
    count = len(maps)
    value_cols = heads * value_size
    outgate = columns_spec(rows, value_cols, (2 * heads * key_size + value_cols) // value_cols)
    return call(
        partial(gate_kernel, sizes, count),
        [
            shape((rows, value_cols)),
            shape((rows, value_cols)),
            shape((heads, key_size, value_size)),
            shape((heads, key_size, value_size)),
        ],
        [order, *maps, state, carried, local, projected, gain],
        "mixer_gate",
        5,
        [smem()] + [None] * (count + 3) + [outgate, None],
    )


def mix_back(target, grad, mixed, top, gain, weight):
    rows, width = grad.shape
    count = target.shape[0]
    return call(
        partial(mix_back_kernel, count),
        [shape((1, width)), shape((rows, width))] + [shape((rows, weight.shape[0] // count))] * count,
        [target, grad, mixed, top, gain, weight],
        "mix_back",
        5,
        [smem()] + [None] * 5,
    )


def mixer_gate_back(sizes, order, pieces, output, projected, gain, carried):
    heads, key_size, value_size = sizes
    rows = projected.shape[0]
    count = len(pieces)
    value_cols = heads * value_size
    outgate = columns_spec(rows, value_cols, (2 * heads * key_size + value_cols) // value_cols)
    return call(
        partial(gate_back_kernel, sizes, count),
        [
            shape((rows, value_cols)),
            shape((rows, value_cols), LOW),
            shape((1, value_size)),
            shape((heads, key_size, value_size)),
        ],
        [order, *pieces, output, projected, gain, carried],
        "mixer_gate_back",
        4,
        [smem()] + [None] * (count + 1) + [outgate, None, None],
        [pltpu.VMEM((rows, value_cols), F32)],
    )


def mixer_local_back(
    sizes, order, maps, entries, state_grad, projected, resets, border, taps, rate, bias, inverse,
    entry_state, output_grad,
):
    heads, key_size, value_size = sizes
    rows = projected.shape[0]
    count = len(maps)
    conv_cols = taps.shape[1]
    return call(
        partial(local_back_kernel, sizes, count),
        [
            shape((rows, conv_cols)),
            shape((8, conv_cols)),
            shape(taps.shape),
            shape((rows, 128), LOW),
            shape((8, 128)),
            shape((heads, key_size, value_size)),
        ],
        [
            order, *maps, *entries, state_grad, projected, resets, border, taps, rate, bias, inverse,
            entry_state, output_grad,
        ],
        "mixer_local_back",
        12,
        [smem()] + [None] * (2 * count + 5) + [smem(), smem(), None, None, None],
    )


def recast_kernel(index_ref, source_ref, *refs):
    refs[-1][...] = source_ref[...].astype(refs[-1].dtype)


def widen(values):
    rows, cols = values.shape
    tile = min(rows, 256)
    spec = pl.BlockSpec((tile, cols), lambda i, index: (i, 0))
    return pl.pallas_call(
        recast_kernel,
        grid_spec=pltpu.PrefetchScalarGridSpec(
            num_scalar_prefetch=1, grid=(rows // tile,), in_specs=[spec], out_specs=spec
        ),
        out_shape=shape((rows, cols)),
        name="widen",
    )(jnp.zeros((1,), jnp.int32), values)


def narrow_into(whole, values, index, total, member, members, pieces):
    rows, cols = values.shape
    tile = rows // pieces
    source = pl.BlockSpec((tile, cols), lambda i, index: (i, 0))
    placed = pl.BlockSpec((tile, cols), lambda i, index: (i * members + member, index[0]))
    more = [] if whole is None else [whole]
    return pl.pallas_call(
        recast_kernel,
        grid_spec=pltpu.PrefetchScalarGridSpec(
            num_scalar_prefetch=1,
            grid=(pieces,),
            in_specs=[source] + [anywhere()] * len(more),
            out_specs=placed,
        ),
        out_shape=shape((rows * members, total), LOW),
        input_output_aliases={2: 0} if more else {},
        name="narrow_into",
    )(index, values, *more)


def enter_kernel(rows_ref, gain_ref, weight_ref, hidden_ref, projected_ref):
    values = rows_ref[...]
    inverse = lax.rsqrt(jnp.mean(values * values, 1, keepdims=True) + EPSILON)
    hidden = (values * inverse * gain_ref[...]).astype(LOW)
    hidden_ref[...] = hidden
    projected_ref[...] = low_dot(hidden, weight_ref[...])


def enter(rows, gain, weight):
    count, width = rows.shape
    return call(
        enter_kernel,
        [shape((count, width), LOW), shape((count, weight.shape[1]))],
        [rows, gain, weight],
        "enter",
        6,
    )


def join_kernel(
    rows_ref, gated_ref, weight_ref, gain_ref, gate_hbm, up_hbm, down_hbm,
    mixed_ref, hidden_ref, gate_ref, up_ref, inner_ref, sums_ref,
    gate_weight, up_weight, down_weight, arrived,
):
    copies = [
        pltpu.make_async_copy(source, target, arrived.at[at])
        for at, (source, target) in enumerate(
            ((gate_hbm, gate_weight), (up_hbm, up_weight), (down_hbm, down_weight))
        )
    ]
    for copy in copies:
        copy.start()
    depth = gated_ref.shape[2]
    mixed = rows_ref[...]
    for part in range(gated_ref.shape[0]):
        mixed = mixed + low_dot(
            gated_ref[part].astype(LOW), weight_ref[part * depth : (part + 1) * depth, :]
        )
    mixed_ref[...] = mixed
    inverse = lax.rsqrt(jnp.mean(mixed * mixed, 1, keepdims=True) + EPSILON)
    hidden = (mixed * inverse * gain_ref[...]).astype(LOW)
    hidden_ref[...] = hidden
    copies[0].wait()
    gate = low_dot(hidden, gate_weight[...])
    gate_ref[...] = gate
    copies[1].wait()
    up = low_dot(hidden, up_weight[...])
    up_ref[...] = up
    inner = (gate * sigmoid(gate) * up).astype(LOW)
    inner_ref[...] = inner
    copies[2].wait()
    sums_ref[...] = low_dot(inner, down_weight[...])


def join_heads(rows, gated, weight, gain, gate_weight, up_weight, down_weight):
    count, width = rows.shape
    hidden = gate_weight.shape[1]
    return call(
        join_kernel,
        [
            shape((count, width)),
            shape((count, width), LOW),
            shape((count, hidden)),
            shape((count, hidden)),
            shape((count, hidden), LOW),
            shape((count, width)),
        ],
        [rows, gated, weight, gain, gate_weight, up_weight, down_weight],
        "join_heads",
        12,
        [None] * 4 + [anywhere()] * 3,
        [
            pltpu.VMEM(gate_weight.shape, LOW),
            pltpu.VMEM(up_weight.shape, LOW),
            pltpu.VMEM(down_weight.shape, LOW),
            pltpu.SemaphoreType.DMA((3,)),
        ],
        56 * 1024 * 1024,
    )


def feed_back_kernel(
    last_ref, given_ref, handed_ref, gate_ref, up_ref, gate_hbm, up_hbm, down_hbm,
    top_ref, gate_grad_ref, up_grad_ref, sums_ref, gate_weight, up_weight, down_weight, arrived,
):
    copies = [
        pltpu.make_async_copy(source, target, arrived.at[at])
        for at, (source, target) in enumerate(
            ((down_hbm, down_weight), (gate_hbm, gate_weight), (up_hbm, up_weight))
        )
    ]
    for copy in copies:
        copy.start()
    top = jnp.where(last_ref[0] == 1, given_ref[...].astype(F32), handed_ref[...]).astype(LOW)
    top_ref[...] = top
    copies[0].wait()
    grad = low_dot(top, down_weight[...], NT)
    gate = gate_ref[...]
    opened = sigmoid(gate)
    gate_grad = (grad * up_ref[...] * (opened * (1.0 + gate * (1.0 - opened)))).astype(LOW)
    up_grad = (grad * gate * opened).astype(LOW)
    gate_grad_ref[...] = gate_grad
    up_grad_ref[...] = up_grad
    copies[1].wait()
    sums = low_dot(gate_grad, gate_weight[...], NT)
    copies[2].wait()
    sums_ref[...] = sums + low_dot(up_grad, up_weight[...], NT)


def feed_back(last, given, handed, gate_act, up_act, gate_weight, up_weight, down_weight):
    count, width = given.shape
    hidden = gate_weight.shape[1]
    return call(
        feed_back_kernel,
        [
            shape((count, width), LOW),
            shape((count, hidden), LOW),
            shape((count, hidden), LOW),
            shape((count, width)),
        ],
        [last, given, handed, gate_act, up_act, gate_weight, up_weight, down_weight],
        "feed_back",
        12,
        [smem()] + [None] * 4 + [anywhere()] * 3,
        [
            pltpu.VMEM(gate_weight.shape, LOW),
            pltpu.VMEM(up_weight.shape, LOW),
            pltpu.VMEM(down_weight.shape, LOW),
            pltpu.SemaphoreType.DMA((3,)),
        ],
    )


def leave_kernel(conv_ref, tail_ref, outgate_ref, side_ref, weight_ref, low_ref, sums_ref):
    rows, conv_cols = conv_ref.shape
    conv = conv_ref[...]
    conv = jnp.concatenate([conv[: rows - 8], conv[rows - 8 :] + tail_ref[...]], 0)
    low = jnp.concatenate([conv.astype(LOW), outgate_ref[...], side_ref[...]], 1)
    low_ref[...] = low
    sums_ref[...] = low_dot(low, weight_ref[...], NT)


def leave(conv, tail, outgate, side, weight):
    count, width = conv.shape[0], weight.shape[0]
    return call(
        leave_kernel,
        [shape((count, weight.shape[1]), LOW), shape((count, width))],
        [conv, tail, outgate, side, weight],
        "leave",
        7,
    )


def row_norm_back(values, gain, grad):
    inverse = lax.rsqrt(jnp.mean(values * values, -1, keepdims=True) + EPSILON)
    unit = values * inverse
    scaled = grad * gain
    back = inverse * (scaled - unit * jnp.mean(unit * scaled, -1, keepdims=True))
    return back, jnp.sum(unit * grad, 0)


def ring(value, axis, steps):
    count = lax.axis_size(axis)
    return lax.ppermute(value, axis, [(at, (at + steps) % count) for at in range(count)])


def all_seq(value):
    return [value] + [ring(value, "seq", step) for step in range(1, lax.axis_size("seq"))]


def handed_on(value, axis, steps):
    count = lax.axis_size(axis)
    first, last = max(0, -steps), min(count, count - steps)
    return lax.ppermute(value, axis, [(at, at + steps) for at in range(first, last)])


def gather_tp(values):
    return lax.all_gather(values, "tp", axis=0, tiled=True)


def scatter_tp(values):
    return lax.psum_scatter(values, "tp", scatter_dimension=0, tiled=True)


def crossed(value, bit):
    return lax.ppermute(value, "seq", [(at, at ^ bit) for at in range(lax.axis_size("seq"))])


def butterfly(value, axis):
    count = lax.axis_size(axis)
    step = 1
    while step < count:
        value = value + lax.ppermute(value, axis, [(at, at ^ step) for at in range(count)])
        step *= 2
    return value


def core_sums(left, right, axis):
    count = lax.axis_size("seq")
    chunk = (left, right)[axis].shape[1] // count
    index = lax.axis_index("seq")
    core, chip, chips = index % 2, index // 2, count // 2

    def product(chip, core):
        place = (chip * 2 + core) * chunk
        if axis:
            return low_dot(left, lax.dynamic_slice_in_dim(right, place, chunk, 1), TN)
        return low_dot(lax.dynamic_slice_in_dim(left, place, chunk, 1), right, TN)

    order = [(chip + step) % chips for step in range(1, chips)] + [chip]
    received = [crossed(product(at, 1 - core), 1) for at in order]
    return [product(at, core) + part for at, part in zip(order, received)]


def chip_sums(parts):
    total = parts[-1]
    for step, part in enumerate(parts[:-1], 1):
        total = total + ring(part, "seq", 2 * step)
    return total


def after(value, *others):
    return lax.optimization_barrier((value, *others))[0]


def local(
    inputs, cotangent, doc_start, norm_in, query_weight, key_weight, value_weight, outgate_weight,
    decay_weight, beta_weight, conv_query, conv_key, conv_value, decay_log, decay_bias, head_norm,
    out_weight, norm_feed, gate_weight, up_weight, down_weight,
):
    query_weight, key_weight, value_weight = query_weight[0], key_weight[0], value_weight[0]
    outgate_weight, decay_weight, beta_weight = outgate_weight[0], decay_weight[0], beta_weight[0]
    gate_weight, up_weight, down_weight, out_weight = (
        gate_weight[0], up_weight[0], down_weight[0], out_weight[0],
    )
    taps = jnp.concatenate([conv_query[0], conv_key[0], conv_value[0]], 1)
    rate, bias = jnp.exp(decay_log[0]), decay_bias[0]
    heads = bias.shape[0]
    key_size = query_weight.shape[1] // heads
    value_size = value_weight.shape[1] // heads
    sizes = (heads, key_size, value_size)
    key_cols, value_cols = heads * key_size, heads * value_size
    micros, own_rows, width = inputs.shape
    rows = cotangent.shape[1]
    seq_size, seq_index = lax.axis_size("seq"), lax.axis_index("seq")
    tp_index = lax.axis_index("tp")
    section = lax.axis_index("section")
    at_start, at_end = seq_index == 0, seq_index == seq_size - 1
    order = (seq_index - jnp.arange(seq_size, dtype=jnp.int32)) % seq_size
    tp_size = lax.axis_size("tp")
    sources = (tp_index - jnp.arange(tp_size, dtype=jnp.int32)) % tp_size
    targets = (tp_index + jnp.arange(tp_size, dtype=jnp.int32)) % tp_size
    last_section = section.astype(jnp.int32).reshape(1)
    group = GROUP if micros % GROUP == 0 else 1
    groups = micros // group

    def own(values):
        return lax.dynamic_slice_in_dim(values, tp_index * own_rows, own_rows, 0)

    def whole_out_weight(whole, piece, member, members):
        for step in range(0, seq_size, 2):
            moved = ring(piece, "seq", step) if step else piece
            for at, values in (
                ((seq_index - step) % seq_size, moved),
                (((seq_index ^ 1) - step) % seq_size, crossed(moved, 1)),
            ):
                if whole is not None:
                    values = after(values, whole)
                whole = narrow_into(
                    whole, values, at.astype(jnp.int32).reshape(1), width, member, members, tp_size
                )
        return whole

    spare = jnp.zeros((width, 128 - 2 * heads), LOW)
    in_weight = jnp.concatenate(
        [query_weight, key_weight, value_weight, outgate_weight, decay_weight, beta_weight, spare], 1
    )
    conv_cols = 2 * key_cols + value_cols
    offsets = jnp.arange(rows, dtype=jnp.int32)

    def micro_of(step, member):
        return jnp.clip(step - section, 0, groups - 1) * group + member

    def reset_flags(micro):
        starts = micro * (rows * seq_size) + seq_index * rows + offsets
        flags = lax.dynamic_index_in_dim(doc_start, micro, 0, keepdims=False) == starts
        return jnp.broadcast_to(flags.astype(F32)[:, None], (rows, 128))

    def mix(residual, step, member, border_carry):
        micro = micro_of(step, member)
        hidden, projected = enter(residual, norm_in, in_weight)
        moved = ring(projected[rows - 8 :, :conv_cols], "seq", 1)
        border = jnp.where(at_start, border_carry, moved)
        resets = reset_flags(micro)
        carried, local_out, maps, inverse = mixer_local(
            sizes, projected, resets, border, taps, rate, bias
        )
        saved[step, member] = dict(
            hidden=hidden, border=border, projected=projected, resets=resets, carried=carried,
            maps=all_seq(maps), inverse=inverse,
        )
        return moved, local_out

    def gate(step, member, local_out, state):
        kept = saved[step, member]
        kept["gated"], kept["output"], kept["entry_state"], state = mixer_gate(
            sizes, order, kept["maps"], state, kept["carried"], local_out, kept["projected"], head_norm
        )
        return state

    def rows_outer(name):
        return jnp.concatenate(
            [
                jnp.where(section == 0, saved[0, member][name], saved[groups, member][name])
                for member in range(group)
            ],
            0,
        )

    def rows_inner(name):
        return jnp.concatenate(
            [saved[at, member][name] for at in range(1, groups) for member in range(group)], 0
        )

    def all_rows(name):
        return jnp.concatenate([rows_outer(name), rows_inner(name)], 0)

    saved = {}
    section_rows = {}
    part = width // seq_size
    entering = [inputs[member].astype(F32) * (section == 0) for member in range(group)]
    residuals = [gather_tp(values) for values in entering]
    out_piece = widen(lax.dynamic_slice_in_dim(out_weight, seq_index * part, part, 1))
    out_pieces = [
        gather_tp(after(values, *entering)) for values in jnp.split(out_piece, 2, 0)
    ]
    out_full = None
    border_carry = jnp.zeros((8, conv_cols), F32)
    state = jnp.zeros((heads, key_size, value_size), F32)
    late_sums = []
    for step in range(groups + 1):
        all_gated = []
        last = None
        for member in range(group):
            residual = residuals[member] if last is None else after(residuals[member], last)
            border_carry, local_out = mix(residual, step, member, border_carry)
            if step == groups and all_gated:
                local_out = after(local_out, all_gated[-1])
            state = gate(step, member, local_out, state)
            last = saved[step, member]["gated"]
            saved[step, member]["entering"] = entering[member]
            residuals[member] = residual
            all_gated.append(lax.all_gather(last, "tp", axis=0))
        if out_full is None:
            for member, piece in enumerate(out_pieces):
                out_full = whole_out_weight(out_full, after(piece, last), member, 2)
        next_entering, next_residuals = [], []
        all_sums = []
        for member in range(group):
            kept = saved[step, member]
            mixed, kept["hidden_feed"], kept["gate_act"], kept["up_act"], kept["inner"], sums = join_heads(
                residuals[member], after(all_gated[member], last), out_full, norm_feed,
                gate_weight, up_weight, down_weight,
            )
            kept["mixed"] = own(mixed)
            all_sums.append(scatter_tp(sums) if step < groups else sums)
        if step == groups:
            late_sums = all_sums
            break
        ready = None
        for member in range(group):
            summed = all_sums[member] if ready is None else after(all_sums[member], ready)
            out_rows = saved[step, member]["mixed"] + summed
            section_rows[step, member] = out_rows
            handed = handed_on(out_rows, "section", 1)
            micro = micro_of(step + 1, member)
            given = lax.dynamic_index_in_dim(inputs, micro, 0, keepdims=False).astype(F32)
            ready = jnp.where(section == 0, given, handed)
            next_entering.append(ready)
            next_residuals.append(gather_tp(ready))
        entering, residuals = next_entering, next_residuals

    nothing = jnp.zeros((rows, width), F32)
    tail_carry = jnp.zeros((8, conv_cols), F32)
    state_grad = jnp.zeros((heads, key_size, value_size), F32)
    in_grads = {}
    norm_in_grad = jnp.zeros((width,), F32)
    norm_feed_grad = jnp.zeros((width,), F32)
    gain_grad = jnp.zeros((value_size,), F32)
    taps_grad = jnp.zeros(taps.shape, F32)
    side_sums = jnp.zeros((8, 128), F32)
    received = [jnp.zeros((own_rows, width), F32)] * group
    handed = [nothing] * group
    members = list(reversed(range(group)))
    for back_step in range(groups + 1):
        step = groups - back_step
        tops, feed_grads = {}, {}
        for member in members:
            kept = saved[step, member]
            given = lax.dynamic_index_in_dim(cotangent, micro_of(step, member), 0, keepdims=False)
            if step == 0:
                given = jnp.where(section == 0, given, jnp.zeros_like(given))
            kept["top_low"], kept["gate_low"], kept["up_low"], sums = feed_back(
                last_section, given, handed[member], kept["gate_act"], kept["up_act"],
                gate_weight, up_weight, down_weight,
            )
            tops[member] = jnp.where(section == 0, received[member], own(given).astype(F32))
            if back_step < groups:
                feed_grads[member] = scatter_tp(sums)
            else:
                summed = scatter_tp(jnp.where(section == 0, sums, late_sums[member]))
                section_rows[groups, member] = saved[groups, member]["mixed"] + summed
                feed_grads[member] = jnp.where(section == 0, summed, 0.0)
        if back_step == groups:
            feed_all, top_all = all_rows("hidden_feed"), all_rows("top_low")
            gate_parts = core_sums(feed_all, all_rows("gate_low"), 0)
            feed_grads[members[0]] = after(feed_grads[members[0]], *gate_parts)
            up_parts = core_sums(feed_all, all_rows("up_low"), 0)
            feed_grads[members[-1]] = after(feed_grads[members[-1]], *up_parts)
        last = None
        all_sums = {}
        for member in members:
            kept = saved[step, member]
            feed_grad = feed_grads[member] if last is None else after(feed_grads[member], conv_grad)
            feed_part, mixed_grad, *pieces = mix_back(
                targets, feed_grad, kept["mixed"], tops[member], norm_feed, out_full
            )
            kept["mixed_grad"] = mixed_grad
            norm_feed_grad = norm_feed_grad + feed_part[0]
            pieces = [ring(piece, "tp", at) if at else piece for at, piece in enumerate(pieces)]
            if last is not None:
                pieces[0] = after(pieces[0], last)
            output_grad, outgate_low, gain_part, entry_grad = mixer_gate_back(
                sizes, sources, pieces, kept["output"], kept["projected"], head_norm, kept["carried"]
            )
            gain_grad = gain_grad + gain_part[0]
            conv_grad, border_grad, taps_part, side_low, sums_part, state_grad = mixer_local_back(
                sizes, order, kept["maps"], all_seq(entry_grad), state_grad, kept["projected"],
                kept["resets"], kept["border"], taps, rate, bias, kept["inverse"],
                kept["entry_state"], output_grad,
            )
            moved = ring(border_grad, "seq", -1)
            tail = jnp.where(at_end, tail_carry, moved)
            tail_carry = moved
            if back_step == groups and member == members[0]:
                grad_gate = chip_sums([after(part, tail) for part in gate_parts])
            elif back_step == groups and member == members[-1]:
                tail = after(tail, grad_gate, all_sums[members[0]])
            taps_grad = taps_grad + taps_part
            side_sums = side_sums + sums_part
            kept["projected_low"], last = leave(conv_grad, tail, outgate_low, side_low, in_weight)
            all_sums[member] = scatter_tp(last)
            if back_step == groups and member == members[0]:
                inner_mixed = gather_tp(after(rows_inner("mixed_grad"), last))
        ready = None
        received, handed = [None] * group, [None] * group
        if back_step == groups:
            outer_mixed = gather_tp(after(rows_outer("mixed_grad"), last))
            in_parts = core_sums(all_rows("hidden"), all_rows("projected_low"), 0)
            down_parts = core_sums(after(all_rows("inner"), in_parts[0]), top_all, 1)
            grad_up = chip_sums([after(part, tail) for part in up_parts])
            inner_mixed = narrow_into(
                None, after(inner_mixed, grad_up, down_parts[0]), jnp.zeros((1,), jnp.int32), width, 0, 1, tp_size
            )
            ready = inner_mixed
        for member in members:
            kept = saved[step, member]
            summed = all_sums[member]
            if ready is not None and (back_step < groups or member == members[-1]):
                summed = after(summed, ready)
            entering_back, in_part = row_norm_back(kept["entering"], norm_in[0], summed)
            norm_in_grad = norm_in_grad + in_part
            own_grad = kept["mixed_grad"] + entering_back
            in_grads[step, member] = own_grad
            if back_step < groups:
                ready = handed_on(own_grad, "section", -1)
                received[member] = ready
                handed[member] = gather_tp(ready)
    def of_section(values):
        return [
            jnp.where(section == 0, values[at, member], values[at + 1, member])
            for at in range(groups)
            for member in range(group)
        ]

    grad_in = chip_sums([after(part, tail) for part in in_parts])
    grad_down = chip_sums([after(part, tail) for part in down_parts])
    outer_mixed = after(outer_mixed, grad_in)
    zero = jnp.zeros((1,), jnp.int32)

    def by_device(name, rows_of, count):
        split = rows_of(name).astype(LOW).reshape(count, tp_size, own_rows, value_cols)
        return jnp.moveaxis(split, 0, 1).reshape(count * rows, value_cols)

    mixed_all = jnp.concatenate(
        [narrow_into(None, outer_mixed, zero, width, 0, 1, tp_size), inner_mixed], 0
    )
    gated_all = jnp.concatenate(
        [by_device("gated", rows_outer, group), by_device("gated", rows_inner, micros - group)], 0
    )
    out_parts = core_sums(gated_all, mixed_all, 1)
    grad_out = chip_sums(out_parts)

    shared = butterfly(jnp.concatenate([norm_in_grad, norm_feed_grad, gain_grad]), "tp")
    small = butterfly(
        jnp.concatenate(
            [
                after(shared, out_parts[0]), taps_grad.reshape(-1), side_sums[0, :heads],
                side_sums[1, :heads],
            ]
        ),
        "seq",
    )
    bounds = [0, width, 2 * width, 2 * width + value_size]
    bounds += [bounds[-1] + taps.size, bounds[-1] + taps.size + heads, bounds[-1] + taps.size + 2 * heads]
    norm_in_grad, norm_feed_grad, gain_grad, taps_grad, log_grad, bias_grad = [
        small[low:high] for low, high in zip(bounds[:-1], bounds[1:])
    ]
    taps_grad = taps_grad.reshape(taps.shape)
    bounds = [
        0, key_cols, 2 * key_cols, conv_cols, conv_cols + value_cols, conv_cols + value_cols + heads,
        conv_cols + value_cols + 2 * heads,
    ]
    in_parts = [grad_in[:, low:high] for low, high in zip(bounds[:-1], bounds[1:])]
    return (
        jnp.stack(of_section(section_rows))[None],
        jnp.stack(of_section(in_grads))[None],
        norm_in_grad[None],
        *[member[None] for member in in_parts],
        taps_grad[None, :, :key_cols],
        taps_grad[None, :, key_cols : 2 * key_cols],
        taps_grad[None, :, 2 * key_cols :],
        log_grad[None],
        bias_grad[None],
        gain_grad[None],
        grad_out[None],
        norm_feed_grad[None],
        grad_gate[None],
        grad_up[None],
        grad_down[None],
    )


def solution(mesh):
    by_column, by_row = P("section", None, "tp"), P("section", "tp", None)
    placed = (
        P(None, ("seq", "tp"), None),
        P(None, "seq", None),
        P(None, "seq"),
        P("section", None),
        *[by_column] * 9,
        P("section", "tp"),
        P("section", "tp"),
        P("section", None),
        by_row,
        P("section", None),
        by_column,
        by_column,
        by_row,
    )
    rows_out = P("section", None, ("seq", "tp"), None)
    both = P("section", "seq", "tp")
    return jax.shard_map(
        local,
        mesh=mesh,
        in_specs=placed,
        out_specs=(
            rows_out,
            rows_out,
            P("section", None),
            *[both] * 6,
            *[by_column] * 3,
            P("section", "tp"),
            P("section", "tp"),
            P("section", None),
            P("section", "tp", "seq"),
            P("section", None),
            both,
            both,
            P("section", "tp", "seq"),
        ),
        check_vma=False,
    )
```

time: 2900 us -> 2090 us (0.72)
  waiting for transfers between devices: 1590 us -> 1160 us
  local copies, waits for them, and re-layouts: 449 us -> 132 us
  matrix products: 290 us -> 87.1 us
  Pallas kernels: 319 us -> 440 us
  starting transfers between devices: 41 us -> 129 us
  other arithmetic: 173 us -> 104 us
    all_gather x36 -> x20, waiting for transfers between devices: 840 us -> 335 us  [the longest x14 237 us: gather_tp(): return lax.all_gather(values, 'tp', axis=0, tiled=True)]
    ppermute x12 -> x73, waiting for transfers between devices: 87.2 us -> 485 us  [ring(): lax.ppermute(value, axis, [(at, (at + steps) % count) for at in range(cou...]
    reduce_scatter x18 -> x16, waiting for transfers between devices: 487 us -> 214 us  [scatter_tp(): return lax.psum_scatter(values, 'tp', scatter_dimension=0, tiled=True)]
    dot_general x59 -> x20, matrix products: 290 us -> 87.1 us  [low_dot(): lax.dot_general(a, b, (contract, ((), ())), preferred_element_type=F32)]
    unnamed x940 -> x751, local copies, waits for them, and re-layouts: 248 us -> 101 us
    pallas_call x36 -> x65, Pallas kernels: 319 us -> 440 us  [the longest x54 398 us: call(): pl.pallas_call(kernel, grid=(1,), in_specs=specs, out_specs=[whole(array)...]
    psum x1 -> x0, waiting for transfers between devices: 83.2 us -> none  [local(): lax.psum(jnp.concatenate([norm_in_grad, norm_feed_grad, gain_grad, jnp.wh...]
    ppermute x12 -> x73, starting transfers between devices: 7.79 us -> 84.8 us  [ring(): lax.ppermute(value, axis, [(at, (at + steps) % count) for at in range(cou...]
  transfers between devices with their start and end apart: 85 -> 135, of which waited for: 56 -> 92; matrix products, arithmetic and copies ran while one was open for 22% -> 10% of each run, Pallas kernels for 9% -> 20%
where the time goes in v2:
time: 2090 us; the launch traced here: 2070 us
  waiting for transfers between devices  1160 us (56%)
  Pallas kernels  440 us (21%)
  local copies, waits for them, and re-layouts  132 us (6%)
  starting transfers between devices  129 us (6%)
  other arithmetic  104 us (5%)
  matrix products  87.1 us (4%)
    ppermute x73, waiting for transfers between devices, ring(): lax.ppermute(value, axis, [(at, (at + steps) % count) for at in range(cou...  485 us
    pallas_call x54, Pallas kernels, call(): pl.pallas_call(kernel, grid=(1,), in_specs=specs, out_specs=[whole(array)...  398 us
    all_gather x14, waiting for transfers between devices, gather_tp(): return lax.all_gather(values, 'tp', axis=0, tiled=True)  237 us
    reduce_scatter x16, waiting for transfers between devices, scatter_tp(): return lax.psum_scatter(values, 'tp', scatter_dimension=0, tiled=True)  214 us
    ppermute x8, waiting for transfers between devices, handed_on(): lax.ppermute(value, axis, [(at, at + steps) for at in range(first, last)])  102 us
    unnamed x751, local copies, waits for them, and re-layouts  101 us
    all_gather x6, waiting for transfers between devices, local(): all_gated.append(lax.all_gather(last, 'tp', axis=0))  98 us
    dot_general x20, matrix products, low_dot(): lax.dot_general(a, b, (contract, ((), ())), preferred_element_type=F32)  87.1 us
  transfers between devices with their start and end apart: 135, of which 92 were waited for; matrix products, arithmetic and copies ran while one was open for 10% of the time, Pallas kernels for 20%

profile of v2, /device:TPU:0, one launch (start us, length us, event | category | flops | bytes accessed | tf_op | source)
XLA Modules:
  0.0 2066.8 jit_solution(16105675592862696154)
XLA Ops:
  28.7 30.1 %all-gather.53.cloned.1.call-done = f32[1,256,2048]{2,1,0:T(8,128)} async-done(((f32[1,64,2048]{2,1,0:T(8,128)}), f32[1,256,2048]{2,1,0:T(8,128)}) %all-gather.53.cloned.1.call-update) | async-done | bytes 2097168 | tf_op jit(solution)/shard_map/all_gather | solution.py:777
  154.0 45.2 %all-gather.29.cloned.1.call-done.source_ref = f32[1024,512]{1,0:T(8,128)} async-done(((f32[256,512]{1,0:T(8,128)}), f32[1024,512]{1,0:T(8,128)}) %all-gather.29.cloned.1.call-update) | async-done | bytes 2097168 | tf_op jit(solution)/shard_map/all_gather | solution.py:777
  201.8 45.0 %collective-permute-done.8.source_ref = f32[1024,512]{1,0:T(8,128)S(1)} collective-permute-done((f32[1024,512]{1,0:T(8,128)}, f32[1024,512]{1,0:T(8,128)S(1)}, u32[]{:S(2)}, u32[]{:S(2)}) %collective-permute-start.8) | collective-permute-done | bytes 2097184 | tf_op jit(solution)/shard_map/ppermute | solution.py:763
  276.5 14.5 join_heads.6
  292.6 14.7 join_heads.7
  307.4 30.7 %reduce-scatter.17.cloned.1.call-done = f32[64,2048]{1,0:T(8,128)} async-done(((f32[256,2048]{1,0:T(8,128)}), f32[64,2048]{1,0:T(8,128)}) %reduce-scatter.17.cloned.1.call-update) | async-done | bytes 524304 | tf_op jit(solution)/shard_map/reduce_scatter | solution.py:781
  356.2 28.1 %reduce-scatter.19.cloned.1.call-done = f32[64,2048]{1,0:T(8,128)} async-done(((f32[256,2048]{1,0:T(8,128)}), f32[64,2048]{1,0:T(8,128)}) %reduce-scatter.19.cloned.1.call-update) | async-done | bytes 524304 | tf_op jit(solution)/shard_map/reduce_scatter | solution.py:781
  402.5 28.6 %all-gather.33.cloned.1.call-done.rows_ref = f32[256,2048]{1,0:T(8,128)} async-done(((f32[64,2048]{1,0:T(8,128)}), f32[256,2048]{1,0:T(8,128)}) %all-gather.33.cloned.1.call-update) | async-done | bytes 2097168 | tf_op jit(solution)/shard_map/all_gather | solution.py:777
  523.5 14.8 join_heads.8
  538.3 31.2 %all-gather.63.cloned.1.call-done = f32[1024,512]{1,0:T(8,128)} async-done(((f32[256,512]{1,0:T(8,128)}), f32[1024,512]{1,0:T(8,128)}) %all-gather.63.cloned.1.call-update) | async-done | bytes 2097168 | tf_op jit(solution)/shard_map/all_gather | solution.py:952
  569.6 14.7 join_heads.9
  584.4 30.7 %reduce-scatter.21.cloned.1.call-done = f32[64,2048]{1,0:T(8,128)} async-done(((f32[256,2048]{1,0:T(8,128)}), f32[64,2048]{1,0:T(8,128)}) %reduce-scatter.21.cloned.1.call-update) | async-done | bytes 524304 | tf_op jit(solution)/shard_map/reduce_scatter | solution.py:781
  633.2 27.8 %reduce-scatter.23.cloned.1.call-done = f32[64,2048]{1,0:T(8,128)} async-done(((f32[256,2048]{1,0:T(8,128)}), f32[64,2048]{1,0:T(8,128)}) %reduce-scatter.23.cloned.1.call-update) | async-done | bytes 524304 | tf_op jit(solution)/shard_map/reduce_scatter | solution.py:781
  679.3 28.4 %all-gather.37.cloned.1.call-done.rows_ref = f32[256,2048]{1,0:T(8,128)} async-done(((f32[64,2048]{1,0:T(8,128)}), f32[256,2048]{1,0:T(8,128)}) %all-gather.37.cloned.1.call-update) | async-done | bytes 2097168 | tf_op jit(solution)/shard_map/all_gather | solution.py:777
  776.8 23.2 %all-gather.65.cloned.1.call-done = f32[1024,512]{1,0:T(8,128)} async-done(((f32[256,512]{1,0:T(8,128)}), f32[1024,512]{1,0:T(8,128)}) %all-gather.65.cloned.1.call-update) | async-done | bytes 2097168 | tf_op jit(solution)/shard_map/all_gather | solution.py:952
  812.4 40.0 %all-gather.67.cloned.1.call-done = f32[1024,512]{1,0:T(8,128)} async-done(((f32[256,512]{1,0:T(8,128)}), f32[1024,512]{1,0:T(8,128)}) %all-gather.67.cloned.1.call-update) | async-done | bytes 2097168 | tf_op jit(solution)/shard_map/all_gather | solution.py:952
  852.4 14.5 join_heads.11
  884.5 14.6 join_heads.10
  1082.4 14.9 collective-permute-done.48
  1097.4 31.3 %reduce-scatter.29.cloned.1.call-done = f32[64,2048]{1,0:T(8,128)} async-done(((f32[256,2048]{1,0:T(8,128)}), f32[64,2048]{1,0:T(8,128)}) %reduce-scatter.29.cloned.1.call-update) | async-done | bytes 524304 | tf_op jit(solution)/shard_map/reduce_scatter | solution.py:781
  1148.9 26.6 %all-gather.43.cloned.1.call-done.handed_ref = f32[256,2048]{1,0:T(8,128)} async-done(((f32[64,2048]{1,0:T(8,128)}), f32[256,2048]{1,0:T(8,128)}) %all-gather.43.cloned.1.call-update) | async-done | bytes 2097168 | tf_op jit(solution)/shard_map/all_gather | solution.py:777
  1194.2 27.4 %all-gather.41.cloned.1.call-done.handed_ref = f32[256,2048]{1,0:T(8,128)} async-done(((f32[64,2048]{1,0:T(8,128)}), f32[256,2048]{1,0:T(8,128)}) %all-gather.41.cloned.1.call-update) | async-done | bytes 2097168 | tf_op jit(solution)/shard_map/all_gather | solution.py:777
  1241.6 25.5 %reduce-scatter.35.cloned.1.call-done.grad_ref = f32[64,2048]{1,0:T(8,128)} async-done(((f32[256,2048]{1,0:T(8,128)}), f32[64,2048]{1,0:T(8,128)}) %reduce-scatter.35.cloned.1.call-update) | async-done | bytes 524304 | tf_op jit(solution)/shard_map/reduce_scatter | solution.py:781
  1410.9 15.1 collective-permute-done.64
  1426.2 31.2 %reduce-scatter.37.cloned.1.call-done = f32[64,2048]{1,0:T(8,128)} async-done(((f32[256,2048]{1,0:T(8,128)}), f32[64,2048]{1,0:T(8,128)}) %reduce-scatter.37.cloned.1.call-update) | async-done | bytes 524304 | tf_op jit(solution)/shard_map/reduce_scatter | solution.py:781
  1483.4 20.8 %all-gather.47.cloned.1.call-done.handed_ref = f32[256,2048]{1,0:T(8,128)} async-done(((f32[64,2048]{1,0:T(8,128)}), f32[256,2048]{1,0:T(8,128)}) %all-gather.47.cloned.1.call-update) | async-done | bytes 2097168 | tf_op jit(solution)/shard_map/all_gather | solution.py:777
  1527.3 23.0 %all-gather.45.cloned.1.call-done.handed_ref = f32[256,2048]{1,0:T(8,128)} async-done(((f32[64,2048]{1,0:T(8,128)}), f32[256,2048]{1,0:T(8,128)}) %all-gather.45.cloned.1.call-update) | async-done | bytes 2097168 | tf_op jit(solution)/shard_map/all_gather | solution.py:777
  1725.9 25.2 %collective-permute-done.82.refs_7_ = f32[2,128,256]{2,1,0:T(8,128)S(1)} collective-permute-done((f32[2,128,256]{2,1,0:T(8,128)S(1)}, f32[2,128,256]{2,1,0:T(8,128)S(1)}, u32[]{:S(2)}, u32[]{:S(2)}) %collective-permute-start.82) | collective-permute-done | bytes 262176 | tf_op jit(solution)/shard_map/ppermute | solution.py:763
  1807.8 55.4 %collective-permute-done.85 = f32[512,1408]{1,0:T(8,128)} collective-permute-done((f32[512,1408]{1,0:T(8,128)}, f32[512,1408]{1,0:T(8,128)}, u32[]{:S(2)}, u32[]{:S(2)}) %collective-permute-start.85) | collective-permute-done | bytes 2883616 | tf_op jit(solution)/shard_map/ppermute | solution.py:763
  1915.4 53.5 %collective-permute-done.91 = f32[512,1664]{1,0:T(8,128)S(1)} collective-permute-done((f32[512,1664]{1,0:T(8,128)S(1)}, f32[512,1664]{1,0:T(8,128)S(1)}, u32[]{:S(2)}, u32[]{:S(2)}) %collective-permute-start.91) | collective-permute-done | bytes 3407904 | tf_op jit(solution)/shard_map/ppermute | solution.py:763
  1998.4 32.4 %collective-permute-done.98 = f32[1408,512]{1,0:T(8,128)} collective-permute-done((f32[1408,512]{1,0:T(8,128)}, f32[1408,512]{1,0:T(8,128)}, u32[]{:S(2)}, u32[]{:S(2)}) %collective-permute-start.98) | collective-permute-done | bytes 2883616 | tf_op jit(solution)/shard_map/ppermute | solution.py:763
  2034.9 18.2 collective-permute-done.94
  (1249 shorter events, 1170.2 us)
Async XLA Ops:
  10.3 143.0 %all-gather.31.cloned.1.call-start = ((), (), s32[]{:S(2)}) async-start(), calls=%async_computation.17 | async-start | bytes 2621440 | tf_op jit(solution)/shard_map/all_gather | solution.py:777
  15.6 183.6 %all-gather.29.cloned.1.call-start = ((), (), s32[]{:S(2)}) async-start(), calls=%async_computation.16 | async-start | bytes 2621440 | tf_op jit(solution)/shard_map/all_gather | solution.py:777
  16.1 242.1 %all-gather.55.cloned.1.call-start = ((), (), s32[]{:S(2)}) async-start(), calls=%async_computation.45 | async-start | bytes 2621440 | tf_op jit(solution)/shard_map/all_gather | solution.py:952
  102.9 189.7 %all-gather.61.cloned.1.call-start = ((), (), s32[]{:S(2)}) async-start(), calls=%async_computation.48 | async-start | bytes 2621440 | tf_op jit(solution)/shard_map/all_gather | solution.py:952
  200.7 137.4 %reduce-scatter.17.cloned.1.call-start = ((), (), s32[]{:S(2)}) async-start(), calls=%async_computation.18 | async-start | bytes 2621440 | tf_op jit(solution)/shard_map/reduce_scatter | solution.py:781
  307.3 123.8 %all-gather.33.cloned.1.call-start = ((), (), s32[]{:S(2)}) async-start(), calls=%async_computation.19 | async-start | bytes 2621440 | tf_op jit(solution)/shard_map/all_gather | solution.py:777
  356.1 121.1 %all-gather.35.cloned.1.call-start = ((), (), s32[]{:S(2)}) async-start(), calls=%async_computation.21 | async-start | bytes 2621440 | tf_op jit(solution)/shard_map/all_gather | solution.py:777
  402.4 121.0 %all-gather.59.cloned.1.call-start = ((), (), s32[]{:S(2)}) async-start(), calls=%async_computation.47 | async-start | bytes 2621440 | tf_op jit(solution)/shard_map/all_gather | solution.py:952
  538.3 122.8 %reduce-scatter.23.cloned.1.call-start = ((), (), s32[]{:S(2)}) async-start(), calls=%async_computation.23 | async-start | bytes 2621440 | tf_op jit(solution)/shard_map/reduce_scatter | solution.py:781
  584.3 123.4 %all-gather.37.cloned.1.call-start = ((), (), s32[]{:S(2)}) async-start(), calls=%async_computation.24 | async-start | bytes 2621440 | tf_op jit(solution)/shard_map/all_gather | solution.py:777
  633.1 120.9 %all-gather.39.cloned.1.call-start = ((), (), s32[]{:S(2)}) async-start(), calls=%async_computation.25 | async-start | bytes 2621440 | tf_op jit(solution)/shard_map/all_gather | solution.py:777
  679.2 120.7 %all-gather.65.cloned.1.call-start = ((), (), s32[]{:S(2)}) async-start(), calls=%async_computation.50 | async-start | bytes 2621440 | tf_op jit(solution)/shard_map/all_gather | solution.py:952
  751.7 100.7 %all-gather.67.cloned.1.call-start = ((), (), s32[]{:S(2)}) async-start(), calls=%async_computation.51 | async-start | bytes 2621440 | tf_op jit(solution)/shard_map/all_gather | solution.py:952
  807.6 119.4 %reduce-scatter.27.cloned.1.call-start = ((), (), s32[]{:S(2)}) async-start(), calls=%async_computation.27 | async-start | bytes 2621440 | tf_op jit(solution)/shard_map/reduce_scatter | solution.py:781
  884.2 116.0 %reduce-scatter.25.cloned.1.call-start = ((), (), s32[]{:S(2)}) async-start(), calls=%async_computation.26 | async-start | bytes 2621440 | tf_op jit(solution)/shard_map/reduce_scatter | solution.py:781
  916.3 160.5 %reduce-scatter.31.cloned.1.call-start = ((), (), s32[]{:S(2)}) async-start(), calls=%async_computation.29 | async-start | bytes 2621440 | tf_op jit(solution)/shard_map/reduce_scatter | solution.py:781
  998.3 130.3 %reduce-scatter.29.cloned.1.call-start = ((), (), s32[]{:S(2)}) async-start(), calls=%async_computation.28 | async-start | bytes 2621440 | tf_op jit(solution)/shard_map/reduce_scatter | solution.py:781
  1076.6 98.9 %all-gather.43.cloned.1.call-start = ((), (), s32[]{:S(2)}) async-start(), calls=%async_computation.32 | async-start | bytes 2621440 | tf_op jit(solution)/shard_map/all_gather | solution.py:777
  1097.3 124.3 %all-gather.41.cloned.1.call-start = ((), (), s32[]{:S(2)}) async-start(), calls=%async_computation.30 | async-start | bytes 2621440 | tf_op jit(solution)/shard_map/all_gather | solution.py:777
  1148.5 118.6 %reduce-scatter.35.cloned.1.call-start = ((), (), s32[]{:S(2)}) async-start(), calls=%async_computation.33 | async-start | bytes 2621440 | tf_op jit(solution)/shard_map/reduce_scatter | solution.py:781
  1194.1 136.3 %reduce-scatter.33.cloned.1.call-start = ((), (), s32[]{:S(2)}) async-start(), calls=%async_computation.31 | async-start | bytes 2621440 | tf_op jit(solution)/shard_map/reduce_scatter | solution.py:781
  1238.9 166.2 %reduce-scatter.39.cloned.1.call-start = ((), (), s32[]{:S(2)}) async-start(), calls=%async_computation.35 | async-start | bytes 2621440 | tf_op jit(solution)/shard_map/reduce_scatter | solution.py:781
  1330.4 127.0 %reduce-scatter.37.cloned.1.call-start = ((), (), s32[]{:S(2)}) async-start(), calls=%async_computation.34 | async-start | bytes 2621440 | tf_op jit(solution)/shard_map/reduce_scatter | solution.py:781
  1405.0 99.3 %all-gather.47.cloned.1.call-start = ((), (), s32[]{:S(2)}) async-start(), calls=%async_computation.38 | async-start | bytes 2621440 | tf_op jit(solution)/shard_map/all_gather | solution.py:777
  1426.1 124.3 %all-gather.45.cloned.1.call-start = ((), (), s32[]{:S(2)}) async-start(), calls=%async_computation.36 | async-start | bytes 2621440 | tf_op jit(solution)/shard_map/all_gather | solution.py:777
  1478.1 117.7 %reduce-scatter.43.cloned.1.call-start = ((), (), s32[]{:S(2)}) async-start(), calls=%async_computation.39 | async-start | bytes 2621440 | tf_op jit(solution)/shard_map/reduce_scatter | solution.py:781
  1525.0 163.1 %reduce-scatter.41.cloned.1.call-start = ((), (), s32[]{:S(2)}) async-start(), calls=%async_computation.37 | async-start | bytes 2621440 | tf_op jit(solution)/shard_map/reduce_scatter | solution.py:781
  1580.0 192.9 %reduce-scatter.45.cloned.1.call-start = ((), (), s32[]{:S(2)}) async-start(), calls=%async_computation.40 | async-start | bytes 2621440 | tf_op jit(solution)/shard_map/reduce_scatter | solution.py:781
  1659.5 210.8 %all-gather.49.cloned.1.call-start = ((), (), s32[]{:S(2)}) async-start(), calls=%async_computation.42 | async-start | bytes 5242880 | tf_op jit(solution)/shard_map/all_gather | solution.py:777
  1688.0 186.9 %reduce-scatter.47.cloned.1.call-start = ((), (), s32[]{:S(2)}) async-start(), calls=%async_computation.41 | async-start | bytes 2621440 | tf_op jit(solution)/shard_map/reduce_scatter | solution.py:781
  1798.4 172.6 %all-gather.51.cloned.1.call-start = ((), (), s32[]{:S(2)}) async-start(), calls=%async_computation.43 | async-start | bytes 5242880 | tf_op jit(solution)/shard_map/all_gather | solution.py:777
  1895.1 135.7 %collective-permute-start.98 = (f32[1408,512]{1,0:T(8,128)}, f32[1408,512]{1,0:T(8,128)}, u32[]{:S(2)}, u32[]{:S(2)}) collective-permute-start(f32[1408,512]{1,0:T(8,128)} %convolution_add_fusion.1), channel_id=1, source_target_pairs={{0,8},{4,12},{8,0},{12,4},{1,9},{5,13},{9,1},{13,5},{2,10},{6,14},... | collective-permute-start | bytes 8650760 | tf_op jit(solution)/shard_map/ppermute | solution.py:763
  (476 other events, 8399.2 us)
Sparse Core Ops, SparseCore 0:
  10.2 48.5 all-gather.52
  60.9 44.7 all-gather.56
  107.8 44.6 all-gather.30
  154.5 44.6 all-gather.28
  201.2 44.6 all-gather.54
  247.9 44.6 all-gather.60
  341.0 43.1 reduce-scatter.18
  385.8 45.2 all-gather.32
  432.5 44.6 all-gather.34
  478.8 44.6 all-gather.58
  524.9 44.6 all-gather.62
  617.9 43.1 reduce-scatter.22
  662.5 45.2 all-gather.36
  709.2 44.8 all-gather.38
  755.5 44.3 all-gather.64
  807.7 44.6 all-gather.66
  929.2 51.4 reduce-scatter.24
  998.4 62.2 reduce-scatter.30
  1076.8 51.8 reduce-scatter.28
  1130.2 45.2 all-gather.42
  1176.9 44.6 all-gather.40
  1224.5 42.5 reduce-scatter.34
  1269.9 51.5 reduce-scatter.32
  1330.5 63.4 reduce-scatter.38
  1405.1 52.2 reduce-scatter.36
  1459.0 45.2 all-gather.46
  1505.7 44.6 all-gather.44
  1598.2 51.5 reduce-scatter.40
  1659.7 55.9 reduce-scatter.44
  1717.8 83.1 all-gather.48
  1804.1 46.4 reduce-scatter.46
  1880.5 89.0 all-gather.50
  (4 shorter events, 170.1 us)

commit v3 on v2

--- a/solution.py
+++ b/solution.py
@@ -11,7 +11,6 @@
 F32 = jnp.float32
 LOW = jnp.bfloat16
 VMEM_BYTES = 48 * 1024 * 1024
-GROUP = 2
 NN = ((1,), (0,))
 NT = ((1,), (1,))
 TN = ((0,), (0,))
@@ -422,6 +421,21 @@
     sums_ref[...] = sums
 
 
+class Clock:
+    latest = None
+
+
+def tick(value):
+    if Clock.latest is None:
+        return value
+    return lax.optimization_barrier((value, Clock.latest))[0]
+
+
+def tock(results):
+    Clock.latest = min(results, key=lambda array: array.size)
+    return results
+
+
 def smem():
     return pl.BlockSpec(memory_space=pltpu.SMEM)
 
@@ -432,9 +446,13 @@
 
 def call(kernel, out_shape, operands, name, micros, in_specs=None, scratch=(), vmem=VMEM_BYTES):
     whole = lambda array: pl.BlockSpec(array.shape, lambda i: (0,) * len(array.shape))
+    vectors = [at for at in range(len(operands)) if in_specs is None or in_specs[at] is None]
+    least = min(vectors, key=lambda at: operands[at].size)
+    operands = list(operands)
+    operands[least] = tick(operands[least])
     specs = [whole(array) for array in operands] if in_specs is None else in_specs
     specs = [whole(array) if spec is None else spec for spec, array in zip(specs, operands)]
-    return pl.pallas_call(
+    results = pl.pallas_call(
         kernel,
         grid=(1,),
         in_specs=specs,
@@ -443,10 +461,11 @@
         scratch_shapes=list(scratch),
         compiler_params=pltpu.CompilerParams(vmem_limit_bytes=vmem),
         cost_estimate=pl.CostEstimate(
-            flops=int(micros * 3e+08), bytes_accessed=int(micros * 900000), transcendentals=0
+            flops=int(micros * 1e+07), bytes_accessed=int(micros * 30000), transcendentals=0
         ),
         name=name,
     )(*operands)
+    return tock(results)
 
 
 def shape(dims, dtype=F32):
@@ -594,7 +613,28 @@
         out_shape=shape((rows * members, total), LOW),
         input_output_aliases={2: 0} if more else {},
         name="narrow_into",
-    )(index, values, *more)
+    )(tick(index), values, *more)
+
+
+def choose_kernel(first_ref, own_ref, other_ref, low_ref):
+    low_ref[...] = jnp.where(first_ref[0] == 1, own_ref[...], other_ref[...]).astype(LOW)
+
+
+def choose(first, paired, single, member, members, pieces):
+    rows, cols = single.shape
+    tile = rows // pieces
+    return pl.pallas_call(
+        choose_kernel,
+        grid=(pieces,),
+        in_specs=[
+            smem(),
+            pl.BlockSpec((tile, cols), lambda i: (i, 0)),
+            pl.BlockSpec((tile, cols), lambda i: (i * members + member, 0)),
+        ],
+        out_specs=pl.BlockSpec((tile, cols), lambda i: (i, 0)),
+        out_shape=shape((rows, cols), LOW),
+        name="choose",
+    )(tick(first), single, paired)
 
 
 def enter_kernel(rows_ref, gain_ref, weight_ref, hidden_ref, projected_ref):
@@ -794,32 +834,49 @@
     return value
 
 
-def core_sums(left, right, axis):
-    count = lax.axis_size("seq")
-    chunk = (left, right)[axis].shape[1] // count
-    index = lax.axis_index("seq")
-    core, chip, chips = index % 2, index // 2, count // 2
-
-    def product(chip, core):
-        place = (chip * 2 + core) * chunk
-        if axis:
-            return low_dot(left, lax.dynamic_slice_in_dim(right, place, chunk, 1), TN)
-        return low_dot(lax.dynamic_slice_in_dim(left, place, chunk, 1), right, TN)
-
-    order = [(chip + step) % chips for step in range(1, chips)] + [chip]
-    received = [crossed(product(at, 1 - core), 1) for at in order]
-    return [product(at, core) + part for at, part in zip(order, received)]
-
-
-def chip_sums(parts):
-    total = parts[-1]
-    for step, part in enumerate(parts[:-1], 1):
-        total = total + ring(part, "seq", 2 * step)
-    return total
+class CoreSums:
+    def __init__(self, left, right, axis):
+        count = lax.axis_size("seq")
+        index = lax.axis_index("seq")
+        self.left, self.right, self.axis = left, right, axis
+        self.chunk = (left, right)[axis].shape[1] // count
+        self.core, chip, chips = index % 2, index // 2, count // 2
+        self.order = [(chip + step) % chips for step in range(1, chips)] + [chip]
+
+    def product(self, chip, core):
+        place = (chip * 2 + core) * self.chunk
+        left, right = self.left, self.right
+        if self.axis:
+            right = lax.dynamic_slice_in_dim(right, place, self.chunk, 1)
+        else:
+            left = lax.dynamic_slice_in_dim(left, place, self.chunk, 1)
+        return tock([low_dot(tick(left), right, TN)])[0]
+
+    def send(self):
+        self.received = [crossed(self.product(at, 1 - self.core), 1) for at in self.order]
+        return self
+
+    def sums(self):
+        return [
+            tock([self.product(at, self.core) + part])[0]
+            for at, part in zip(self.order, self.received)
+        ]
+
+
+def chip_moves(parts):
+    return [ring(part, "seq", 2 * step) for step, part in enumerate(parts[:-1], 1)]
+
+
+def total(parts, moved):
+    return sum(moved, parts[-1])
 
 
 def after(value, *others):
     return lax.optimization_barrier((value, *others))[0]
+
+
+def after_all(parts, *others):
+    return [None if part is None else after(part, *others) for part in parts]
 
 
 def local(
@@ -827,6 +884,7 @@
     decay_weight, beta_weight, conv_query, conv_key, conv_value, decay_log, decay_bias, head_norm,
     out_weight, norm_feed, gate_weight, up_weight, down_weight,
 ):
+    Clock.latest = None
     query_weight, key_weight, value_weight = query_weight[0], key_weight[0], value_weight[0]
     outgate_weight, decay_weight, beta_weight = outgate_weight[0], decay_weight[0], beta_weight[0]
     gate_weight, up_weight, down_weight, out_weight = (
@@ -850,8 +908,8 @@
     sources = (tp_index - jnp.arange(tp_size, dtype=jnp.int32)) % tp_size
     targets = (tp_index + jnp.arange(tp_size, dtype=jnp.int32)) % tp_size
     last_section = section.astype(jnp.int32).reshape(1)
-    group = GROUP if micros % GROUP == 0 else 1
-    groups = micros // group
+    groups = 2
+    group = micros // groups
 
     def own(values):
         return lax.dynamic_slice_in_dim(values, tp_index * own_rows, own_rows, 0)
@@ -863,11 +921,10 @@
                 ((seq_index - step) % seq_size, moved),
                 (((seq_index ^ 1) - step) % seq_size, crossed(moved, 1)),
             ):
-                if whole is not None:
-                    values = after(values, whole)
                 whole = narrow_into(
                     whole, values, at.astype(jnp.int32).reshape(1), width, member, members, tp_size
                 )
+                tock([whole])
         return whole
 
     spare = jnp.zeros((width, 128 - 2 * heads), LOW)
@@ -885,7 +942,7 @@
         flags = lax.dynamic_index_in_dim(doc_start, micro, 0, keepdims=False) == starts
         return jnp.broadcast_to(flags.astype(F32)[:, None], (rows, 128))
 
-    def mix(residual, step, member, border_carry):
+    def enter_mixer(residual, step, member, border_carry):
         micro = micro_of(step, member)
         hidden, projected = enter(residual, norm_in, in_weight)
         moved = ring(projected[rows - 8 :, :conv_cols], "seq", 1)
@@ -910,19 +967,50 @@
     def rows_outer(name):
         return jnp.concatenate(
             [
-                jnp.where(section == 0, saved[0, member][name], saved[groups, member][name])
+                jnp.where(section == 0, saved[0, member][name], saved[2, member][name])
                 for member in range(group)
             ],
             0,
         )
 
     def rows_inner(name):
-        return jnp.concatenate(
-            [saved[at, member][name] for at in range(1, groups) for member in range(group)], 0
-        )
-
-    def all_rows(name):
+        return jnp.concatenate([saved[1, member][name] for member in range(group)], 0)
+
+    def rows_of(name):
         return jnp.concatenate([rows_outer(name), rows_inner(name)], 0)
+
+    def rounded(values):
+        zero = jnp.zeros((1,), jnp.int32)
+        return tock([narrow_into(None, values, zero, width, 0, 1, tp_size)])[0]
+
+    def enter_mixer(residual, step, member, border_carry):
+        micro = micro_of(step, member)
+        hidden, projected = enter(residual, norm_in, in_weight)
+        moved = ring(projected[rows - 8 :, :conv_cols], "seq", 1)
+        border = jnp.where(at_start, border_carry, moved)
+        resets = reset_flags(micro)
+        carried, local_out, maps, inverse = mixer_local(
+            sizes, projected, resets, border, taps, rate, bias
+        )
+        saved[step, member] = dict(
+            hidden=hidden, border=border, projected=projected, resets=resets, carried=carried,
+            maps=all_seq(maps), inverse=inverse,
+        )
+        return moved, local_out
+
+    def gate(step, member, local_out, state):
+        kept = saved[step, member]
+        kept["gated"], kept["output"], kept["entry_state"], state = mixer_gate(
+            sizes, order, kept["maps"], state, kept["carried"], local_out, kept["projected"], head_norm
+        )
+        return state
+
+    def rows_of(name):
+        outer = [
+            jnp.where(section == 0, saved[0, member][name], saved[2, member][name])
+            for member in range(group)
+        ]
+        return jnp.concatenate(outer + [saved[1, member][name] for member in range(group)], 0)
 
     saved = {}
     section_rows = {}
@@ -936,37 +1024,56 @@
     out_full = None
     border_carry = jnp.zeros((8, conv_cols), F32)
     state = jnp.zeros((heads, key_size, value_size), F32)
-    late_sums = []
+    nothing = jnp.zeros((rows, width), F32)
+    members = list(reversed(range(group)))
+    early, late = members[0], members[-1]
+    tops, feed_grads, late_sums = {}, {}, {}
+
+    def feed(back_step, member, received, handed):
+        step = groups - back_step
+        kept = saved[step, member]
+        given = lax.dynamic_index_in_dim(cotangent, micro_of(step, member), 0, keepdims=False)
+        if step == 0:
+            given = jnp.where(section == 0, given, jnp.zeros_like(given))
+        kept["top_low"], kept["gate_low"], kept["up_low"], sums = feed_back(
+            last_section, given, handed, kept["gate_act"], kept["up_act"],
+            gate_weight, up_weight, down_weight,
+        )
+        tops[member] = jnp.where(section == 0, received, own(given).astype(F32))
+        if step:
+            feed_grads[member] = scatter_tp(sums)
+        else:
+            summed = scatter_tp(jnp.where(section == 0, sums, late_sums[member]))
+            section_rows[groups, member] = saved[groups, member]["mixed"] + summed
+            feed_grads[member] = jnp.where(section == 0, summed, 0.0)
+
     for step in range(groups + 1):
         all_gated = []
-        last = None
         for member in range(group):
-            residual = residuals[member] if last is None else after(residuals[member], last)
-            border_carry, local_out = mix(residual, step, member, border_carry)
-            if step == groups and all_gated:
-                local_out = after(local_out, all_gated[-1])
+            border_carry, local_out = enter_mixer(residuals[member], step, member, border_carry)
             state = gate(step, member, local_out, state)
-            last = saved[step, member]["gated"]
             saved[step, member]["entering"] = entering[member]
-            residuals[member] = residual
-            all_gated.append(lax.all_gather(last, "tp", axis=0))
+            all_gated.append(lax.all_gather(saved[step, member]["gated"], "tp", axis=0))
         if out_full is None:
             for member, piece in enumerate(out_pieces):
-                out_full = whole_out_weight(out_full, after(piece, last), member, 2)
-        next_entering, next_residuals = [], []
+                out_full = whole_out_weight(out_full, after(piece, state), member, 2)
         all_sums = []
         for member in range(group):
             kept = saved[step, member]
             mixed, kept["hidden_feed"], kept["gate_act"], kept["up_act"], kept["inner"], sums = join_heads(
-                residuals[member], after(all_gated[member], last), out_full, norm_feed,
+                residuals[member], all_gated[member], out_full, norm_feed,
                 gate_weight, up_weight, down_weight,
             )
             kept["mixed"] = own(mixed)
-            all_sums.append(scatter_tp(sums) if step < groups else sums)
+            if step < groups:
+                all_sums.append(scatter_tp(sums))
+            else:
+                late_sums[member] = sums
+                feed(0, member, jnp.zeros((own_rows, width), F32), nothing)
         if step == groups:
-            late_sums = all_sums
             break
         ready = None
+        entering, residuals = [], []
         for member in range(group):
             summed = all_sums[member] if ready is None else after(all_sums[member], ready)
             out_rows = saved[step, member]["mixed"] + summed
@@ -975,11 +1082,9 @@
             micro = micro_of(step + 1, member)
             given = lax.dynamic_index_in_dim(inputs, micro, 0, keepdims=False).astype(F32)
             ready = jnp.where(section == 0, given, handed)
-            next_entering.append(ready)
-            next_residuals.append(gather_tp(ready))
-        entering, residuals = next_entering, next_residuals
-
-    nothing = jnp.zeros((rows, width), F32)
+            entering.append(ready)
+            residuals.append(gather_tp(ready))
+
     tail_carry = jnp.zeros((8, conv_cols), F32)
     state_grad = jnp.zeros((heads, key_size, value_size), F32)
     in_grads = {}
@@ -988,90 +1093,91 @@
     gain_grad = jnp.zeros((value_size,), F32)
     taps_grad = jnp.zeros(taps.shape, F32)
     side_sums = jnp.zeros((8, 128), F32)
-    received = [jnp.zeros((own_rows, width), F32)] * group
-    handed = [nothing] * group
-    members = list(reversed(range(group)))
+    received, handed = [None] * group, [None] * group
     for back_step in range(groups + 1):
         step = groups - back_step
-        tops, feed_grads = {}, {}
+        final = back_step == groups
+        if back_step:
+            for member in members:
+                feed(back_step, member, received[member], handed[member])
+        if final:
+            feed_all, top_all = rows_of("hidden_feed"), rows_of("top_low")
+            gate_sums = CoreSums(feed_all, rows_of("gate_low"), 0).send()
+            gate_parts = gate_sums.sums()
+        all_sums = {}
+
+        def depart(member, tail):
+            kept = saved[step, member]
+            kept["projected_low"], sums = leave(
+                kept["conv_grad"], tail, kept["outgate_low"], kept["side_low"], in_weight
+            )
+            all_sums[member] = scatter_tp(sums)
+            return sums
+
+        def mix(member):
+            kept = saved[step, member]
+            feed_part, kept["mixed_grad"], *pieces = mix_back(
+                targets, feed_grads[member], kept["mixed"], tops[member], norm_feed, out_full
+            )
+            return feed_part[0], [ring(piece, "tp", at) if at else piece for at, piece in enumerate(pieces)]
+
         for member in members:
             kept = saved[step, member]
-            given = lax.dynamic_index_in_dim(cotangent, micro_of(step, member), 0, keepdims=False)
-            if step == 0:
-                given = jnp.where(section == 0, given, jnp.zeros_like(given))
-            kept["top_low"], kept["gate_low"], kept["up_low"], sums = feed_back(
-                last_section, given, handed[member], kept["gate_act"], kept["up_act"],
-                gate_weight, up_weight, down_weight,
-            )
-            tops[member] = jnp.where(section == 0, received[member], own(given).astype(F32))
-            if back_step < groups:
-                feed_grads[member] = scatter_tp(sums)
-            else:
-                summed = scatter_tp(jnp.where(section == 0, sums, late_sums[member]))
-                section_rows[groups, member] = saved[groups, member]["mixed"] + summed
-                feed_grads[member] = jnp.where(section == 0, summed, 0.0)
-        if back_step == groups:
-            feed_all, top_all = all_rows("hidden_feed"), all_rows("top_low")
-            gate_parts = core_sums(feed_all, all_rows("gate_low"), 0)
-            feed_grads[members[0]] = after(feed_grads[members[0]], *gate_parts)
-            up_parts = core_sums(feed_all, all_rows("up_low"), 0)
-            feed_grads[members[-1]] = after(feed_grads[members[-1]], *up_parts)
-        last = None
-        all_sums = {}
-        for member in members:
-            kept = saved[step, member]
-            feed_grad = feed_grads[member] if last is None else after(feed_grads[member], conv_grad)
-            feed_part, mixed_grad, *pieces = mix_back(
-                targets, feed_grad, kept["mixed"], tops[member], norm_feed, out_full
-            )
-            kept["mixed_grad"] = mixed_grad
-            norm_feed_grad = norm_feed_grad + feed_part[0]
-            pieces = [ring(piece, "tp", at) if at else piece for at, piece in enumerate(pieces)]
-            if last is not None:
-                pieces[0] = after(pieces[0], last)
-            output_grad, outgate_low, gain_part, entry_grad = mixer_gate_back(
+            feed_part, pieces = mix(member)
+            norm_feed_grad = norm_feed_grad + feed_part
+            if final and member == early:
+                up_sums = CoreSums(feed_all, rows_of("up_low"), 0).send()
+            elif final:
+                inner_mixed = gather_tp(rows_inner("mixed_grad"))
+                outer_mixed = gather_tp(rows_outer("mixed_grad"))
+                pieces[0] = after(pieces[0], *gate_moved)
+            output_grad, kept["outgate_low"], gain_part, entry_grad = mixer_gate_back(
                 sizes, sources, pieces, kept["output"], kept["projected"], head_norm, kept["carried"]
             )
             gain_grad = gain_grad + gain_part[0]
-            conv_grad, border_grad, taps_part, side_low, sums_part, state_grad = mixer_local_back(
-                sizes, order, kept["maps"], all_seq(entry_grad), state_grad, kept["projected"],
+            all_entries = all_seq(entry_grad)
+            if final and member == early:
+                up_parts = up_sums.sums()
+            elif final:
+                down_parts = CoreSums(rows_of("inner"), top_all, 1).send().sums()
+                output_grad = after(output_grad, *up_parts)
+            kept["conv_grad"], border_grad, taps_part, kept["side_low"], sums_part, state_grad = mixer_local_back(
+                sizes, order, kept["maps"], all_entries, state_grad, kept["projected"],
                 kept["resets"], kept["border"], taps, rate, bias, kept["inverse"],
                 kept["entry_state"], output_grad,
             )
             moved = ring(border_grad, "seq", -1)
             tail = jnp.where(at_end, tail_carry, moved)
             tail_carry = moved
-            if back_step == groups and member == members[0]:
-                grad_gate = chip_sums([after(part, tail) for part in gate_parts])
-            elif back_step == groups and member == members[-1]:
-                tail = after(tail, grad_gate, all_sums[members[0]])
+            if final and member == early:
+                gate_moved = chip_moves(after_all(gate_parts, tail))
+            elif final:
+                up_moved = chip_moves(after_all(up_parts, tail))
+                down_moved = chip_moves(after_all(down_parts, tail))
+                tail = after(tail, all_sums[early])
             taps_grad = taps_grad + taps_part
             side_sums = side_sums + sums_part
-            kept["projected_low"], last = leave(conv_grad, tail, outgate_low, side_low, in_weight)
-            all_sums[member] = scatter_tp(last)
-            if back_step == groups and member == members[0]:
-                inner_mixed = gather_tp(after(rows_inner("mixed_grad"), last))
+            last = depart(member, tail)
         ready = None
         received, handed = [None] * group, [None] * group
-        if back_step == groups:
-            outer_mixed = gather_tp(after(rows_outer("mixed_grad"), last))
-            in_parts = core_sums(all_rows("hidden"), all_rows("projected_low"), 0)
-            down_parts = core_sums(after(all_rows("inner"), in_parts[0]), top_all, 1)
-            grad_up = chip_sums([after(part, tail) for part in up_parts])
-            inner_mixed = narrow_into(
-                None, after(inner_mixed, grad_up, down_parts[0]), jnp.zeros((1,), jnp.int32), width, 0, 1, tp_size
-            )
-            ready = inner_mixed
+        if final:
+            in_sums = CoreSums(rows_of("hidden"), rows_of("projected_low"), 0).send()
+            in_sums.left = after(in_sums.left, *up_moved)
+            in_parts = in_sums.sums()
+            in_moved = chip_moves(in_parts)
+            inner_mixed = rounded(inner_mixed)
+            outer_mixed = rounded(outer_mixed)
+            ready = outer_mixed
         for member in members:
             kept = saved[step, member]
             summed = all_sums[member]
-            if ready is not None and (back_step < groups or member == members[-1]):
+            if ready is not None and (not final or member == late):
                 summed = after(summed, ready)
             entering_back, in_part = row_norm_back(kept["entering"], norm_in[0], summed)
             norm_in_grad = norm_in_grad + in_part
             own_grad = kept["mixed_grad"] + entering_back
             in_grads[step, member] = own_grad
-            if back_step < groups:
+            if not final:
                 ready = handed_on(own_grad, "section", -1)
                 received[member] = ready
                 handed[member] = gather_tp(ready)
@@ -1082,23 +1188,24 @@
             for member in range(group)
         ]
 
-    grad_in = chip_sums([after(part, tail) for part in in_parts])
-    grad_down = chip_sums([after(part, tail) for part in down_parts])
-    outer_mixed = after(outer_mixed, grad_in)
-    zero = jnp.zeros((1,), jnp.int32)
-
-    def by_device(name, rows_of, count):
-        split = rows_of(name).astype(LOW).reshape(count, tp_size, own_rows, value_cols)
-        return jnp.moveaxis(split, 0, 1).reshape(count * rows, value_cols)
-
-    mixed_all = jnp.concatenate(
-        [narrow_into(None, outer_mixed, zero, width, 0, 1, tp_size), inner_mixed], 0
-    )
-    gated_all = jnp.concatenate(
-        [by_device("gated", rows_outer, group), by_device("gated", rows_inner, micros - group)], 0
-    )
-    out_parts = core_sums(gated_all, mixed_all, 1)
-    grad_out = chip_sums(out_parts)
+    def by_device(values):
+        split = values.astype(LOW).reshape(-1, tp_size, own_rows, value_cols)
+        return jnp.moveaxis(split, 0, 1).reshape(-1, value_cols)
+
+    out_sums = CoreSums(
+        jnp.concatenate([by_device(rows_outer("gated")), by_device(rows_inner("gated"))], 0),
+        jnp.concatenate([outer_mixed, inner_mixed], 0),
+        1,
+    )
+    out_parts = out_sums.send().sums()
+    grad_out = total(out_parts, chip_moves(after_all(out_parts, *down_moved)))
+    grad_gate, grad_up, grad_in, grad_down = [
+        total(after_all(parts, out_parts[-1]), moved)
+        for parts, moved in (
+            (gate_parts, gate_moved), (up_parts, up_moved), (in_parts, in_moved),
+            (down_parts, down_moved),
+        )
+    ]
 
     shared = butterfly(jnp.concatenate([norm_in_grad, norm_feed_grad, gain_grad]), "tp")
     small = butterfly(

time: 2090 us -> 2050 us (0.981)
    ppermute x73, waiting for transfers between devices: 485 us -> 403 us  [ring(): lax.ppermute(value, axis, [(at, (at + steps) % count) for at in range(cou...]
    reduce_scatter x16, waiting for transfers between devices: 214 us -> 289 us  [scatter_tp(): return lax.psum_scatter(values, 'tp', scatter_dimension=0, tiled=True)]
    all_gather x6, waiting for transfers between devices: 98 us -> 44.8 us  [local(): all_gated.append(lax.all_gather(saved[step, member]['gated'], 'tp', axis=0))]
    ppermute x4, waiting for transfers between devices: 18.3 us -> 49.3 us  [butterfly(): lax.ppermute(value, axis, [(at, at ^ step) for at in range(count)])]
    unnamed x751 -> x845, local copies, waits for them, and re-layouts: 101 us -> 108 us
  transfers between devices with their start and end apart: 135 -> 135, of which waited for: 92 -> 95; matrix products, arithmetic and copies ran while one was open for 10% -> 10% of each run, Pallas kernels for 20% -> 20%
where the time goes in v3:
time: 2050 us; the launch traced here: 2030 us
  waiting for transfers between devices  1150 us (56%)
  Pallas kernels  433 us (21%)
  local copies, waits for them, and re-layouts  139 us (7%)
  starting transfers between devices  116 us (6%)
  other arithmetic  104 us (5%)
  matrix products  74.7 us (4%)
    ppermute x73, waiting for transfers between devices, ring(): lax.ppermute(value, axis, [(at, (at + steps) % count) for at in range(cou...  403 us
    pallas_call x54, Pallas kernels, call(): pl.pallas_call(kernel, grid=(1,), in_specs=specs, out_specs=[whole(array)...  393 us
    reduce_scatter x16, waiting for transfers between devices, scatter_tp(): return lax.psum_scatter(values, 'tp', scatter_dimension=0, tiled=True)  289 us
    all_gather x14, waiting for transfers between devices, gather_tp(): return lax.all_gather(values, 'tp', axis=0, tiled=True)  257 us
    unnamed x845, local copies, waits for them, and re-layouts  108 us
    ppermute x8, waiting for transfers between devices, handed_on(): lax.ppermute(value, axis, [(at, at + steps) for at in range(first, last)])  102 us
    ppermute x73, starting transfers between devices, ring(): lax.ppermute(value, axis, [(at, (at + steps) % count) for at in range(cou...  85.6 us
    dot_general x20, matrix products, low_dot(): lax.dot_general(a, b, (contract, ((), ())), preferred_element_type=F32)  74.7 us
  transfers between devices with their start and end apart: 135, of which 95 were waited for; matrix products, arithmetic and copies ran while one was open for 10% of the time, Pallas kernels for 20%

profile of v3, /device:TPU:0, one launch (start us, length us, event | category | flops | bytes accessed | tf_op | source)
XLA Modules:
  0.0 2034.2 jit_solution(8785410622208189011)
XLA Ops:
  29.2 29.5 %all-gather.53.cloned.1.call-done = f32[1,256,2048]{2,1,0:T(8,128)} async-done(((f32[1,64,2048]{2,1,0:T(8,128)}), f32[1,256,2048]{2,1,0:T(8,128)}) %all-gather.53.cloned.1.call-update) | async-done | bytes 2097168 | tf_op jit(solution)/shard_map/all_gather | solution.py:817
  154.4 44.8 %all-gather.31.cloned.1.call-done.source_ref = f32[1024,512]{1,0:T(8,128)} async-done(((f32[256,512]{1,0:T(8,128)}), f32[1024,512]{1,0:T(8,128)}) %all-gather.31.cloned.1.call-update) | async-done | bytes 2097168 | tf_op jit(solution)/shard_map/all_gather | solution.py:817
  201.8 45.1 %collective-permute-done.12.source_ref = f32[1024,512]{1,0:T(8,128)} collective-permute-done((f32[1024,512]{1,0:T(8,128)}, f32[1024,512]{1,0:T(8,128)}, u32[]{:S(2)}, u32[]{:S(2)}) %collective-permute-start.12) | collective-permute-done | bytes 2097184 | tf_op jit(solution)/shard_map/ppermute | solution.py:803
  276.1 14.5 join_heads.6
  292.6 14.7 join_heads.7
  307.4 30.7 %reduce-scatter.17.cloned.1.call-done = f32[64,2048]{1,0:T(8,128)} async-done(((f32[256,2048]{1,0:T(8,128)}), f32[64,2048]{1,0:T(8,128)}) %reduce-scatter.17.cloned.1.call-update) | async-done | bytes 524304 | tf_op jit(solution)/shard_map/reduce_scatter | solution.py:821
  356.0 28.2 %reduce-scatter.19.cloned.1.call-done = f32[64,2048]{1,0:T(8,128)} async-done(((f32[256,2048]{1,0:T(8,128)}), f32[64,2048]{1,0:T(8,128)}) %reduce-scatter.19.cloned.1.call-update) | async-done | bytes 524304 | tf_op jit(solution)/shard_map/reduce_scatter | solution.py:821
  402.5 28.6 %all-gather.33.cloned.1.call-done.rows_ref = f32[256,2048]{1,0:T(8,128)} async-done(((f32[64,2048]{1,0:T(8,128)}), f32[256,2048]{1,0:T(8,128)}) %all-gather.33.cloned.1.call-update) | async-done | bytes 2097168 | tf_op jit(solution)/shard_map/all_gather | solution.py:817
  523.4 14.9 join_heads.8
  538.4 31.2 %all-gather.63.cloned.1.call-done = f32[1024,512]{1,0:T(8,128)} async-done(((f32[256,512]{1,0:T(8,128)}), f32[1024,512]{1,0:T(8,128)}) %all-gather.63.cloned.1.call-update) | async-done | bytes 2097168 | tf_op jit(solution)/shard_map/all_gather | solution.py:1056
  569.5 14.7 join_heads.9
  584.3 30.7 %reduce-scatter.21.cloned.1.call-done = f32[64,2048]{1,0:T(8,128)} async-done(((f32[256,2048]{1,0:T(8,128)}), f32[64,2048]{1,0:T(8,128)}) %reduce-scatter.21.cloned.1.call-update) | async-done | bytes 524304 | tf_op jit(solution)/shard_map/reduce_scatter | solution.py:821
  635.3 25.8 %reduce-scatter.23.cloned.1.call-done = f32[64,2048]{1,0:T(8,128)} async-done(((f32[256,2048]{1,0:T(8,128)}), f32[64,2048]{1,0:T(8,128)}) %reduce-scatter.23.cloned.1.call-update) | async-done | bytes 524304 | tf_op jit(solution)/shard_map/reduce_scatter | solution.py:821
  681.1 26.7 %all-gather.37.cloned.1.call-done.rows_ref = f32[256,2048]{1,0:T(8,128)} async-done(((f32[64,2048]{1,0:T(8,128)}), f32[256,2048]{1,0:T(8,128)}) %all-gather.37.cloned.1.call-update) | async-done | bytes 2097168 | tf_op jit(solution)/shard_map/all_gather | solution.py:817
  803.3 15.0 join_heads.10
  846.1 14.7 join_heads.11
  883.5 37.0 %reduce-scatter.27.cloned.1.call-done.grad_ref = f32[64,2048]{1,0:T(8,128)} async-done(((f32[256,2048]{1,0:T(8,128)}), f32[64,2048]{1,0:T(8,128)}) %reduce-scatter.27.cloned.1.call-update) | async-done | bytes 524304 | tf_op jit(solution)/shard_map/reduce_scatter | solution.py:821
  1078.1 15.0 collective-permute-done.48
  1093.1 32.0 %reduce-scatter.29.cloned.1.call-done = f32[64,2048]{1,0:T(8,128)} async-done(((f32[256,2048]{1,0:T(8,128)}), f32[64,2048]{1,0:T(8,128)}) %reduce-scatter.29.cloned.1.call-update) | async-done | bytes 524304 | tf_op jit(solution)/shard_map/reduce_scatter | solution.py:821
  1145.3 26.6 %all-gather.43.cloned.1.call-done.handed_ref = f32[256,2048]{1,0:T(8,128)} async-done(((f32[64,2048]{1,0:T(8,128)}), f32[256,2048]{1,0:T(8,128)}) %all-gather.43.cloned.1.call-update) | async-done | bytes 2097168 | tf_op jit(solution)/shard_map/all_gather | solution.py:817
  1190.7 27.4 %all-gather.41.cloned.1.call-done.handed_ref = f32[256,2048]{1,0:T(8,128)} async-done(((f32[64,2048]{1,0:T(8,128)}), f32[256,2048]{1,0:T(8,128)}) %all-gather.41.cloned.1.call-update) | async-done | bytes 2097168 | tf_op jit(solution)/shard_map/all_gather | solution.py:817
  1239.3 24.2 %reduce-scatter.35.cloned.1.call-done.grad_ref = f32[64,2048]{1,0:T(8,128)} async-done(((f32[256,2048]{1,0:T(8,128)}), f32[64,2048]{1,0:T(8,128)}) %reduce-scatter.35.cloned.1.call-update) | async-done | bytes 524304 | tf_op jit(solution)/shard_map/reduce_scatter | solution.py:821
  1408.0 15.3 collective-permute-done.64
  1424.2 30.5 %reduce-scatter.37.cloned.1.call-done = f32[64,2048]{1,0:T(8,128)} async-done(((f32[256,2048]{1,0:T(8,128)}), f32[64,2048]{1,0:T(8,128)}) %reduce-scatter.37.cloned.1.call-update) | async-done | bytes 524304 | tf_op jit(solution)/shard_map/reduce_scatter | solution.py:821
  1480.6 21.0 %all-gather.47.cloned.1.call-done.handed_ref = f32[256,2048]{1,0:T(8,128)} async-done(((f32[64,2048]{1,0:T(8,128)}), f32[256,2048]{1,0:T(8,128)}) %all-gather.47.cloned.1.call-update) | async-done | bytes 2097168 | tf_op jit(solution)/shard_map/all_gather | solution.py:817
  1522.4 25.3 %all-gather.45.cloned.1.call-done.handed_ref = f32[256,2048]{1,0:T(8,128)} async-done(((f32[64,2048]{1,0:T(8,128)}), f32[256,2048]{1,0:T(8,128)}) %all-gather.45.cloned.1.call-update) | async-done | bytes 2097168 | tf_op jit(solution)/shard_map/all_gather | solution.py:817
  1577.4 15.8 reduce-scatter.43.cloned.1.call-done
  1704.3 36.5 %collective-permute-done.77 = f32[512,1408]{1,0:T(8,128)} collective-permute-done((f32[512,1408]{1,0:T(8,128)}, f32[512,1408]{1,0:T(8,128)}, u32[]{:S(2)}, u32[]{:S(2)}) %collective-permute-start.77) | collective-permute-done | bytes 2883616 | tf_op jit(solution)/shard_map/ppermute | solution.py:803
  1805.4 53.0 %collective-permute-done.87 = f32[512,1408]{1,0:T(8,128)} collective-permute-done((f32[512,1408]{1,0:T(8,128)}, f32[512,1408]{1,0:T(8,128)}, u32[]{:S(2)}, u32[]{:S(2)}) %collective-permute-start.87) | collective-permute-done | bytes 2883616 | tf_op jit(solution)/shard_map/ppermute | solution.py:803
  1873.9 21.1 %all-gather.51.cloned.1.call-done.source_ref = f32[512,2048]{1,0:T(8,128)} async-done(((f32[128,2048]{1,0:T(8,128)}), f32[512,2048]{1,0:T(8,128)}) %all-gather.51.cloned.1.call-update) | async-done | bytes 4194320 | tf_op jit(solution)/shard_map/all_gather | solution.py:817
  1906.5 33.7 %reduce-scatter.47.cloned.1.call-done = f32[64,2048]{1,0:T(8,128)} async-done(((f32[256,2048]{1,0:T(8,128)}), f32[64,2048]{1,0:T(8,128)}) %reduce-scatter.47.cloned.1.call-update) | async-done | bytes 524304 | tf_op jit(solution)/shard_map/reduce_scatter | solution.py:821
  1969.6 45.9 %collective-permute-done.94 = f32[8452]{0:T(1024)S(1)} collective-permute-done((f32[8452]{0:T(1024)S(1)}, f32[8452]{0:T(1024)S(1)}, u32[]{:S(2)}, u32[]{:S(2)}) %collective-permute-start.94) | collective-permute-done | bytes 33840 | tf_op jit(solution)/shard_map/ppermute | solution.py:832
  (1349 shorter events, 1144.7 us)
Async XLA Ops:
  10.3 143.6 %all-gather.29.cloned.1.call-start = ((), (), s32[]{:S(2)}) async-start(), calls=%async_computation.16 | async-start | bytes 2621440 | tf_op jit(solution)/shard_map/all_gather | solution.py:817
  15.6 183.6 %all-gather.31.cloned.1.call-start = ((), (), s32[]{:S(2)}) async-start(), calls=%async_computation.17 | async-start | bytes 2621440 | tf_op jit(solution)/shard_map/all_gather | solution.py:817
  16.1 260.0 %all-gather.55.cloned.1.call-start = ((), (), s32[]{:S(2)}) async-start(), calls=%async_computation.45 | async-start | bytes 2621440 | tf_op jit(solution)/shard_map/all_gather | solution.py:1056
  102.9 189.7 %all-gather.59.cloned.1.call-start = ((), (), s32[]{:S(2)}) async-start(), calls=%async_computation.47 | async-start | bytes 2621440 | tf_op jit(solution)/shard_map/all_gather | solution.py:1056
  200.7 137.4 %reduce-scatter.17.cloned.1.call-start = ((), (), s32[]{:S(2)}) async-start(), calls=%async_computation.18 | async-start | bytes 2621440 | tf_op jit(solution)/shard_map/reduce_scatter | solution.py:821
  307.3 123.8 %all-gather.33.cloned.1.call-start = ((), (), s32[]{:S(2)}) async-start(), calls=%async_computation.19 | async-start | bytes 2621440 | tf_op jit(solution)/shard_map/all_gather | solution.py:817
  356.0 121.2 %all-gather.35.cloned.1.call-start = ((), (), s32[]{:S(2)}) async-start(), calls=%async_computation.21 | async-start | bytes 2621440 | tf_op jit(solution)/shard_map/all_gather | solution.py:817
  402.4 121.0 %all-gather.61.cloned.1.call-start = ((), (), s32[]{:S(2)}) async-start(), calls=%async_computation.48 | async-start | bytes 2621440 | tf_op jit(solution)/shard_map/all_gather | solution.py:1056
  538.3 122.7 %reduce-scatter.23.cloned.1.call-start = ((), (), s32[]{:S(2)}) async-start(), calls=%async_computation.23 | async-start | bytes 2621440 | tf_op jit(solution)/shard_map/reduce_scatter | solution.py:821
  584.3 123.5 %all-gather.37.cloned.1.call-start = ((), (), s32[]{:S(2)}) async-start(), calls=%async_computation.24 | async-start | bytes 2621440 | tf_op jit(solution)/shard_map/all_gather | solution.py:817
  635.2 118.7 %all-gather.39.cloned.1.call-start = ((), (), s32[]{:S(2)}) async-start(), calls=%async_computation.25 | async-start | bytes 2621440 | tf_op jit(solution)/shard_map/all_gather | solution.py:817
  681.0 122.3 %all-gather.65.cloned.1.call-start = ((), (), s32[]{:S(2)}) async-start(), calls=%async_computation.50 | async-start | bytes 2621440 | tf_op jit(solution)/shard_map/all_gather | solution.py:1056
  797.6 122.9 %reduce-scatter.27.cloned.1.call-start = ((), (), s32[]{:S(2)}) async-start(), calls=%async_computation.27 | async-start | bytes 2621440 | tf_op jit(solution)/shard_map/reduce_scatter | solution.py:821
  877.7 117.5 %reduce-scatter.25.cloned.1.call-start = ((), (), s32[]{:S(2)}) async-start(), calls=%async_computation.26 | async-start | bytes 2621440 | tf_op jit(solution)/shard_map/reduce_scatter | solution.py:821
  878.3 194.2 %reduce-scatter.31.cloned.1.call-start = ((), (), s32[]{:S(2)}) async-start(), calls=%async_computation.29 | async-start | bytes 2621440 | tf_op jit(solution)/shard_map/reduce_scatter | solution.py:821
  993.3 131.8 %reduce-scatter.29.cloned.1.call-start = ((), (), s32[]{:S(2)}) async-start(), calls=%async_computation.28 | async-start | bytes 2621440 | tf_op jit(solution)/shard_map/reduce_scatter | solution.py:821
  1072.4 99.6 %all-gather.43.cloned.1.call-start = ((), (), s32[]{:S(2)}) async-start(), calls=%async_computation.31 | async-start | bytes 2621440 | tf_op jit(solution)/shard_map/all_gather | solution.py:817
  1093.1 125.0 %all-gather.41.cloned.1.call-start = ((), (), s32[]{:S(2)}) async-start(), calls=%async_computation.30 | async-start | bytes 2621440 | tf_op jit(solution)/shard_map/all_gather | solution.py:817
  1144.9 118.7 %reduce-scatter.35.cloned.1.call-start = ((), (), s32[]{:S(2)}) async-start(), calls=%async_computation.33 | async-start | bytes 2621440 | tf_op jit(solution)/shard_map/reduce_scatter | solution.py:821
  1190.6 138.2 %reduce-scatter.33.cloned.1.call-start = ((), (), s32[]{:S(2)}) async-start(), calls=%async_computation.32 | async-start | bytes 2621440 | tf_op jit(solution)/shard_map/reduce_scatter | solution.py:821
  1236.6 165.1 %reduce-scatter.39.cloned.1.call-start = ((), (), s32[]{:S(2)}) async-start(), calls=%async_computation.35 | async-start | bytes 2621440 | tf_op jit(solution)/shard_map/reduce_scatter | solution.py:821
  1328.7 126.0 %reduce-scatter.37.cloned.1.call-start = ((), (), s32[]{:S(2)}) async-start(), calls=%async_computation.34 | async-start | bytes 2621440 | tf_op jit(solution)/shard_map/reduce_scatter | solution.py:821
  1401.6 100.0 %all-gather.47.cloned.1.call-start = ((), (), s32[]{:S(2)}) async-start(), calls=%async_computation.37 | async-start | bytes 2621440 | tf_op jit(solution)/shard_map/all_gather | solution.py:817
  1424.1 123.6 %all-gather.45.cloned.1.call-start = ((), (), s32[]{:S(2)}) async-start(), calls=%async_computation.36 | async-start | bytes 2621440 | tf_op jit(solution)/shard_map/all_gather | solution.py:817
  1474.8 118.4 %reduce-scatter.43.cloned.1.call-start = ((), (), s32[]{:S(2)}) async-start(), calls=%async_computation.39 | async-start | bytes 2621440 | tf_op jit(solution)/shard_map/reduce_scatter | solution.py:821
  1522.2 160.6 %reduce-scatter.41.cloned.1.call-start = ((), (), s32[]{:S(2)}) async-start(), calls=%async_computation.38 | async-start | bytes 2621440 | tf_op jit(solution)/shard_map/reduce_scatter | solution.py:821
  1607.1 174.8 %reduce-scatter.45.cloned.1.call-start = ((), (), s32[]{:S(2)}) async-start(), calls=%async_computation.40 | async-start | bytes 2621440 | tf_op jit(solution)/shard_map/reduce_scatter | solution.py:821
  1666.8 202.9 %all-gather.49.cloned.1.call-start = ((), (), s32[]{:S(2)}) async-start(), calls=%async_computation.42 | async-start | bytes 5242880 | tf_op jit(solution)/shard_map/all_gather | solution.py:817
  1667.9 227.0 %all-gather.51.cloned.1.call-start = ((), (), s32[]{:S(2)}) async-start(), calls=%async_computation.43 | async-start | bytes 5242880 | tf_op jit(solution)/shard_map/all_gather | solution.py:817
  1750.6 189.6 %reduce-scatter.47.cloned.1.call-start = ((), (), s32[]{:S(2)}) async-start(), calls=%async_computation.41 | async-start | bytes 2621440 | tf_op jit(solution)/shard_map/reduce_scatter | solution.py:821
  1804.6 158.8 %collective-permute-start.97 = (f32[1408,512]{1,0:T(8,128)}, f32[1408,512]{1,0:T(8,128)}, u32[]{:S(2)}, u32[]{:S(2)}) collective-permute-start(f32[1408,512]{1,0:T(8,128)} %convolution_add_fusion.1), channel_id=1, source_target_pairs={{0,8},{4,12},{8,0},{12,4},{1,9},{5,13},{9,1},{13,5},{2,10},{6,14},... | collective-permute-start | bytes 8650760 | tf_op jit(solution)/shard_map/ppermute | solution.py:803
  1905.0 114.6 %collective-permute-start.96 = (f32[512,1664]{1,0:T(8,128)}, f32[512,1664]{1,0:T(8,128)}, u32[]{:S(2)}, u32[]{:S(2)}) collective-permute-start(f32[512,1664]{1,0:T(8,128)} %convolution_add_fusion.7), channel_id=1, source_target_pairs={{0,8},{4,12},{8,0},{12,4},{1,9},{5,13},{9,1},{13,5},{2,10},{6,14},... | collective-permute-start | bytes 10223624 | tf_op jit(solution)/shard_map/ppermute | solution.py:803
  (523 other events, 10526.2 us)
Sparse Core Ops, SparseCore 0:
  10.2 48.5 all-gather.52
  60.9 44.7 all-gather.56
  107.8 44.6 all-gather.28
  154.5 44.6 all-gather.30
  201.2 44.6 all-gather.54
  247.9 44.6 all-gather.58
  341.0 43.1 reduce-scatter.18
  385.8 45.2 all-gather.32
  432.5 44.6 all-gather.34
  478.8 44.5 all-gather.60
  524.8 44.6 all-gather.62
  572.4 42.6 reduce-scatter.20
  617.9 43.1 reduce-scatter.22
  662.5 45.2 all-gather.36
  709.2 44.6 all-gather.38
  755.3 44.6 all-gather.64
  801.5 44.5 all-gather.66
  923.2 51.5 reduce-scatter.24
  993.4 62.4 reduce-scatter.30
  1072.5 52.5 reduce-scatter.28
  1126.7 45.2 all-gather.42
  1173.4 44.6 all-gather.40
  1220.9 42.5 reduce-scatter.34
  1266.4 51.4 reduce-scatter.32
  1328.8 61.5 reduce-scatter.38
  1401.7 52.9 reduce-scatter.36
  1456.3 45.2 all-gather.46
  1503.0 44.6 all-gather.44
  1607.2 51.6 reduce-scatter.40
  1666.9 63.1 reduce-scatter.44
  1731.8 81.6 all-gather.48
  1815.6 79.2 all-gather.50
  (4 shorter events, 169.9 us)

commit v4 on v3

--- a/solution.py
+++ b/solution.py
@@ -856,11 +856,13 @@
         self.received = [crossed(self.product(at, 1 - self.core), 1) for at in self.order]
         return self
 
-    def sums(self):
-        return [
-            tock([self.product(at, self.core) + part])[0]
-            for at, part in zip(self.order, self.received)
-        ]
+    def sums(self, *others):
+        sums = []
+        for at, part in zip(self.order, self.received):
+            if len(sums) == len(self.order) - 1 and others:
+                self.left = after(self.left, *others)
+            sums.append(tock([self.product(at, self.core) + part])[0])
+        return sums
 
 
 def chip_moves(parts):
@@ -1104,6 +1106,7 @@
             feed_all, top_all = rows_of("hidden_feed"), rows_of("top_low")
             gate_sums = CoreSums(feed_all, rows_of("gate_low"), 0).send()
             gate_parts = gate_sums.sums()
+            gate_moved = chip_moves(gate_parts)
         all_sums = {}
 
         def depart(member, tail):
@@ -1130,17 +1133,18 @@
             elif final:
                 inner_mixed = gather_tp(rows_inner("mixed_grad"))
                 outer_mixed = gather_tp(rows_outer("mixed_grad"))
-                pieces[0] = after(pieces[0], *gate_moved)
             output_grad, kept["outgate_low"], gain_part, entry_grad = mixer_gate_back(
                 sizes, sources, pieces, kept["output"], kept["projected"], head_norm, kept["carried"]
             )
             gain_grad = gain_grad + gain_part[0]
             all_entries = all_seq(entry_grad)
             if final and member == early:
+                up_sums.left = after(up_sums.left, *gate_moved)
                 up_parts = up_sums.sums()
             elif final:
-                down_parts = CoreSums(rows_of("inner"), top_all, 1).send().sums()
-                output_grad = after(output_grad, *up_parts)
+                down_sums = CoreSums(after(rows_of("inner"), *up_moved), top_all, 1).send()
+                down_parts = down_sums.sums()
+                inner_mixed = rounded(inner_mixed)
             kept["conv_grad"], border_grad, taps_part, kept["side_low"], sums_part, state_grad = mixer_local_back(
                 sizes, order, kept["maps"], all_entries, state_grad, kept["projected"],
                 kept["resets"], kept["border"], taps, rate, bias, kept["inverse"],
@@ -1150,9 +1154,8 @@
             tail = jnp.where(at_end, tail_carry, moved)
             tail_carry = moved
             if final and member == early:
-                gate_moved = chip_moves(after_all(gate_parts, tail))
+                up_moved = chip_moves(after_all(up_parts, tail))
             elif final:
-                up_moved = chip_moves(after_all(up_parts, tail))
                 down_moved = chip_moves(after_all(down_parts, tail))
                 tail = after(tail, all_sums[early])
             taps_grad = taps_grad + taps_part
@@ -1162,11 +1165,9 @@
         received, handed = [None] * group, [None] * group
         if final:
             in_sums = CoreSums(rows_of("hidden"), rows_of("projected_low"), 0).send()
-            in_sums.left = after(in_sums.left, *up_moved)
-            in_parts = in_sums.sums()
+            in_parts = in_sums.sums(*down_moved)
             in_moved = chip_moves(in_parts)
-            inner_mixed = rounded(inner_mixed)
-            outer_mixed = rounded(outer_mixed)
+            outer_mixed = rounded(after(outer_mixed, *in_moved))
             ready = outer_mixed
         for member in members:
             kept = saved[step, member]
@@ -1198,7 +1199,7 @@
         1,
     )
     out_parts = out_sums.send().sums()
-    grad_out = total(out_parts, chip_moves(after_all(out_parts, *down_moved)))
+    grad_out = total(out_parts, chip_moves(out_parts))
     grad_gate, grad_up, grad_in, grad_down = [
         total(after_all(parts, out_parts[-1]), moved)
         for parts, moved in (

time: 2050 us -> 2020 us (0.985)
  waiting for transfers between devices: 1150 us -> 1100 us
    ppermute x73, waiting for transfers between devices: 403 us -> 471 us  [ring(): lax.ppermute(value, axis, [(at, (at + steps) % count) for at in range(cou...]
    reduce_scatter x16, waiting for transfers between devices: 289 us -> 242 us  [scatter_tp(): return lax.psum_scatter(values, 'tp', scatter_dimension=0, tiled=True)]
    ppermute x4, waiting for transfers between devices: 49.3 us -> 5.41 us  [butterfly(): lax.ppermute(value, axis, [(at, at ^ step) for at in range(count)])]
    all_gather x14, waiting for transfers between devices: 257 us -> 231 us  [gather_tp(): return lax.all_gather(values, 'tp', axis=0, tiled=True)]
    unnamed x845 -> x855, local copies, waits for them, and re-layouts: 108 us -> 121 us
  transfers between devices with their start and end apart: 135 -> 135, of which waited for: 95 -> 97; matrix products, arithmetic and copies ran while one was open for 10% -> 11% of each run, Pallas kernels for 20% -> 20%
where the time goes in v4:
time: 2020 us; the launch traced here: 2000 us
  waiting for transfers between devices  1100 us (54%)
  Pallas kernels  434 us (21%)
  local copies, waits for them, and re-layouts  155 us (8%)
  starting transfers between devices  107 us (5%)
  other arithmetic  105 us (5%)
  matrix products  84.2 us (4%)
    ppermute x73, waiting for transfers between devices, ring(): lax.ppermute(value, axis, [(at, (at + steps) % count) for at in range(cou...  471 us
    pallas_call x54, Pallas kernels, call(): pl.pallas_call(kernel, grid=(1,), in_specs=specs, out_specs=[whole(array)...  394 us
    reduce_scatter x16, waiting for transfers between devices, scatter_tp(): return lax.psum_scatter(values, 'tp', scatter_dimension=0, tiled=True)  242 us
    all_gather x14, waiting for transfers between devices, gather_tp(): return lax.all_gather(values, 'tp', axis=0, tiled=True)  231 us
    unnamed x855, local copies, waits for them, and re-layouts  121 us
    ppermute x8, waiting for transfers between devices, handed_on(): lax.ppermute(value, axis, [(at, at + steps) for at in range(first, last)])  102 us
    dot_general x20, matrix products, low_dot(): lax.dot_general(a, b, (contract, ((), ())), preferred_element_type=F32)  84.2 us
    ppermute x73, starting transfers between devices, ring(): lax.ppermute(value, axis, [(at, (at + steps) % count) for at in range(cou...  76.2 us
  transfers between devices with their start and end apart: 135, of which 97 were waited for; matrix products, arithmetic and copies ran while one was open for 11% of the time, Pallas kernels for 20%

profile of v4, /device:TPU:0, one launch (start us, length us, event | category | flops | bytes accessed | tf_op | source)
XLA Modules:
  0.0 2004.7 jit_solution(12415698915224894821)
XLA Ops:
  29.2 29.5 %all-gather.53.cloned.1.call-done = f32[1,256,2048]{2,1,0:T(8,128)} async-done(((f32[1,64,2048]{2,1,0:T(8,128)}), f32[1,256,2048]{2,1,0:T(8,128)}) %all-gather.53.cloned.1.call-update) | async-done | bytes 2097168 | tf_op jit(solution)/shard_map/all_gather | solution.py:817
  154.6 44.6 %all-gather.31.cloned.1.call-done.source_ref = f32[1024,512]{1,0:T(8,128)} async-done(((f32[256,512]{1,0:T(8,128)}), f32[1024,512]{1,0:T(8,128)}) %all-gather.31.cloned.1.call-update) | async-done | bytes 2097168 | tf_op jit(solution)/shard_map/all_gather | solution.py:817
  201.9 44.9 %collective-permute-done.12.source_ref = f32[1024,512]{1,0:T(8,128)} collective-permute-done((f32[1024,512]{1,0:T(8,128)}, f32[1024,512]{1,0:T(8,128)}, u32[]{:S(2)}, u32[]{:S(2)}) %collective-permute-start.12) | collective-permute-done | bytes 2097184 | tf_op jit(solution)/shard_map/ppermute | solution.py:803
  276.1 14.5 join_heads.6
  292.6 14.7 join_heads.7
  307.4 30.7 %reduce-scatter.17.cloned.1.call-done = f32[64,2048]{1,0:T(8,128)} async-done(((f32[256,2048]{1,0:T(8,128)}), f32[64,2048]{1,0:T(8,128)}) %reduce-scatter.17.cloned.1.call-update) | async-done | bytes 524304 | tf_op jit(solution)/shard_map/reduce_scatter | solution.py:821
  356.2 28.1 %reduce-scatter.19.cloned.1.call-done = f32[64,2048]{1,0:T(8,128)} async-done(((f32[256,2048]{1,0:T(8,128)}), f32[64,2048]{1,0:T(8,128)}) %reduce-scatter.19.cloned.1.call-update) | async-done | bytes 524304 | tf_op jit(solution)/shard_map/reduce_scatter | solution.py:821
  402.4 28.7 %all-gather.33.cloned.1.call-done.rows_ref = f32[256,2048]{1,0:T(8,128)} async-done(((f32[64,2048]{1,0:T(8,128)}), f32[256,2048]{1,0:T(8,128)}) %all-gather.33.cloned.1.call-update) | async-done | bytes 2097168 | tf_op jit(solution)/shard_map/all_gather | solution.py:817
  523.5 14.8 join_heads.8
  538.4 31.2 %all-gather.63.cloned.1.call-done = f32[1024,512]{1,0:T(8,128)} async-done(((f32[256,512]{1,0:T(8,128)}), f32[1024,512]{1,0:T(8,128)}) %all-gather.63.cloned.1.call-update) | async-done | bytes 2097168 | tf_op jit(solution)/shard_map/all_gather | solution.py:1058
  569.6 14.7 join_heads.9
  584.4 30.7 %reduce-scatter.21.cloned.1.call-done = f32[64,2048]{1,0:T(8,128)} async-done(((f32[256,2048]{1,0:T(8,128)}), f32[64,2048]{1,0:T(8,128)}) %reduce-scatter.21.cloned.1.call-update) | async-done | bytes 524304 | tf_op jit(solution)/shard_map/reduce_scatter | solution.py:821
  635.2 25.8 %reduce-scatter.23.cloned.1.call-done = f32[64,2048]{1,0:T(8,128)} async-done(((f32[256,2048]{1,0:T(8,128)}), f32[64,2048]{1,0:T(8,128)}) %reduce-scatter.23.cloned.1.call-update) | async-done | bytes 524304 | tf_op jit(solution)/shard_map/reduce_scatter | solution.py:821
  681.0 26.7 %all-gather.37.cloned.1.call-done.rows_ref = f32[256,2048]{1,0:T(8,128)} async-done(((f32[64,2048]{1,0:T(8,128)}), f32[256,2048]{1,0:T(8,128)}) %all-gather.37.cloned.1.call-update) | async-done | bytes 2097168 | tf_op jit(solution)/shard_map/all_gather | solution.py:817
  803.4 14.9 join_heads.10
  846.1 14.7 join_heads.11
  883.5 37.0 %reduce-scatter.27.cloned.1.call-done.grad_ref = f32[64,2048]{1,0:T(8,128)} async-done(((f32[256,2048]{1,0:T(8,128)}), f32[64,2048]{1,0:T(8,128)}) %reduce-scatter.27.cloned.1.call-update) | async-done | bytes 524304 | tf_op jit(solution)/shard_map/reduce_scatter | solution.py:821
  1077.8 15.0 collective-permute-done.48
  1092.8 32.0 %reduce-scatter.29.cloned.1.call-done = f32[64,2048]{1,0:T(8,128)} async-done(((f32[256,2048]{1,0:T(8,128)}), f32[64,2048]{1,0:T(8,128)}) %reduce-scatter.29.cloned.1.call-update) | async-done | bytes 524304 | tf_op jit(solution)/shard_map/reduce_scatter | solution.py:821
  1130.5 14.2 collective-permute-done.49
  1145.1 26.6 %all-gather.43.cloned.1.call-done.handed_ref = f32[256,2048]{1,0:T(8,128)} async-done(((f32[64,2048]{1,0:T(8,128)}), f32[256,2048]{1,0:T(8,128)}) %all-gather.43.cloned.1.call-update) | async-done | bytes 2097168 | tf_op jit(solution)/shard_map/all_gather | solution.py:817
  1190.4 27.5 %all-gather.41.cloned.1.call-done.handed_ref = f32[256,2048]{1,0:T(8,128)} async-done(((f32[64,2048]{1,0:T(8,128)}), f32[256,2048]{1,0:T(8,128)}) %all-gather.41.cloned.1.call-update) | async-done | bytes 2097168 | tf_op jit(solution)/shard_map/all_gather | solution.py:817
  1239.1 24.2 %reduce-scatter.35.cloned.1.call-done.grad_ref = f32[64,2048]{1,0:T(8,128)} async-done(((f32[256,2048]{1,0:T(8,128)}), f32[64,2048]{1,0:T(8,128)}) %reduce-scatter.35.cloned.1.call-update) | async-done | bytes 524304 | tf_op jit(solution)/shard_map/reduce_scatter | solution.py:821
  1408.3 15.1 collective-permute-done.64
  1424.3 30.6 %reduce-scatter.37.cloned.1.call-done = f32[64,2048]{1,0:T(8,128)} async-done(((f32[256,2048]{1,0:T(8,128)}), f32[64,2048]{1,0:T(8,128)}) %reduce-scatter.37.cloned.1.call-update) | async-done | bytes 524304 | tf_op jit(solution)/shard_map/reduce_scatter | solution.py:821
  1461.1 14.1 collective-permute-done.65
  1478.6 23.1 %all-gather.47.cloned.1.call-done.handed_ref = f32[256,2048]{1,0:T(8,128)} async-done(((f32[64,2048]{1,0:T(8,128)}), f32[256,2048]{1,0:T(8,128)}) %all-gather.47.cloned.1.call-update) | async-done | bytes 2097168 | tf_op jit(solution)/shard_map/all_gather | solution.py:817
  1503.1 13.4 feed_back.10
  1529.6 18.3 all-gather.45.cloned.1.call-done.handed_ref
  1726.6 14.2 collective-permute-done.84
  1823.9 50.2 %collective-permute-done.88 = f32[1408,512]{1,0:T(8,128)} collective-permute-done((f32[1408,512]{1,0:T(8,128)}, f32[1408,512]{1,0:T(8,128)}, u32[]{:S(2)}, u32[]{:S(2)}) %collective-permute-start.88) | collective-permute-done | bytes 2883616 | tf_op jit(solution)/shard_map/ppermute | solution.py:803
  1881.1 65.6 %collective-permute-done.91 = f32[512,1664]{1,0:T(8,128)} collective-permute-done((f32[512,1664]{1,0:T(8,128)}, f32[512,1664]{1,0:T(8,128)}, u32[]{:S(2)}, u32[]{:S(2)}) %collective-permute-start.91) | collective-permute-done | bytes 3407904 | tf_op jit(solution)/shard_map/ppermute | solution.py:803
  (1360 shorter events, 1155.4 us)
Async XLA Ops:
  9.5 96.1 %all-gather.57.cloned.1.call-start = ((), (), s32[]{:S(2)}) async-start(), calls=%async_computation.46 | async-start | bytes 2621440 | tf_op jit(solution)/shard_map/all_gather | solution.py:817
  10.3 143.8 %all-gather.29.cloned.1.call-start = ((), (), s32[]{:S(2)}) async-start(), calls=%async_computation.16 | async-start | bytes 2621440 | tf_op jit(solution)/shard_map/all_gather | solution.py:817
  15.6 183.6 %all-gather.31.cloned.1.call-start = ((), (), s32[]{:S(2)}) async-start(), calls=%async_computation.17 | async-start | bytes 2621440 | tf_op jit(solution)/shard_map/all_gather | solution.py:817
  16.1 260.0 %all-gather.55.cloned.1.call-start = ((), (), s32[]{:S(2)}) async-start(), calls=%async_computation.45 | async-start | bytes 2621440 | tf_op jit(solution)/shard_map/all_gather | solution.py:1058
  102.9 189.7 %all-gather.59.cloned.1.call-start = ((), (), s32[]{:S(2)}) async-start(), calls=%async_computation.47 | async-start | bytes 2621440 | tf_op jit(solution)/shard_map/all_gather | solution.py:1058
  200.7 137.4 %reduce-scatter.17.cloned.1.call-start = ((), (), s32[]{:S(2)}) async-start(), calls=%async_computation.18 | async-start | bytes 2621440 | tf_op jit(solution)/shard_map/reduce_scatter | solution.py:821
  307.3 123.8 %all-gather.33.cloned.1.call-start = ((), (), s32[]{:S(2)}) async-start(), calls=%async_computation.19 | async-start | bytes 2621440 | tf_op jit(solution)/shard_map/all_gather | solution.py:817
  356.1 121.1 %all-gather.35.cloned.1.call-start = ((), (), s32[]{:S(2)}) async-start(), calls=%async_computation.21 | async-start | bytes 2621440 | tf_op jit(solution)/shard_map/all_gather | solution.py:817
  402.4 121.1 %all-gather.61.cloned.1.call-start = ((), (), s32[]{:S(2)}) async-start(), calls=%async_computation.48 | async-start | bytes 2621440 | tf_op jit(solution)/shard_map/all_gather | solution.py:1058
  538.3 122.7 %reduce-scatter.23.cloned.1.call-start = ((), (), s32[]{:S(2)}) async-start(), calls=%async_computation.23 | async-start | bytes 2621440 | tf_op jit(solution)/shard_map/reduce_scatter | solution.py:821
  584.3 123.4 %all-gather.37.cloned.1.call-start = ((), (), s32[]{:S(2)}) async-start(), calls=%async_computation.24 | async-start | bytes 2621440 | tf_op jit(solution)/shard_map/all_gather | solution.py:817
  635.2 118.7 %all-gather.39.cloned.1.call-start = ((), (), s32[]{:S(2)}) async-start(), calls=%async_computation.25 | async-start | bytes 2621440 | tf_op jit(solution)/shard_map/all_gather | solution.py:817
  681.0 122.4 %all-gather.65.cloned.1.call-start = ((), (), s32[]{:S(2)}) async-start(), calls=%async_computation.50 | async-start | bytes 2621440 | tf_op jit(solution)/shard_map/all_gather | solution.py:1058
  797.6 122.8 %reduce-scatter.27.cloned.1.call-start = ((), (), s32[]{:S(2)}) async-start(), calls=%async_computation.27 | async-start | bytes 2621440 | tf_op jit(solution)/shard_map/reduce_scatter | solution.py:821
  877.7 117.3 %reduce-scatter.25.cloned.1.call-start = ((), (), s32[]{:S(2)}) async-start(), calls=%async_computation.26 | async-start | bytes 2621440 | tf_op jit(solution)/shard_map/reduce_scatter | solution.py:821
  878.3 193.9 %reduce-scatter.31.cloned.1.call-start = ((), (), s32[]{:S(2)}) async-start(), calls=%async_computation.29 | async-start | bytes 2621440 | tf_op jit(solution)/shard_map/reduce_scatter | solution.py:821
  993.0 131.8 %reduce-scatter.29.cloned.1.call-start = ((), (), s32[]{:S(2)}) async-start(), calls=%async_computation.28 | async-start | bytes 2621440 | tf_op jit(solution)/shard_map/reduce_scatter | solution.py:821
  1072.1 99.6 %all-gather.43.cloned.1.call-start = ((), (), s32[]{:S(2)}) async-start(), calls=%async_computation.31 | async-start | bytes 2621440 | tf_op jit(solution)/shard_map/all_gather | solution.py:817
  1092.8 125.1 %all-gather.41.cloned.1.call-start = ((), (), s32[]{:S(2)}) async-start(), calls=%async_computation.30 | async-start | bytes 2621440 | tf_op jit(solution)/shard_map/all_gather | solution.py:817
  1144.7 118.6 %reduce-scatter.35.cloned.1.call-start = ((), (), s32[]{:S(2)}) async-start(), calls=%async_computation.33 | async-start | bytes 2621440 | tf_op jit(solution)/shard_map/reduce_scatter | solution.py:821
  1190.3 138.5 %reduce-scatter.33.cloned.1.call-start = ((), (), s32[]{:S(2)}) async-start(), calls=%async_computation.32 | async-start | bytes 2621440 | tf_op jit(solution)/shard_map/reduce_scatter | solution.py:821
  1236.4 165.6 %reduce-scatter.39.cloned.1.call-start = ((), (), s32[]{:S(2)}) async-start(), calls=%async_computation.35 | async-start | bytes 2621440 | tf_op jit(solution)/shard_map/reduce_scatter | solution.py:821
  1328.7 126.2 %reduce-scatter.37.cloned.1.call-start = ((), (), s32[]{:S(2)}) async-start(), calls=%async_computation.34 | async-start | bytes 2621440 | tf_op jit(solution)/shard_map/reduce_scatter | solution.py:821
  1401.9 99.9 %all-gather.47.cloned.1.call-start = ((), (), s32[]{:S(2)}) async-start(), calls=%async_computation.37 | async-start | bytes 2621440 | tf_op jit(solution)/shard_map/all_gather | solution.py:817
  1424.2 123.6 %all-gather.45.cloned.1.call-start = ((), (), s32[]{:S(2)}) async-start(), calls=%async_computation.36 | async-start | bytes 2621440 | tf_op jit(solution)/shard_map/all_gather | solution.py:817
  1476.0 117.3 %reduce-scatter.43.cloned.1.call-start = ((), (), s32[]{:S(2)}) async-start(), calls=%async_computation.39 | async-start | bytes 2621440 | tf_op jit(solution)/shard_map/reduce_scatter | solution.py:821
  1522.6 171.9 %reduce-scatter.41.cloned.1.call-start = ((), (), s32[]{:S(2)}) async-start(), calls=%async_computation.38 | async-start | bytes 2621440 | tf_op jit(solution)/shard_map/reduce_scatter | solution.py:821
  1572.9 196.7 %all-gather.49.cloned.1.call-start = ((), (), s32[]{:S(2)}) async-start(), calls=%async_computation.40 | async-start | bytes 5242880 | tf_op jit(solution)/shard_map/all_gather | solution.py:817
  1611.2 180.1 %reduce-scatter.45.cloned.1.call-start = ((), (), s32[]{:S(2)}) async-start(), calls=%async_computation.41 | async-start | bytes 2621440 | tf_op jit(solution)/shard_map/reduce_scatter | solution.py:821
  1694.4 186.7 %all-gather.51.cloned.1.call-start = ((), (), s32[]{:S(2)}) async-start(), calls=%async_computation.43 | async-start | bytes 5242880 | tf_op jit(solution)/shard_map/all_gather | solution.py:817
  1755.4 198.7 %reduce-scatter.47.cloned.1.call-start = ((), (), s32[]{:S(2)}) async-start(), calls=%async_computation.42 | async-start | bytes 2621440 | tf_op jit(solution)/shard_map/reduce_scatter | solution.py:821
  1817.4 129.3 %collective-permute-start.91 = (f32[512,1664]{1,0:T(8,128)}, f32[512,1664]{1,0:T(8,128)}, u32[]{:S(2)}, u32[]{:S(2)}) collective-permute-start(f32[512,1664]{1,0:T(8,128)} %convolution_add_fusion.7), channel_id=1, source_target_pairs={{0,8},{4,12},{8,0},{12,4},{1,9},{5,13},{9,1},{13,5},{2,10},{6,14},... | collective-permute-start | bytes 10223624 | tf_op jit(solution)/shard_map/ppermute | solution.py:803
  (528 other events, 9880.0 us)
Sparse Core Ops, SparseCore 0:
  10.2 48.5 all-gather.52
  60.9 44.7 all-gather.56
  107.8 44.6 all-gather.28
  154.5 44.6 all-gather.30
  201.2 44.6 all-gather.54
  247.9 44.6 all-gather.58
  295.4 42.5 reduce-scatter.16
  341.0 43.1 reduce-scatter.18
  385.8 45.2 all-gather.32
  432.5 44.6 all-gather.34
  478.8 44.6 all-gather.60
  524.9 44.6 all-gather.62
  572.4 42.5 reduce-scatter.20
  617.9 43.1 reduce-scatter.22
  662.4 45.2 all-gather.36
  709.2 44.6 all-gather.38
  755.3 44.6 all-gather.64
  801.4 44.6 all-gather.66
  922.7 51.5 reduce-scatter.24
  993.2 62.5 reduce-scatter.30
  1072.2 52.5 reduce-scatter.28
  1126.4 45.2 all-gather.42
  1173.2 44.6 all-gather.40
  1220.7 42.5 reduce-scatter.34
  1266.1 51.4 reduce-scatter.32
  1328.9 61.4 reduce-scatter.38
  1402.0 52.8 reduce-scatter.36
  1456.5 45.2 all-gather.46
  1503.2 44.6 all-gather.44
  1595.7 51.5 reduce-scatter.40
  1648.7 92.7 all-gather.48
  1788.3 80.0 all-gather.50
  (4 shorter events, 169.6 us)

commit v5 on v4

--- a/solution.py
+++ b/solution.py
@@ -1043,6 +1043,8 @@
         )
         tops[member] = jnp.where(section == 0, received, own(given).astype(F32))
         if step:
+            if not back_step and feed_grads:
+                sums = after(sums, *feed_grads.values())
             feed_grads[member] = scatter_tp(sums)
         else:
             summed = scatter_tp(jnp.where(section == 0, sums, late_sums[member]))
@@ -1096,6 +1098,7 @@
     taps_grad = jnp.zeros(taps.shape, F32)
     side_sums = jnp.zeros((8, 128), F32)
     received, handed = [None] * group, [None] * group
+    up_sums = up_parts = up_moved = down_parts = down_moved = inner_mixed = outer_mixed = None
     for back_step in range(groups + 1):
         step = groups - back_step
         final = back_step == groups
@@ -1124,7 +1127,8 @@
             )
             return feed_part[0], [ring(piece, "tp", at) if at else piece for at, piece in enumerate(pieces)]
 
-        for member in members:
+        def begin(member):
+            nonlocal norm_feed_grad, gain_grad, up_sums, up_parts, down_parts, inner_mixed, outer_mixed
             kept = saved[step, member]
             feed_part, pieces = mix(member)
             norm_feed_grad = norm_feed_grad + feed_part
@@ -1145,6 +1149,11 @@
                 down_sums = CoreSums(after(rows_of("inner"), *up_moved), top_all, 1).send()
                 down_parts = down_sums.sums()
                 inner_mixed = rounded(inner_mixed)
+            return output_grad, all_entries
+
+        def finish(member, output_grad, all_entries):
+            nonlocal state_grad, tail_carry, up_moved, down_moved, taps_grad, side_sums
+            kept = saved[step, member]
             kept["conv_grad"], border_grad, taps_part, kept["side_low"], sums_part, state_grad = mixer_local_back(
                 sizes, order, kept["maps"], all_entries, state_grad, kept["projected"],
                 kept["resets"], kept["border"], taps, rate, bias, kept["inverse"],
@@ -1160,7 +1169,15 @@
                 tail = after(tail, all_sums[early])
             taps_grad = taps_grad + taps_part
             side_sums = side_sums + sums_part
-            last = depart(member, tail)
+            return tail
+
+        if back_step:
+            for member in members:
+                last = depart(member, finish(member, *begin(member)))
+        else:
+            begun = {member: begin(member) for member in range(group)}
+            for member in members:
+                last = depart(member, finish(member, *begun[member]))
         ready = None
         received, handed = [None] * group, [None] * group
         if final:

time: 2020 us -> 2000 us (0.990)
    unnamed x855 -> x863, local copies, waits for them, and re-layouts: 121 us -> 129 us
  transfers between devices with their start and end apart: 135 -> 135, of which waited for: 97 -> 96; matrix products, arithmetic and copies ran while one was open for 11% -> 11% of each run, Pallas kernels for 20% -> 21%
where the time goes in v5:
time: 2000 us; the launch traced here: 1980 us
  waiting for transfers between devices  1080 us (54%)
  Pallas kernels  435 us (22%)
  local copies, waits for them, and re-layouts  163 us (8%)
  other arithmetic  104 us (5%)
  starting transfers between devices  101 us (5%)
  matrix products  84.3 us (4%)
    ppermute x73, waiting for transfers between devices, ring(): lax.ppermute(value, axis, [(at, (at + steps) % count) for at in range(cou...  458 us
    pallas_call x54, Pallas kernels, call(): pl.pallas_call(kernel, grid=(1,), in_specs=specs, out_specs=[whole(array)...  395 us
    reduce_scatter x16, waiting for transfers between devices, scatter_tp(): return lax.psum_scatter(values, 'tp', scatter_dimension=0, tiled=True)  234 us
    all_gather x14, waiting for transfers between devices, gather_tp(): return lax.all_gather(values, 'tp', axis=0, tiled=True)  231 us
    unnamed x863, local copies, waits for them, and re-layouts  129 us
    ppermute x8, waiting for transfers between devices, handed_on(): lax.ppermute(value, axis, [(at, at + steps) for at in range(first, last)])  102 us
    dot_general x20, matrix products, low_dot(): lax.dot_general(a, b, (contract, ((), ())), preferred_element_type=F32)  84.3 us
    ppermute x73, starting transfers between devices, ring(): lax.ppermute(value, axis, [(at, (at + steps) % count) for at in range(cou...  70 us
  transfers between devices with their start and end apart: 135, of which 96 were waited for; matrix products, arithmetic and copies ran while one was open for 11% of the time, Pallas kernels for 21%

profile of v5, /device:TPU:0, one launch (start us, length us, event | category | flops | bytes accessed | tf_op | source)
XLA Modules:
  0.0 1983.7 jit_solution(11259084116483224562)
XLA Ops:
  29.2 29.5 %all-gather.53.cloned.1.call-done = f32[1,256,2048]{2,1,0:T(8,128)} async-done(((f32[1,64,2048]{2,1,0:T(8,128)}), f32[1,256,2048]{2,1,0:T(8,128)}) %all-gather.53.cloned.1.call-update) | async-done | bytes 2097168 | tf_op jit(solution)/shard_map/all_gather | solution.py:817
  154.6 44.6 %all-gather.31.cloned.1.call-done.source_ref = f32[1024,512]{1,0:T(8,128)} async-done(((f32[256,512]{1,0:T(8,128)}), f32[1024,512]{1,0:T(8,128)}) %all-gather.31.cloned.1.call-update) | async-done | bytes 2097168 | tf_op jit(solution)/shard_map/all_gather | solution.py:817
  201.9 44.9 %collective-permute-done.12.source_ref = f32[1024,512]{1,0:T(8,128)} collective-permute-done((f32[1024,512]{1,0:T(8,128)}, f32[1024,512]{1,0:T(8,128)}, u32[]{:S(2)}, u32[]{:S(2)}) %collective-permute-start.12) | collective-permute-done | bytes 2097184 | tf_op jit(solution)/shard_map/ppermute | solution.py:803
  276.1 14.5 join_heads.6
  292.6 14.7 join_heads.7
  307.4 30.7 %reduce-scatter.17.cloned.1.call-done = f32[64,2048]{1,0:T(8,128)} async-done(((f32[256,2048]{1,0:T(8,128)}), f32[64,2048]{1,0:T(8,128)}) %reduce-scatter.17.cloned.1.call-update) | async-done | bytes 524304 | tf_op jit(solution)/shard_map/reduce_scatter | solution.py:821
  356.2 28.1 %reduce-scatter.19.cloned.1.call-done = f32[64,2048]{1,0:T(8,128)} async-done(((f32[256,2048]{1,0:T(8,128)}), f32[64,2048]{1,0:T(8,128)}) %reduce-scatter.19.cloned.1.call-update) | async-done | bytes 524304 | tf_op jit(solution)/shard_map/reduce_scatter | solution.py:821
  402.5 28.6 %all-gather.33.cloned.1.call-done.rows_ref = f32[256,2048]{1,0:T(8,128)} async-done(((f32[64,2048]{1,0:T(8,128)}), f32[256,2048]{1,0:T(8,128)}) %all-gather.33.cloned.1.call-update) | async-done | bytes 2097168 | tf_op jit(solution)/shard_map/all_gather | solution.py:817
  523.5 14.9 join_heads.8
  538.5 31.0 %all-gather.63.cloned.1.call-done = f32[1024,512]{1,0:T(8,128)} async-done(((f32[256,512]{1,0:T(8,128)}), f32[1024,512]{1,0:T(8,128)}) %all-gather.63.cloned.1.call-update) | async-done | bytes 2097168 | tf_op jit(solution)/shard_map/all_gather | solution.py:1060
  569.4 14.7 join_heads.9
  584.2 30.7 %reduce-scatter.21.cloned.1.call-done = f32[64,2048]{1,0:T(8,128)} async-done(((f32[256,2048]{1,0:T(8,128)}), f32[64,2048]{1,0:T(8,128)}) %reduce-scatter.21.cloned.1.call-update) | async-done | bytes 524304 | tf_op jit(solution)/shard_map/reduce_scatter | solution.py:821
  635.2 25.9 %reduce-scatter.23.cloned.1.call-done = f32[64,2048]{1,0:T(8,128)} async-done(((f32[256,2048]{1,0:T(8,128)}), f32[64,2048]{1,0:T(8,128)}) %reduce-scatter.23.cloned.1.call-update) | async-done | bytes 524304 | tf_op jit(solution)/shard_map/reduce_scatter | solution.py:821
  681.1 26.6 %all-gather.37.cloned.1.call-done.rows_ref = f32[256,2048]{1,0:T(8,128)} async-done(((f32[64,2048]{1,0:T(8,128)}), f32[256,2048]{1,0:T(8,128)}) %all-gather.37.cloned.1.call-update) | async-done | bytes 2097168 | tf_op jit(solution)/shard_map/all_gather | solution.py:817
  803.3 14.9 join_heads.10
  846.1 14.8 join_heads.11
  925.6 19.7 reduce-scatter.27.cloned.1.call-done.grad_ref
  1063.5 14.2 collective-permute-done.48
  1077.8 26.3 %reduce-scatter.29.cloned.1.call-done = f32[64,2048]{1,0:T(8,128)} async-done(((f32[256,2048]{1,0:T(8,128)}), f32[64,2048]{1,0:T(8,128)}) %reduce-scatter.29.cloned.1.call-update) | async-done | bytes 524304 | tf_op jit(solution)/shard_map/reduce_scatter | solution.py:821
  1109.8 14.2 collective-permute-done.49
  1124.5 26.6 %all-gather.43.cloned.1.call-done.handed_ref = f32[256,2048]{1,0:T(8,128)} async-done(((f32[64,2048]{1,0:T(8,128)}), f32[256,2048]{1,0:T(8,128)}) %all-gather.43.cloned.1.call-update) | async-done | bytes 2097168 | tf_op jit(solution)/shard_map/all_gather | solution.py:817
  1169.7 27.4 %all-gather.41.cloned.1.call-done.handed_ref = f32[256,2048]{1,0:T(8,128)} async-done(((f32[64,2048]{1,0:T(8,128)}), f32[256,2048]{1,0:T(8,128)}) %all-gather.41.cloned.1.call-update) | async-done | bytes 2097168 | tf_op jit(solution)/shard_map/all_gather | solution.py:817
  1218.4 24.2 %reduce-scatter.35.cloned.1.call-done.grad_ref = f32[64,2048]{1,0:T(8,128)} async-done(((f32[256,2048]{1,0:T(8,128)}), f32[64,2048]{1,0:T(8,128)}) %reduce-scatter.35.cloned.1.call-update) | async-done | bytes 524304 | tf_op jit(solution)/shard_map/reduce_scatter | solution.py:821
  1387.4 15.3 collective-permute-done.64
  1403.6 30.4 %reduce-scatter.37.cloned.1.call-done = f32[64,2048]{1,0:T(8,128)} async-done(((f32[256,2048]{1,0:T(8,128)}), f32[64,2048]{1,0:T(8,128)}) %reduce-scatter.37.cloned.1.call-update) | async-done | bytes 524304 | tf_op jit(solution)/shard_map/reduce_scatter | solution.py:821
  1440.2 14.1 collective-permute-done.65
  1457.7 23.2 %all-gather.47.cloned.1.call-done.handed_ref = f32[256,2048]{1,0:T(8,128)} async-done(((f32[64,2048]{1,0:T(8,128)}), f32[256,2048]{1,0:T(8,128)}) %all-gather.47.cloned.1.call-update) | async-done | bytes 2097168 | tf_op jit(solution)/shard_map/all_gather | solution.py:817
  1482.2 13.4 feed_back.10
  1508.7 18.3 all-gather.45.cloned.1.call-done.handed_ref
  1705.6 14.2 collective-permute-done.84
  1802.8 50.2 %collective-permute-done.88 = f32[1408,512]{1,0:T(8,128)} collective-permute-done((f32[1408,512]{1,0:T(8,128)}, f32[1408,512]{1,0:T(8,128)}, u32[]{:S(2)}, u32[]{:S(2)}) %collective-permute-start.88) | collective-permute-done | bytes 2883616 | tf_op jit(solution)/shard_map/ppermute | solution.py:803
  1860.2 65.5 %collective-permute-done.91 = f32[512,1664]{1,0:T(8,128)} collective-permute-done((f32[512,1664]{1,0:T(8,128)}, f32[512,1664]{1,0:T(8,128)}, u32[]{:S(2)}, u32[]{:S(2)}) %collective-permute-start.91) | collective-permute-done | bytes 3407904 | tf_op jit(solution)/shard_map/ppermute | solution.py:803
  (1368 shorter events, 1158.1 us)
Async XLA Ops:
  9.5 96.1 %all-gather.57.cloned.1.call-start = ((), (), s32[]{:S(2)}) async-start(), calls=%async_computation.46 | async-start | bytes 2621440 | tf_op jit(solution)/shard_map/all_gather | solution.py:817
  10.3 143.8 %all-gather.29.cloned.1.call-start = ((), (), s32[]{:S(2)}) async-start(), calls=%async_computation.16 | async-start | bytes 2621440 | tf_op jit(solution)/shard_map/all_gather | solution.py:817
  15.6 183.6 %all-gather.31.cloned.1.call-start = ((), (), s32[]{:S(2)}) async-start(), calls=%async_computation.17 | async-start | bytes 2621440 | tf_op jit(solution)/shard_map/all_gather | solution.py:817
  16.1 260.0 %all-gather.55.cloned.1.call-start = ((), (), s32[]{:S(2)}) async-start(), calls=%async_computation.45 | async-start | bytes 2621440 | tf_op jit(solution)/shard_map/all_gather | solution.py:1060
  102.9 189.7 %all-gather.59.cloned.1.call-start = ((), (), s32[]{:S(2)}) async-start(), calls=%async_computation.47 | async-start | bytes 2621440 | tf_op jit(solution)/shard_map/all_gather | solution.py:1060
  200.7 137.4 %reduce-scatter.17.cloned.1.call-start = ((), (), s32[]{:S(2)}) async-start(), calls=%async_computation.18 | async-start | bytes 2621440 | tf_op jit(solution)/shard_map/reduce_scatter | solution.py:821
  307.3 123.8 %all-gather.33.cloned.1.call-start = ((), (), s32[]{:S(2)}) async-start(), calls=%async_computation.19 | async-start | bytes 2621440 | tf_op jit(solution)/shard_map/all_gather | solution.py:817
  356.1 121.1 %all-gather.35.cloned.1.call-start = ((), (), s32[]{:S(2)}) async-start(), calls=%async_computation.21 | async-start | bytes 2621440 | tf_op jit(solution)/shard_map/all_gather | solution.py:817
  402.4 121.1 %all-gather.61.cloned.1.call-start = ((), (), s32[]{:S(2)}) async-start(), calls=%async_computation.48 | async-start | bytes 2621440 | tf_op jit(solution)/shard_map/all_gather | solution.py:1060
  475.2 94.2 %all-gather.63.cloned.1.call-start = ((), (), s32[]{:S(2)}) async-start(), calls=%async_computation.49 | async-start | bytes 2621440 | tf_op jit(solution)/shard_map/all_gather | solution.py:1060
  538.4 122.6 %reduce-scatter.23.cloned.1.call-start = ((), (), s32[]{:S(2)}) async-start(), calls=%async_computation.23 | async-start | bytes 2621440 | tf_op jit(solution)/shard_map/reduce_scatter | solution.py:821
  584.2 123.5 %all-gather.37.cloned.1.call-start = ((), (), s32[]{:S(2)}) async-start(), calls=%async_computation.24 | async-start | bytes 2621440 | tf_op jit(solution)/shard_map/all_gather | solution.py:817
  635.1 118.7 %all-gather.39.cloned.1.call-start = ((), (), s32[]{:S(2)}) async-start(), calls=%async_computation.25 | async-start | bytes 2621440 | tf_op jit(solution)/shard_map/all_gather | solution.py:817
  681.0 122.3 %all-gather.65.cloned.1.call-start = ((), (), s32[]{:S(2)}) async-start(), calls=%async_computation.50 | async-start | bytes 2621440 | tf_op jit(solution)/shard_map/all_gather | solution.py:1060
  751.8 94.3 %all-gather.67.cloned.1.call-start = ((), (), s32[]{:S(2)}) async-start(), calls=%async_computation.51 | async-start | bytes 2621440 | tf_op jit(solution)/shard_map/all_gather | solution.py:1060
  835.5 109.7 %reduce-scatter.27.cloned.1.call-start = ((), (), s32[]{:S(2)}) async-start(), calls=%async_computation.27 | async-start | bytes 2621440 | tf_op jit(solution)/shard_map/reduce_scatter | solution.py:821
  891.0 167.0 %reduce-scatter.31.cloned.1.call-start = ((), (), s32[]{:S(2)}) async-start(), calls=%async_computation.29 | async-start | bytes 2621440 | tf_op jit(solution)/shard_map/reduce_scatter | solution.py:821
  1055.6 95.4 %all-gather.43.cloned.1.call-start = ((), (), s32[]{:S(2)}) async-start(), calls=%async_computation.31 | async-start | bytes 2621440 | tf_op jit(solution)/shard_map/all_gather | solution.py:817
  1077.7 119.4 %all-gather.41.cloned.1.call-start = ((), (), s32[]{:S(2)}) async-start(), calls=%async_computation.30 | async-start | bytes 2621440 | tf_op jit(solution)/shard_map/all_gather | solution.py:817
  1124.0 118.6 %reduce-scatter.35.cloned.1.call-start = ((), (), s32[]{:S(2)}) async-start(), calls=%async_computation.33 | async-start | bytes 2621440 | tf_op jit(solution)/shard_map/reduce_scatter | solution.py:821
  1169.6 138.4 %reduce-scatter.33.cloned.1.call-start = ((), (), s32[]{:S(2)}) async-start(), calls=%async_computation.32 | async-start | bytes 2621440 | tf_op jit(solution)/shard_map/reduce_scatter | solution.py:821
  1215.6 165.4 %reduce-scatter.39.cloned.1.call-start = ((), (), s32[]{:S(2)}) async-start(), calls=%async_computation.35 | async-start | bytes 2621440 | tf_op jit(solution)/shard_map/reduce_scatter | solution.py:821
  1308.0 126.0 %reduce-scatter.37.cloned.1.call-start = ((), (), s32[]{:S(2)}) async-start(), calls=%async_computation.34 | async-start | bytes 2621440 | tf_op jit(solution)/shard_map/reduce_scatter | solution.py:821
  1380.9 100.0 %all-gather.47.cloned.1.call-start = ((), (), s32[]{:S(2)}) async-start(), calls=%async_computation.37 | async-start | bytes 2621440 | tf_op jit(solution)/shard_map/all_gather | solution.py:817
  1403.5 123.5 %all-gather.45.cloned.1.call-start = ((), (), s32[]{:S(2)}) async-start(), calls=%async_computation.36 | async-start | bytes 2621440 | tf_op jit(solution)/shard_map/all_gather | solution.py:817
  1455.1 117.3 %reduce-scatter.43.cloned.1.call-start = ((), (), s32[]{:S(2)}) async-start(), calls=%async_computation.39 | async-start | bytes 2621440 | tf_op jit(solution)/shard_map/reduce_scatter | solution.py:821
  1501.7 171.9 %reduce-scatter.41.cloned.1.call-start = ((), (), s32[]{:S(2)}) async-start(), calls=%async_computation.38 | async-start | bytes 2621440 | tf_op jit(solution)/shard_map/reduce_scatter | solution.py:821
  1552.1 196.7 %all-gather.49.cloned.1.call-start = ((), (), s32[]{:S(2)}) async-start(), calls=%async_computation.40 | async-start | bytes 5242880 | tf_op jit(solution)/shard_map/all_gather | solution.py:817
  1590.3 180.2 %reduce-scatter.45.cloned.1.call-start = ((), (), s32[]{:S(2)}) async-start(), calls=%async_computation.41 | async-start | bytes 2621440 | tf_op jit(solution)/shard_map/reduce_scatter | solution.py:821
  1673.5 186.7 %all-gather.51.cloned.1.call-start = ((), (), s32[]{:S(2)}) async-start(), calls=%async_computation.43 | async-start | bytes 5242880 | tf_op jit(solution)/shard_map/all_gather | solution.py:817
  1734.5 198.6 %reduce-scatter.47.cloned.1.call-start = ((), (), s32[]{:S(2)}) async-start(), calls=%async_computation.42 | async-start | bytes 2621440 | tf_op jit(solution)/shard_map/reduce_scatter | solution.py:821
  1796.4 129.3 %collective-permute-start.91 = (f32[512,1664]{1,0:T(8,128)}, f32[512,1664]{1,0:T(8,128)}, u32[]{:S(2)}, u32[]{:S(2)}) collective-permute-start(f32[512,1664]{1,0:T(8,128)} %convolution_add_fusion.7), channel_id=1, source_target_pairs={{0,8},{4,12},{8,0},{12,4},{1,9},{5,13},{9,1},{13,5},{2,10},{6,14},... | collective-permute-start | bytes 10223624 | tf_op jit(solution)/shard_map/ppermute | solution.py:803
  (532 other events, 9237.3 us)
Sparse Core Ops, SparseCore 0:
  10.2 48.5 all-gather.52
  60.9 44.7 all-gather.56
  107.8 44.6 all-gather.28
  154.5 44.6 all-gather.30
  201.2 44.6 all-gather.54
  247.9 44.6 all-gather.58
  295.4 42.5 reduce-scatter.16
  341.0 43.1 reduce-scatter.18
  385.8 45.2 all-gather.32
  432.5 44.6 all-gather.34
  478.8 44.6 all-gather.60
  524.9 44.5 all-gather.62
  572.3 42.6 reduce-scatter.20
  617.8 43.1 reduce-scatter.22
  662.4 45.2 all-gather.36
  709.2 44.6 all-gather.38
  755.3 44.8 all-gather.64
  801.6 44.4 all-gather.66
  893.8 51.4 reduce-scatter.26
  1011.5 46.3 reduce-scatter.30
  1060.9 43.1 reduce-scatter.28
  1105.7 45.2 all-gather.42
  1152.4 44.6 all-gather.40
  1200.0 42.5 reduce-scatter.34
  1245.4 51.5 reduce-scatter.32
  1308.1 61.5 reduce-scatter.38
  1381.0 52.9 reduce-scatter.36
  1435.6 45.2 all-gather.46
  1482.3 44.6 all-gather.44
  1574.8 51.5 reduce-scatter.40
  1627.8 92.7 all-gather.48
  1767.4 80.0 all-gather.50
  (4 shorter events, 169.5 us)
